TPU v7x, 32 devices: a whole 2x2x4 slice. The times are simulated.
32 devices in a mesh: req: 8 (over y, x, core), tp: 4 (over z).
Axes of the slice: x: 2, y: 2, z: 4, core: 2. Of those that a mesh axis runs over, the one named last changes fastest.
Arguments:
- hidden: bfloat16 [8, 128, 2048], P('req', None, 'tp'), may hold values from -600 to 600
- norm_gain: bfloat16 [2048], replicated, may hold values from 0.099609375 to 1.8984375
- w_query: bfloat16 [2048, 2048], P('req', 'tp'), may hold values from -0.125 to 0.125
- w_key: bfloat16 [2048, 512], P('req', 'tp'), may hold values from -0.125 to 0.125
- w_value: bfloat16 [2048, 512], P('req', 'tp'), may hold values from -0.125 to 0.125
- w_out: bfloat16 [2048, 2048], P('tp', 'req'), may hold values from -0.125 to 0.125
- cache_keys: bfloat16 [8, 2048, 512], P('req', None, 'tp'), may hold values from -72 to 72
- cache_values: bfloat16 [8, 2048, 512], P('req', None, 'tp'), may hold values from -6 to 6
- cache_lengths: int32 [8], replicated, may hold values from 1 to 2048, 8192 in all
Outputs:
- attn_out: bfloat16 [8, 128, 2048], P('req', None, 'tp')
- new_keys: bfloat16 [8, 128, 512], P('req', None, 'tp')
- new_values: bfloat16 [8, 128, 512], P('req', None, 'tp')
Inputs may be any that keep to these rules, and one draw needn't show every extreme that they name: `cache_lengths`: one request has exactly 2048 cached positions; all requests together have 8 * 1024.
All inputs are finite; a program needn't handle non-finite values.
Results may differ from a plain program's by a relative error of at most 0.015.
Values may be sent and summed in bfloat16 or wider, within the bound.
No kernel may reach another device: no remote copies, remote signals or barrier semaphores. Data moves between devices by JAX's collectives and lax.ppermute only.
A program may use at most 64 MiB of HBM per device.

v0:
```python
import jax
import jax.numpy as jnp
from jax import lax
from jax.sharding import PartitionSpec as P

HD = 64


rope_base = 1000000.0
norm_eps = 1e-05
masked_score = -1e30


def rotate(tensor, cosine_table, sine_table):
    half_width = tensor.shape[-1] // 2
    front_half = tensor[..., :half_width]
    back_half = tensor[..., half_width:]
    return jnp.concatenate(
        [
            front_half * cosine_table - back_half * sine_table,
            back_half * cosine_table + front_half * sine_table,
        ],
        axis=-1,
    )


def phases(length_now, row_count, head_width):
    positions = (length_now + jnp.arange(row_count, dtype=jnp.int32)).astype(jnp.float32)
    inverse = rope_base ** (
        -jnp.arange(0, head_width, 2, dtype=jnp.int32).astype(jnp.float32) / head_width
    )
    phase_grid = positions[:, None] * inverse[None, :]
    return (jnp.cos(phase_grid)[:, None, :], jnp.sin(phase_grid)[:, None, :])


def group_queries(flat_queries, key_heads, group_size, head_width):
    token_count = flat_queries.shape[0]
    shaped = flat_queries.reshape(token_count, key_heads, group_size, head_width).transpose(
        1, 2, 0, 3
    )
    return shaped.reshape(key_heads, group_size * token_count, head_width)


def attend_block(running, grouped, key_block, value_block, visible):
    peak_old, total_old, accum_old = running
    scores = jnp.einsum(
        "gqd,kgd->gqk", grouped, key_block, preferred_element_type=jnp.float32
    ) * grouped.shape[-1] ** (-0.5)
    scores = jnp.where(visible, scores, masked_score)
    peak_new = jnp.maximum(peak_old, jnp.max(scores, axis=-1))
    weights = jnp.where(visible, jnp.exp(scores - peak_new[..., None]), 0.0)
    factor = jnp.exp(peak_old - peak_new)
    total_new = total_old * factor + jnp.sum(weights, axis=-1)
    accum_new = accum_old * factor[:, None, :] + jnp.einsum(
        "gqk,kgd->gdq",
        weights.astype(jnp.bfloat16),
        value_block,
        preferred_element_type=jnp.float32,
    )
    return (peak_new, total_new, accum_new)


def cache_pass(
    running, grouped, key_cache, value_cache, buffer_first, lower_row, upper_row, block_rows
):
    first_block = lower_row // block_rows
    last_block = jnp.where(
        lower_row < upper_row, (upper_row + block_rows - 1) // block_rows, first_block
    )

    def step_body(block_index, running_now):
        position_first = block_index * block_rows
        local_first = position_first - buffer_first
        key_block = lax.dynamic_slice_in_dim(key_cache, local_first, block_rows, 0)
        value_block = lax.dynamic_slice_in_dim(value_cache, local_first, block_rows, 0)
        positions = position_first + jnp.arange(block_rows, dtype=jnp.int32)
        visible = ((positions >= lower_row) & (positions < upper_row))[None, None, :]
        return attend_block(running_now, grouped, key_block, value_block, visible)

    return lax.fori_loop(first_block, last_block, step_body, running)


def new_pass(running, grouped, fresh_keys, fresh_values, token_count, block_rows):
    token_of_row = jnp.arange(grouped.shape[1], dtype=jnp.int32) % token_count
    positions = 0 + jnp.arange(block_rows, dtype=jnp.int32)
    visible = (positions[None, :] <= token_of_row[:, None])[None]
    running = attend_block(running, grouped, fresh_keys, fresh_values, visible)
    return running


def per_device(
    hidden, norm_gain, w_query, w_key, w_value, w_out, cache_keys, cache_values, cache_lengths
):
    token_count = hidden.shape[1]
    gathered = lax.all_gather(hidden[0], "tp", axis=1, tiled=True)
    as_float = gathered.astype(jnp.float32)
    mean_square = jnp.mean(as_float * as_float, axis=-1, keepdims=True)
    normed = (as_float * lax.rsqrt(mean_square + norm_eps) * norm_gain.astype(jnp.float32)).astype(
        jnp.bfloat16
    )
    query_width = w_query.shape[1]
    key_width = w_key.shape[1]
    query_sum = jnp.dot(
        normed,
        lax.all_gather(w_query, "req", axis=0, tiled=True),
        preferred_element_type=jnp.float32,
    )
    key_sum = jnp.dot(
        normed, lax.all_gather(w_key, "req", axis=0, tiled=True), preferred_element_type=jnp.float32
    )
    value_sum = jnp.dot(
        normed,
        lax.all_gather(w_value, "req", axis=0, tiled=True),
        preferred_element_type=jnp.float32,
    )
    device_index = lax.axis_index("req")
    length_own = cache_lengths[device_index]
    head_width = HD
    local_heads = query_width // head_width
    key_heads = key_width // head_width
    group_size = local_heads // key_heads
    cosine_table, sine_table = phases(length_own, token_count, head_width)
    flat_queries = (
        rotate(query_sum.reshape(token_count, local_heads, head_width), cosine_table, sine_table)
        .astype(jnp.bfloat16)
        .reshape(token_count, query_width)
    )
    fresh_keys = rotate(
        key_sum.reshape(token_count, key_heads, head_width), cosine_table, sine_table
    ).astype(jnp.bfloat16)
    fresh_values = value_sum.reshape(token_count, key_heads, head_width).astype(jnp.bfloat16)
    grouped = group_queries(flat_queries, key_heads, group_size, head_width)
    cache_rows = cache_keys.shape[1]
    key_cache = cache_keys[0].reshape(cache_rows, key_heads, head_width)
    value_cache = cache_values[0].reshape(cache_rows, key_heads, head_width)
    block_cache = min(512, cache_rows // 2)
    block_new = min(512, token_count)
    query_count = group_size * token_count
    start_state = (
        jnp.full((key_heads, query_count), masked_score, jnp.float32),
        jnp.zeros((key_heads, query_count), jnp.float32),
        jnp.zeros((key_heads, head_width, query_count), jnp.float32),
    )
    own_part = cache_pass(
        start_state, grouped, key_cache, value_cache, 0, 0, length_own, block_cache
    )
    combined = new_pass(own_part, grouped, fresh_keys, fresh_values, token_count, block_new)
    accumulated = combined[2] / combined[1][:, None, :]
    mixed_heads = (
        accumulated.reshape(key_heads, head_width, group_size, token_count)
        .transpose(3, 0, 2, 1)
        .reshape(token_count, query_width)
        .astype(jnp.bfloat16)
    )
    partial_out = jnp.dot(
        mixed_heads,
        lax.all_gather(w_out, "req", axis=1, tiled=True),
        preferred_element_type=jnp.float32,
    )
    summed = lax.psum_scatter(
        partial_out.astype(jnp.bfloat16), "tp", scatter_dimension=1, tiled=True
    )
    return (
        summed[None],
        fresh_keys.reshape(token_count, key_width)[None],
        fresh_values.reshape(token_count, key_width)[None],
    )


def solution(mesh):
    in_specs = (
        P("req", None, "tp"),
        P(),
        P("req", "tp"),
        P("req", "tp"),
        P("req", "tp"),
        P("tp", "req"),
        P("req", None, "tp"),
        P("req", None, "tp"),
        P(),
    )
    out_specs = (P("req", None, "tp"), P("req", None, "tp"), P("req", None, "tp"))
    return jax.shard_map(
        per_device, mesh=mesh, in_specs=in_specs, out_specs=out_specs, check_vma=False
    )
```

profile of v0, /device:TPU:0, one launch (start us, length us, event | category | flops | bytes accessed | tf_op | source)
XLA Modules:
  0.0 103.3 jit_solution(8021541833808100703)
XLA Ops:
  7.2 0.7 all-gather.4.cloned.1.call-update
  8.0 0.7 all-gather.6.cloned.1.call-update
  8.7 1.2 %dynamic_slice.9 = s32[1]{0:T(128)} dynamic-slice(s32[8]{0:T(128)} %param.19, s32[]{:T(128)S(6)} %select_n.45), dynamic_slice_sizes={1} | dynamic-slice | bytes 12 | tf_op jit(solution)/shard_map/dynamic_slice | solution.py:117
  11.3 0.6 add_convert_fusion.1
  12.0 17.6 %all-gather = bf16[1,128,2048]{2,1,0:T(8,128)(2,1)S(1)} all-gather(bf16[1,128,512]{2,1,0:T(8,128)(2,1)} %param.11), channel_id=2, replica_groups=mesh['req'=8,'tp'=4] {'tp'}, dimensions={2}, use_global_device_ids=true | all-gather | bytes 655360 | tf_op jit(solution)/shard_map/all_gather | solution.py:95
  29.7 0.7 convert_element_type.70
  30.7 0.2 copy.27
  30.9 11.0 %all_gather.17 = bf16[2048,128]{1,0:T(8,128)(2,1)S(1)} all-gather(bf16[256,128]{1,0:T(8,128)(2,1)S(1)} %copy-done.2), channel_id=1, replica_groups=mesh['req'=8,'tp'=4] {'req'}, dimensions={0}, use_global_device_ids=true | all-gather | bytes 589824 | tf_op jit(solution)/shard_map/all_gather | solution.py:109
  42.0 9.8 %all_gather.18 = bf16[2048,128]{1,0:T(8,128)(2,1)S(1)} all-gather(bf16[256,128]{1,0:T(8,128)(2,1)S(1)} %copy-done.3), channel_id=1, replica_groups=mesh['req'=8,'tp'=4] {'req'}, dimensions={0}, use_global_device_ids=true | all-gather | bytes 589824 | tf_op jit(solution)/shard_map/all_gather | solution.py:113
  51.8 0.4 fusion.39
  52.2 0.4 convolution_convert_fusion.1
  52.8 2.6 %fusion.41 = f32[128,512]{0,1:T(8,128)S(1)} fusion(bf16[2048,512]{1,0:T(8,128)(2,1)} %all-gather.4.cloned.1.call-done, bf16[1,128,2048]{2,1,0:T(8,128)(2,1)S(1)} %all-gather, f32[2048]{0:T(1024)S(1)} %convert_element_type.70, f32[128]{0:T(128)S(1)} %add_rsqrt_fusion), kind=kOutput, calls=%fused_computation.68 | convolution fusion | flops 269484032 | bytes 2892288 | tf_op jit(solution)/shard_map/dot_general | solution.py:103
  55.7 0.3 fusion.43
  56.0 2.6 %while.14 = (s32[]{:T(128)}, f32[2,512]{1,0:T(2,128)S(1)}, f32[2,512]{1,0:T(2,128)S(1)}, f32[2,64,512]{2,1,0:T(8,128)S(1)}, s32[]{:T(128)}, /*index=5*/s32[]{:T(...) while((s32[]{:T(128)}, f32[2,512]{1,0:T(2,128)S(1)}, ...), condition=%wide.region_4.5_spmd, body=%wide.region_1.4_spmd.sunk | while | flops 141168640 | bytes 7277243 | solution.py:80
  56.0 0.7 fusion.60
  56.7 0.5 bitcast_reduce_fusion.2
  57.3 0.6 fusion.61
  57.9 0.7 convolution_add_fusion.3
  58.8 0.3 fusion.24
  59.1 13.0 %all-gather.6.cloned.1.call-done = bf16[512,2048]{1,0:T(8,128)(2,1)} async-done(((bf16[512,256]{1,0:T(8,128)(2,1)}), bf16[512,2048]{1,0:T(8,128)(2,1)}) %all-gather.6.cloned.1.call-update) | async-done | bytes 2097168 | tf_op jit(solution)/shard_map/all_gather | solution.py:157
  72.1 2.9 %convolution_convert_fusion = bf16[128,2048]{1,0:T(8,128)(2,1)} fusion(bf16[128,512]{0,1:T(8,128)(2,1)S(1)} %bitcast.61, bf16[512,2048]{1,0:T(8,128)(2,1)} %all-gather.6.cloned.1.call-done), kind=kOutput, calls=%fused_computation.27 | convolution fusion | flops 268697600 | bytes 2752512 | tf_op jit(solution)/shard_map/dot_general | solution.py:155
  75.0 0.7 copy.30
  75.7 0.7 copy.31
  76.4 20.3 %reduce-scatter.2.cloned.1.call-done = bf16[128,512]{1,0:T(8,128)(2,1)} async-done(((bf16[128,2048]{1,0:T(8,128)(2,1)}), bf16[128,512]{1,0:T(8,128)(2,1)}) %reduce-scatter.2.cloned.1.call-update) | async-done | bytes 131088 | tf_op jit(solution)/shard_map/reduce_scatter | solution.py:160
  (37 shorter events, 1.3 us)
Async XLA Ops:
  7.2 23.3 %copy-start = (bf16[1,2048,128]{2,1,0:T(8,128)(2,1)S(1)}, bf16[1,2048,128]{2,1,0:T(8,128)(2,1)}, u32[]{:S(2)}) copy-start(bf16[1,2048,128]{2,1,0:T(8,128)(2,1)} %param.17) | copy-start | bytes 1572868
  7.2 23.5 %copy-start.1 = (bf16[1,2048,128]{2,1,0:T(8,128)(2,1)S(1)}, bf16[1,2048,128]{2,1,0:T(8,128)(2,1)}, u32[]{:S(2)}) copy-start(bf16[1,2048,128]{2,1,0:T(8,128)(2,1)} %param.18) | copy-start | bytes 1572868
  7.2 23.7 %copy-start.2 = (bf16[256,128]{1,0:T(8,128)(2,1)S(1)}, bf16[256,128]{1,0:T(8,128)(2,1)}, u32[]{:S(2)}) copy-start(bf16[256,128]{1,0:T(8,128)(2,1)} %param.14) | copy-start | bytes 196612
  7.2 45.6 %all-gather.4.cloned.1.call-start = ((), (), s32[]{:S(2)}) async-start(), calls=%async_computation.1 | async-start | bytes 2359296 | tf_op jit(solution)/shard_map/all_gather | solution.py:105
  7.9 34.0 %copy-start.3 = (bf16[256,128]{1,0:T(8,128)(2,1)S(1)}, bf16[256,128]{1,0:T(8,128)(2,1)}, u32[]{:S(2)}) copy-start(bf16[256,128]{1,0:T(8,128)(2,1)} %param.15) | copy-start | bytes 196612
  7.9 64.1 %all-gather.6.cloned.1.call-start = ((), (), s32[]{:S(2)}) async-start(), calls=%async_computation.2 | async-start | bytes 2359296 | tf_op jit(solution)/shard_map/all_gather | solution.py:157
  8.7 88.1 %reduce-scatter.2.cloned.1.call-start = ((), (), s32[]{:S(2)}) async-start(), calls=%async_computation.3 | async-start | bytes 655360 | tf_op jit(solution)/shard_map/reduce_scatter | solution.py:160
Sparse Core Ops, SparseCore 0:
  9.9 32.0 all-gather.3
  43.9 28.1 all-gather.5
  75.1 21.6 reduce-scatter.1
where the time goes:
time: 104 us; the launch traced here: 103 us
  blocking collectives  38.4 us (37%)
  waiting for transfers between devices  34.8 us (33%)
  between operations  15.3 us (15%)
  matrix products  8 us (8%)
  other arithmetic  3.33 us (3%)
  local copies, waits for them, and re-layouts  3.31 us (3%)
    reduce_scatter x1, waiting for transfers between devices, per_device(): lax.psum_scatter(partial_out.astype(jnp.bfloat16), 'tp', scatter_dimensio...  20.3 us
    all_gather x1, blocking collectives, per_device(): gathered = lax.all_gather(hidden[0], 'tp', axis=1, tiled=True)  17.6 us
    all_gather x1, waiting for transfers between devices, per_device(): lax.all_gather(w_out, 'req', axis=1, tiled=True)  13 us
    all_gather x1, blocking collectives, per_device(): lax.all_gather(w_key, 'req', axis=0, tiled=True)  11 us
    all_gather x1, blocking collectives, per_device(): lax.all_gather(w_value, 'req', axis=0, tiled=True)  9.82 us
    dot_general x1, matrix products, per_device(): jnp.dot(mixed_heads, lax.all_gather(w_out, 'req', axis=1, tiled=True), pr...  2.86 us
    dot_general x1, matrix products, per_device(): jnp.dot(normed, lax.all_gather(w_query, 'req', axis=0, tiled=True), prefe...  2.56 us
  transfers between devices with their start and end apart: 3, of which 2 were waited for; matrix products, arithmetic and copies ran while one was open for 11% of the time, Pallas kernels for 0%

commit v1 on v0

--- a/solution.py
+++ b/solution.py
@@ -1,17 +1,392 @@
+import functools
+import math
+
 import jax
 import jax.numpy as jnp
 from jax import lax
+from jax.experimental import pallas as pl
+from jax.experimental.pallas import tpu as pltpu
 from jax.sharding import PartitionSpec as P
 
 HD = 64
-
-
 rope_base = 1000000.0
 norm_eps = 1e-05
 masked_score = -1e30
-
-
-def rotate(tensor, cosine_table, sine_table):
+KV_BLOCK = 512
+FLOPS_PER_US = 1.1e9
+VMEM_BYTES = 16 * 1024 * 1024
+
+VM = pl.BlockSpec(memory_space=pltpu.VMEM)
+HB = pl.BlockSpec(memory_space=pltpu.HBM)
+SM = pl.BlockSpec(memory_space=pltpu.SMEM)
+
+
+def call(kernel, out_shape, in_specs, scratch=(), busy=1.0, name=None):
+    run = pl.pallas_call(
+        kernel,
+        out_shape=out_shape,
+        in_specs=in_specs,
+        out_specs=jax.tree.map(lambda _: VM, out_shape),
+        scratch_shapes=list(scratch),
+        compiler_params=pltpu.CompilerParams(vmem_limit_bytes=VMEM_BYTES),
+        cost_estimate=pl.CostEstimate(
+            flops=int(busy * FLOPS_PER_US), bytes_accessed=1 << 16, transcendentals=0
+        ),
+        name=name,
+    )
+
+    def placed(*operands):
+        return run(
+            *[
+                pltpu.with_memory_space_constraint(x, pltpu.HBM) if spec is HB else x
+                for x, spec in zip(operands, in_specs, strict=True)
+            ]
+        )
+
+    return placed
+
+
+def like(shape, dtype=jnp.bfloat16):
+    return jax.ShapeDtypeStruct(shape, dtype)
+
+
+def fetch(pairs, sems):
+    copies = [pltpu.make_async_copy(src, dst, sems.at[i]) for i, (src, dst) in enumerate(pairs)]
+    for copy in copies:
+        copy.start()
+    return copies
+
+
+def pack_kernel(place_ref, hidden_ref, wq_ref, wk_ref, wv_ref, w_out, keep_out, send_out, sems):
+    odd = place_ref[1]
+    half = keep_out.shape[1]
+    mine = pl.ds(pl.multiple_of(odd * half, half), half)
+    other = pl.ds(pl.multiple_of((1 - odd) * half, half), half)
+    pairs = [(hidden_ref.at[:, other], send_out), (hidden_ref.at[:, mine], keep_out)]
+    first = 0
+    for w in (wq_ref, wk_ref, wv_ref):
+        width = w.shape[1]
+        pairs.append((w, w_out.at[:, pl.ds(first, width)]))
+        first += width
+    for copy in fetch(pairs, sems):
+        copy.wait()
+
+
+def pack(place, hidden, w_query, w_key, w_value):
+    width = w_query.shape[1] + w_key.shape[1] + w_value.shape[1]
+    columns = like((hidden.shape[0], hidden.shape[1] // 2))
+    return call(
+        pack_kernel,
+        (like((w_query.shape[0], width)), columns, columns),
+        [SM] + [HB] * 4,
+        scratch=[pltpu.SemaphoreType.DMA((5,))],
+        name="pack",
+    )(place, hidden, w_query, w_key, w_value)
+
+
+def near_kernel(shards, place_ref, gain_ref, *refs):
+    columns, weights = refs[:shards], refs[shards : 2 * shards - 1]
+    partial_out, last_out, square_out, buf = refs[2 * shards - 1 :]
+    mine, odd, plane = place_ref[0], place_ref[1], place_ref[2]
+    square = 0.0
+    for m in range(shards):
+        rows = columns[m][...].astype(jnp.float32)
+        square += jnp.sum(rows * rows, axis=-1, keepdims=True)
+        gain = gain_ref[2 * (plane ^ m) + odd].astype(jnp.float32)
+        buf[m] = (rows * gain).astype(jnp.bfloat16)
+    square_out[...] = jnp.broadcast_to(square, square_out.shape)
+    partial_out[...] = sum(
+        jnp.dot(buf[mine ^ j], w[...], preferred_element_type=jnp.float32)
+        for j, w in enumerate(weights)
+    )
+    last_out[...] = buf[mine ^ (shards - 1)]
+
+
+def near_products(place, gain, columns, weights):
+    shards = len(columns)
+    rows, width = columns[0].shape
+    return call(
+        functools.partial(near_kernel, shards),
+        (
+            like((rows, weights[0].shape[1]), jnp.float32),
+            like((rows, width)),
+            like((rows, 128), jnp.float32),
+        ),
+        [SM, VM] + [VM] * (2 * shards - 1),
+        scratch=[pltpu.VMEM((shards, rows, width), jnp.bfloat16)],
+        busy=2.0,
+        name="near_products",
+    )(place, gain.reshape(2 * shards, 1, width), *columns, *weights)
+
+
+def far_kernel(partial_ref, last_ref, square_ref, top_ref, bottom_ref, keep_out, send_out):
+    half = top_ref.shape[0]
+    total = partial_ref[...]
+    for i, w in enumerate((top_ref, bottom_ref)):
+        part = last_ref[:, i * half : (i + 1) * half]
+        total += jnp.dot(part, w[...], preferred_element_type=jnp.float32)
+    tokens = keep_out.shape[0]
+    width = total.shape[1]
+    for out, first in ((keep_out, 0), (send_out, tokens)):
+        out[:, :width] = total[first : first + tokens]
+        out[:, width:] = square_ref[first : first + tokens, :]
+
+
+def far_products(partial, last, square, top, bottom):
+    rows, width = partial.shape
+    out = like((rows // 2, width + 128), jnp.float32)
+    return call(
+        far_kernel,
+        (out, out),
+        [VM] * 5,
+        busy=1.0,
+        name="far_products",
+    )(partial, last, square, top, bottom)
+
+
+def rotate(rows, cosine, sine):
+    lane = lax.broadcasted_iota(jnp.int32, (rows.shape[0], 128), 1)
+    front = (lane % HD) < HD // 2
+    slabs = []
+    for s in range(rows.shape[1] // 128):
+        slab = rows[:, s * 128 : (s + 1) * 128]
+        other = jnp.where(
+            front, -pltpu.roll(slab, 128 - HD // 2, 1), pltpu.roll(slab, HD // 2, 1)
+        )
+        slabs.append(slab * cosine + other * sine)
+    return slabs
+
+
+def place_queries(slabs, q_ref):
+    rows = slabs[0].shape[0]
+    factor = HD ** (-0.5) * math.log2(math.e)
+    low = lax.broadcasted_iota(jnp.int32, (rows, 128), 1) < HD
+    head = 0
+    for s, slab in enumerate(slabs):
+        slab = slab * factor
+        rolled = pltpu.roll(slab, HD, 1)
+        for odd_head in (0, 1):
+            group = 0 if s < len(slabs) // 2 else 1
+            keep = low if group == 0 else jnp.logical_not(low)
+            value = jnp.where(keep, slab if group == odd_head else rolled, 0.0)
+            q_ref[head * rows : (head + 1) * rows, :] = value.astype(jnp.bfloat16)
+            head += 1
+
+
+def attend(q_ref, acc_ref, peak_ref, keys, values, mask):
+    half = q_ref.shape[0] // 2
+    low = lax.broadcasted_iota(jnp.int32, values.shape, 1) < HD
+    one = jnp.ones_like(values)
+    for g in range(2):
+        part = pl.ds(g * half, half)
+        scores = lax.dot_general(
+            q_ref[part, :], keys, (((1,), (1,)), ((), ())), preferred_element_type=jnp.float32
+        )
+        if mask is not None:
+            scores = jnp.where(mask(scores.shape), scores, masked_score)
+        old = peak_ref[part, :]
+        new = jnp.maximum(old, jnp.max(scores, axis=-1, keepdims=True))
+        weights = jnp.exp2(scores - jnp.tile(new, (1, scores.shape[1] // 128))).astype(jnp.bfloat16)
+        mine = jnp.where(low if g == 0 else jnp.logical_not(low), values, one)
+        acc_ref[part, :] = acc_ref[part, :] * jnp.exp2(old - new) + jnp.dot(
+            weights, mine, preferred_element_type=jnp.float32
+        )
+        peak_ref[part, :] = new
+
+
+def finish(acc_ref, out_ref, tokens):
+    heads = acc_ref.shape[0] // tokens
+    low = lax.broadcasted_iota(jnp.int32, (tokens, 128), 1) < HD
+    slabs = []
+    for h in range(heads):
+        acc = acc_ref[h * tokens : (h + 1) * tokens, :]
+        mixed = acc / pltpu.roll(acc, HD, 1)
+        straight = (h % 2 == 0) == (h < heads // 2)
+        slabs.append(mixed if straight else pltpu.roll(mixed, HD, 1))
+    for s in range(heads // 2):
+        both = jnp.where(low, slabs[2 * s], slabs[2 * s + 1])
+        out_ref[:, s * 128 : (s + 1) * 128] = both.astype(jnp.bfloat16)
+
+
+def attention_kernel(
+    features,
+    kv_width,
+    length_ref,
+    cos_ref,
+    sin_ref,
+    here_ref,
+    there_ref,
+    k_ref,
+    v_ref,
+    *refs,
+):
+    out_ref, nk_ref, nv_ref, q_ref, acc_ref, peak_ref, k_buf, v_buf, sems = refs
+    cache = fetch([(k_ref, k_buf), (v_ref, v_buf)], sems)
+    total = here_ref[...] + there_ref[...]
+    width = total.shape[1] - 128
+    scale = lax.rsqrt(total[:, width:] / features + norm_eps)
+    total = total[:, :width] * jnp.tile(scale, (1, width // 128))
+    tokens = total.shape[0]
+    q_width = width - 2 * kv_width
+    cosine, sine = cos_ref[...], sin_ref[...]
+    place_queries(rotate(total[:, :q_width], cosine, sine), q_ref)
+    (keys,) = rotate(total[:, q_width : q_width + kv_width], cosine, sine)
+    nk_ref[...] = keys.astype(jnp.bfloat16)
+    nv_ref[...] = total[:, q_width + kv_width :].astype(jnp.bfloat16)
+
+    length = length_ref[0]
+    acc_ref[...] = jnp.zeros_like(acc_ref)
+    peak_ref[...] = jnp.full_like(peak_ref, masked_score)
+    run = functools.partial(attend, q_ref, acc_ref, peak_ref)
+    run(
+        nk_ref[...],
+        nv_ref[...],
+        lambda shape: lax.broadcasted_iota(jnp.int32, shape, 1)
+        <= lax.broadcasted_iota(jnp.int32, shape, 0) % tokens,
+    )
+    for copy in cache:
+        copy.wait()
+
+    def step(i, _):
+        rows = pl.ds(pl.multiple_of(i * KV_BLOCK, KV_BLOCK), KV_BLOCK)
+        run(k_buf[rows, :], v_buf[rows, :], None)
+        return 0
+
+    full = length // KV_BLOCK
+    lax.fori_loop(0, full, step, 0)
+    left = length - full * KV_BLOCK
+
+    @pl.when(left > 0)
+    def _():
+        rows = pl.ds(pl.multiple_of(full * KV_BLOCK, KV_BLOCK), KV_BLOCK)
+        run(
+            k_buf[rows, :],
+            v_buf[rows, :],
+            lambda shape: lax.broadcasted_iota(jnp.int32, shape, 1) < left,
+        )
+
+    finish(acc_ref, out_ref, tokens)
+
+
+def attention(length, features, cosine, sine, here, there, keys, values):
+    tokens = here.shape[0]
+    kv_width = keys.shape[1]
+    q_width = here.shape[1] - 128 - 2 * kv_width
+    queries = q_width // HD * tokens
+    fresh = like((tokens, kv_width))
+    return call(
+        functools.partial(attention_kernel, features, kv_width),
+        (like((tokens, q_width)), fresh, fresh),
+        [SM, VM, VM, VM, VM, HB, HB],
+        scratch=[
+            pltpu.VMEM((queries, 128), jnp.bfloat16),
+            pltpu.VMEM((queries, 128), jnp.float32),
+            pltpu.VMEM((queries, 128), jnp.float32),
+            pltpu.VMEM(keys.shape, jnp.bfloat16),
+            pltpu.VMEM(keys.shape, jnp.bfloat16),
+            pltpu.SemaphoreType.DMA((2,)),
+        ],
+        busy=9.0,
+        name="attention",
+    )(length, cosine, sine, here, there, keys, values)
+
+
+def out_kernel(chips, place_ref, mixed_ref, *refs):
+    weights, outs = refs[: 2 * chips], refs[2 * chips :]
+    mine, odd = place_ref[0], place_ref[1]
+    width = weights[0].shape[1]
+    mixed = mixed_ref[...]
+    for j in range(chips):
+        own, sib = [
+            jnp.dot(mixed, w[...], preferred_element_type=jnp.float32).astype(jnp.bfloat16)
+            for w in weights[2 * j : 2 * j + 2]
+        ]
+        lower = jnp.where(odd == 0, own, sib)
+        upper = jnp.where(odd == 0, sib, own)
+        for m in range(chips):
+
+            @pl.when((mine ^ j) == m)
+            def _(m=m, lower=lower, upper=upper):
+                outs[m][:, :width] = lower
+                outs[m][:, width:] = upper
+
+
+def project(mixed, place, weights):
+    chips = len(weights) // 2
+    rows = mixed.shape[0]
+    width = weights[0].shape[1]
+    return call(
+        functools.partial(out_kernel, chips),
+        tuple(like((rows, 2 * width)) for _ in range(chips)),
+        [SM, VM] + [VM] * len(weights),
+        busy=3.0,
+        name="project",
+    )(place, mixed, *weights)
+
+
+def phases(length_now, row_count):
+    positions = (length_now + jnp.arange(row_count, dtype=jnp.int32)).astype(jnp.float32)
+    inverse = rope_base ** (-jnp.arange(0, HD, 2, dtype=jnp.int32).astype(jnp.float32) / HD)
+    phase = positions[:, None] * jnp.tile(inverse, 4)[None, :]
+    return jnp.cos(phase), jnp.sin(phase)
+
+
+def swap(x, axis, mask):
+    count = lax.axis_size(axis)
+    return lax.ppermute(x, axis, [(i, i ^ mask) for i in range(count)])
+
+
+CORE, SIDE_X, SIDE_Y = 1, 2, 4
+
+
+def core(x):
+    return swap(x, "req", CORE)
+
+
+def per_device(
+    hidden, norm_gain, w_query, w_key, w_value, w_out, cache_keys, cache_values, cache_lengths
+):
+    chip = lax.axis_index("req") // 2
+    odd = lax.axis_index("req") % 2
+    plane = lax.axis_index("tp")
+    place = jnp.stack([chip ^ plane, odd, plane])
+    length = lax.dynamic_slice_in_dim(cache_lengths, lax.axis_index("req"), 1, 0)
+    tokens = hidden.shape[1]
+
+    own, keep, send = pack(place, hidden[0], w_query, w_key, w_value)
+    from_x, from_y = swap(own, "req", SIDE_X), swap(own, "req", SIDE_Y)
+    columns = jnp.concatenate([keep, core(send)], axis=0)
+    arrived = {m: swap(columns, "tp", m) for m in (2, 3, 1)}
+    columns = [columns] + [arrived[m] for m in (1, 2, 3)]
+    half = own.shape[0] // 2
+    top, bottom, w_out_later = lax.optimization_barrier((from_x[:half], from_y[half:], w_out))
+    top, bottom = swap(top, "req", SIDE_Y), swap(bottom, "req", SIDE_X)
+    o_x, o_y, o_d = [swap(w_out_later, "req", m) for m in (SIDE_X, SIDE_Y, SIDE_X | SIDE_Y)]
+
+    partial, last, square = near_products(place, norm_gain, columns, [own, from_x, from_y])
+    cosine, sine = phases(length[0], tokens)
+    partial, cosine, sine = lax.optimization_barrier((partial, cosine, sine))
+    here, there = far_products(partial, last, square, top, bottom)
+    mixed, new_keys, new_values = attention(
+        length,
+        norm_gain.shape[0],
+        cosine,
+        sine,
+        here,
+        core(there),
+        cache_keys[0],
+        cache_values[0],
+    )
+    mixed, o_x, o_y, o_d = lax.optimization_barrier((mixed, o_x, o_y, o_d))
+    o_blocks = [w for block in (w_out, o_x, o_y, o_d) for w in (block, core(block))]
+    terms = project(mixed, place, o_blocks)
+    total = terms[0].astype(jnp.float32)
+    for m in (2, 3, 1):
+        total = total + swap(terms[m], "tp", m).astype(jnp.float32)
+    return total.astype(jnp.bfloat16)[None], new_keys[None], new_values[None]
+
+
+def general_rotate(tensor, cosine_table, sine_table):
     half_width = tensor.shape[-1] // 2
     front_half = tensor[..., :half_width]
     back_half = tensor[..., half_width:]
@@ -24,13 +399,9 @@
     )
 
 
-def phases(length_now, row_count, head_width):
-    positions = (length_now + jnp.arange(row_count, dtype=jnp.int32)).astype(jnp.float32)
-    inverse = rope_base ** (
-        -jnp.arange(0, head_width, 2, dtype=jnp.int32).astype(jnp.float32) / head_width
-    )
-    phase_grid = positions[:, None] * inverse[None, :]
-    return (jnp.cos(phase_grid)[:, None, :], jnp.sin(phase_grid)[:, None, :])
+def general_phases(length_now, row_count):
+    cosine, sine = phases(length_now, row_count)
+    return cosine[:, None, : HD // 2], sine[:, None, : HD // 2]
 
 
 def group_queries(flat_queries, key_heads, group_size, head_width):
@@ -88,7 +459,7 @@
     return running
 
 
-def per_device(
+def general_device(
     hidden, norm_gain, w_query, w_key, w_value, w_out, cache_keys, cache_values, cache_lengths
 ):
     token_count = hidden.shape[1]
@@ -119,13 +490,13 @@
     local_heads = query_width // head_width
     key_heads = key_width // head_width
     group_size = local_heads // key_heads
-    cosine_table, sine_table = phases(length_own, token_count, head_width)
+    cosine_table, sine_table = general_phases(length_own, token_count)
     flat_queries = (
-        rotate(query_sum.reshape(token_count, local_heads, head_width), cosine_table, sine_table)
+        general_rotate(query_sum.reshape(token_count, local_heads, head_width), cosine_table, sine_table)
         .astype(jnp.bfloat16)
         .reshape(token_count, query_width)
     )
-    fresh_keys = rotate(
+    fresh_keys = general_rotate(
         key_sum.reshape(token_count, key_heads, head_width), cosine_table, sine_table
     ).astype(jnp.bfloat16)
     fresh_values = value_sum.reshape(token_count, key_heads, head_width).astype(jnp.bfloat16)
@@ -180,6 +551,11 @@
         P(),
     )
     out_specs = (P("req", None, "tp"), P("req", None, "tp"), P("req", None, "tp"))
+    ringed = mesh.shape["req"] == 8 and mesh.shape["tp"] == 4
     return jax.shard_map(
-        per_device, mesh=mesh, in_specs=in_specs, out_specs=out_specs, check_vma=False
-    )
+        per_device if ringed else general_device,
+        mesh=mesh,
+        in_specs=in_specs,
+        out_specs=out_specs,
+        check_vma=False,
+    )

time: 104 us -> 61.5 us (0.59)
  blocking collectives: 38.4 us -> 0 us
  starting transfers between devices: 0.11 us -> 20.4 us
  between operations: 15.3 us -> 0.81 us
  Pallas kernels: 0 us -> 11.7 us
  waiting for transfers between devices: 34.8 us -> 24.8 us
  matrix products: 8 us -> 0 us
  other arithmetic: 3.33 us -> 1.76 us
  local copies, waits for them, and re-layouts: 3.31 us -> 1.87 us
    all_gather x3 -> x0, blocking collectives: 38.4 us -> none  [the longest x1 17.6 us: per_device(): gathered = lax.all_gather(hidden[0], 'tp', axis=1, tiled=True)]
    ppermute x0 -> x19, waiting for transfers between devices: none -> 24.8 us  [swap(): return lax.ppermute(x, axis, [(i, i ^ mask) for i in range(count)])]
    ppermute x0 -> x19, starting transfers between devices: none -> 20.4 us  [swap(): return lax.ppermute(x, axis, [(i, i ^ mask) for i in range(count)])]
    reduce_scatter x1 -> x0, waiting for transfers between devices: 20.3 us -> none  [per_device(): lax.psum_scatter(partial_out.astype(jnp.bfloat16), 'tp', scatter_dimensio...]
    all_gather x2 -> x0, waiting for transfers between devices: 13 us -> none  [the longest x1 13 us: per_device(): lax.all_gather(w_out, 'req', axis=1, tiled=True)]
    pallas_call x0 -> x5, Pallas kernels: none -> 11.7 us  [placed(): run(*[pltpu.with_memory_space_constraint(x, pltpu.HBM) if spec is HB else...]
    dot_general x8 -> x0, matrix products: 8 us -> none  [the longest x1 2.86 us: per_device(): jnp.dot(mixed_heads, lax.all_gather(w_out, 'req', axis=1, tiled=True), pr...]
    unnamed x3 -> x0, waiting for transfers between devices: 1.39 us -> none
  transfers between devices with their start and end apart: 3 -> 19, of which waited for: 2 -> 10; matrix products, arithmetic and copies ran while one was open for 11% -> 3% of each run, Pallas kernels for 0% -> 13%
where the time goes in v1:
time: 61.5 us; the launch traced here: 61.3 us
  waiting for transfers between devices  24.8 us (40%)
  starting transfers between devices  20.4 us (33%)
  Pallas kernels  11.7 us (19%)
  local copies, waits for them, and re-layouts  1.87 us (3%)
  other arithmetic  1.76 us (3%)
  between operations  0.81 us (1%)
    ppermute x19, waiting for transfers between devices, swap(): return lax.ppermute(x, axis, [(i, i ^ mask) for i in range(count)])  24.8 us
    ppermute x19, starting transfers between devices, swap(): return lax.ppermute(x, axis, [(i, i ^ mask) for i in range(count)])  20.4 us
    pallas_call x5, Pallas kernels, placed(): run(*[pltpu.with_memory_space_constraint(x, pltpu.HBM) if spec is HB else...  11.7 us
  transfers between devices with their start and end apart: 19, of which 10 were waited for; matrix products, arithmetic and copies ran while one was open for 3% of the time, Pallas kernels for 13%

profile of v1, /device:TPU:0, one launch (start us, length us, event | category | flops | bytes accessed | tf_op | source)
XLA Modules:
  0.0 61.3 jit_solution(16205658966528571362)
XLA Ops:
  0.7 1.6 %pack.1 = (bf16[256,768]{1,0:T(8,128)(2,1)S(1)}, bf16[128,256]{1,0:T(8,128)(2,1)S(1)}, bf16[128,256]{1,0:T(8,128)(2,1)S(1)}) custom-call(s32[3]{0:T(128)S(1)} %pad_add_fusion.place_ref, bf16[128,512]{1,0:T(8,128)(2,1)} %bitcast.13, bf16[256,512]{1,0:T(8,128)(2,1)} %wq_ref.1, bf16[256,128]{1,0:T(8,128)(2,1)} %wk_ref.1, bf16[256,128]{1,0:T(8,128)(2,1)} %wv_ref.1), custom_call_target="tpu_custom_call" | custom-call | flops 1100000000 | bytes 65536 | tf_op jit(solution)/shard_map/pack/pallas_call | solution.py:39
  2.4 3.0 %collective-permute-start.4 = (bf16[256,768]{1,0:T(8,128)(2,1)S(1)}, bf16[256,768]{1,0:T(8,128)(2,1)S(1)}, u32[]{:S(2)}, u32[]{:S(2)}) collective-permute-start(bf16[256,768]{1,0:T(8,128)(2,1)S(1)} %get-tuple-element.30.refs_4_), channel_id=1, source_target_pairs={{0,8},{4,12},{8,0},{12,4},{16,24},{20,28},{24,16},{28,20},{1,9},{5... | collective-permute-start | bytes 1179656 | tf_op jit(solution)/shard_map/ppermute | solution.py:336
  5.4 1.5 %collective-permute-start.5 = (bf16[256,768]{1,0:T(8,128)(2,1)S(1)}, bf16[256,768]{1,0:T(8,128)(2,1)S(1)}, u32[]{:S(2)}, u32[]{:S(2)}) collective-permute-start(bf16[256,768]{1,0:T(8,128)(2,1)S(1)} %get-tuple-element.30.refs_4_), channel_id=1, source_target_pairs={{0,16},{4,20},{8,24},{12,28},{16,0},{20,4},{24,8},{28,12},{1,17},{... | collective-permute-start | bytes 1179656 | tf_op jit(solution)/shard_map/ppermute | solution.py:336
  6.9 0.6 %copy-done.2 = s32[8]{0:T(128)S(1)} copy-done((s32[8]{0:T(128)S(1)}, s32[8]{0:T(128)}, u32[]{:S(2)}) %copy-start.2) | copy-done | bytes 56
  7.6 0.6 dynamic_slice.3.length_ref
  8.1 0.6 %add_convert_fusion.1 = f32[128]{0:T(128)S(1)} fusion(s32[]{:T(128)} %bitcast.4), kind=kLoop, calls=%fused_computation.8 | loop fusion | flops 256 | bytes 516 | tf_op jit(solution)/shard_map/convert_element_type | solution.py:328
  8.9 1.6 %collective-permute-start.1 = (bf16[256,256]{1,0:T(8,128)(2,1)S(1)}, bf16[256,256]{1,0:T(8,128)(2,1)S(1)}, u32[]{:S(2)}, u32[]{:S(2)}) collective-permute-start(bf16[256,256]{1,0:T(8,128)(2,1)S(1)} %constant_dynamic-update-slice_fusion.refs_0_), channel_id=1, source_target_pairs={{0,1},{1,0},{2,3},{3,2},{4,5},{5,4},{6,7},{7,6},{8,9},{9,8},{10,11... | collective-permute-start | bytes 393224 | tf_op jit(solution)/shard_map/ppermute | solution.py:336
  10.6 2.6 %collective-permute-start.2 = (bf16[256,256]{1,0:T(8,128)(2,1)S(1)}, bf16[256,256]{1,0:T(8,128)(2,1)S(1)}, u32[]{:S(2)}, u32[]{:S(2)}) collective-permute-start(bf16[256,256]{1,0:T(8,128)(2,1)S(1)} %constant_dynamic-update-slice_fusion.refs_0_), channel_id=1, source_target_pairs={{0,2},{1,3},{2,0},{3,1},{4,6},{5,7},{6,4},{7,5},{8,10},{9,11},{10,... | collective-permute-start | bytes 393224 | tf_op jit(solution)/shard_map/ppermute | solution.py:336
  13.7 0.8 %collective-permute-done.4.refs_5_ = bf16[256,768]{1,0:T(8,128)(2,1)S(1)} collective-permute-done((bf16[256,768]{1,0:T(8,128)(2,1)S(1)}, bf16[256,768]{1,0:T(8,128)(2,1)S(1)}, u32[]{:S(2)}, u32[]{:S(2)}) %collective-permute-start.4) | collective-permute-done | bytes 393248 | tf_op jit(solution)/shard_map/ppermute | solution.py:336
  14.5 1.4 %collective-permute-done.5.refs_6_ = bf16[256,768]{1,0:T(8,128)(2,1)S(1)} collective-permute-done((bf16[256,768]{1,0:T(8,128)(2,1)S(1)}, bf16[256,768]{1,0:T(8,128)(2,1)S(1)}, u32[]{:S(2)}, u32[]{:S(2)}) %collective-permute-start.5) | collective-permute-done | bytes 393248 | tf_op jit(solution)/shard_map/ppermute | solution.py:336
  16.0 1.6 %collective-permute-start.6 = (bf16[128,768]{1,0:T(8,128)(2,1)S(1)}, bf16[128,768]{1,0:T(8,128)(2,1)S(1)}, u32[]{:S(2)}, u32[]{:S(2)}) collective-permute-start(bf16[128,768]{1,0:T(8,128)(2,1)S(1)} %slice.8), channel_id=1, source_target_pairs={{0,16},{4,20},{8,24},{12,28},{16,0},{20,4},{24,8},{28,12},{1,17},{... | collective-permute-start | bytes 589832 | tf_op jit(solution)/shard_map/ppermute | solution.py:336
  18.1 5.4 %collective-permute-done.2.refs_2_ = bf16[256,256]{1,0:T(8,128)(2,1)S(1)} collective-permute-done((bf16[256,256]{1,0:T(8,128)(2,1)S(1)}, bf16[256,256]{1,0:T(8,128)(2,1)S(1)}, u32[]{:S(2)}, u32[]{:S(2)}) %collective-permute-start.2) | collective-permute-done | bytes 131104 | tf_op jit(solution)/shard_map/ppermute | solution.py:336
  23.5 1.2 %near_products.1 = (f32[256,768]{1,0:T(8,128)S(1)}, bf16[256,256]{1,0:T(8,128)(2,1)S(1)}, f32[256,128]{1,0:T(8,128)S(1)}) custom-call(s32[3]{0:T(128)S(1)} %pad_add_fusion.place_ref, bf16[8,1,256]{2,1,0:T(2,128)(2,1)S(1)} %reshape.24.gain_ref, bf16[256,256]{1,0:T(8,128)(2,1)S(1)} %constant_dynamic-update-slice_fusion.refs_0_, ...), custom_call_target="tpu_custom_call" | custom-call | flops 2200000000 | bytes 65536 | tf_op jit(solution)/shard_map/near_products/pallas_call | solution.py:39
  26.7 2.5 %collective-permute-start.11 = (bf16[512,256]{1,0:T(8,128)(2,1)S(1)}, bf16[512,256]{1,0:T(8,128)(2,1)S(1)}, u32[]{:S(2)}, u32[]{:S(2)}) collective-permute-start(bf16[512,256]{1,0:T(8,128)(2,1)S(1)} %copy-done), channel_id=1, source_target_pairs={{0,24},{4,28},{8,16},{12,20},{16,8},{20,12},{24,0},{28,4},{1,25},{... | collective-permute-start | bytes 786440 | tf_op jit(solution)/shard_map/ppermute | solution.py:336
  29.1 7.0 %attention.1 = (bf16[128,512]{1,0:T(8,128)(2,1)S(1)}, bf16[128,128]{1,0:T(8,128)(2,1)}, bf16[128,128]{1,0:T(8,128)(2,1)}) custom-call(s32[1]{0:T(128)} %dynamic_slice.3.length_ref, f32[128,128]{1,0:T(8,128)S(1)} %get-tuple-element.32.cos_ref, f32[128,128]{1,0:T(8,128)S(1)} %get-tuple-element.33.sin_ref, f32[128,896]{1,0:T(8,128)S(1)} %get-tuple-element.39.here_ref, ...), custom_call_target="tpu_custom_call" | custom-call | flops 9900000256 | bytes 65536 | tf_op jit(solution)/shard_map/attention/pallas_call | solution.py:39
  36.1 4.1 %collective-permute-done.10.refs_4_ = bf16[512,256]{1,0:T(8,128)(2,1)S(1)} collective-permute-done((bf16[512,256]{1,0:T(8,128)(2,1)S(1)}, bf16[512,256]{1,0:T(8,128)(2,1)S(1)}, u32[]{:S(2)}, u32[]{:S(2)}) %collective-permute-start.10) | collective-permute-done | bytes 262176 | tf_op jit(solution)/shard_map/ppermute | solution.py:336
  40.7 1.0 %collective-permute-done.13.refs_3_ = bf16[512,256]{1,0:T(8,128)(2,1)S(1)} collective-permute-done((bf16[512,256]{1,0:T(8,128)(2,1)S(1)}, bf16[512,256]{1,0:T(8,128)(2,1)S(1)}, u32[]{:S(2)}, u32[]{:S(2)}) %collective-permute-start.13) | collective-permute-done | bytes 262176 | tf_op jit(solution)/shard_map/ppermute | solution.py:336
  42.5 1.6 %project.1 = (bf16[128,512]{1,0:T(8,128)(2,1)S(1)}, bf16[128,512]{1,0:T(8,128)(2,1)S(1)}, bf16[128,512]{1,0:T(8,128)(2,1)S(1)}, bf16[128,512]{1,0:T(8,128)(2,1)S(1)}) custom-call(s32[3]{0:T(128)S(1)} %pad_add_fusion.place_ref, bf16[128,512]{1,0:T(8,128)(2,1)S(1)} %get-tuple-element.43.mixed_ref, bf16[512,256]{1,0:T(8,128)(2,1)S(1)} %copy-done, ...), custom_call_target="tpu_custom_call" | custom-call | flops 3300000000 | bytes 65536 | tf_op jit(solution)/shard_map/project/pallas_call | solution.py:39
  44.1 2.7 %collective-permute-start.18 = (bf16[128,512]{1,0:T(8,128)(2,1)S(1)}, bf16[128,512]{1,0:T(8,128)(2,1)S(1)}, u32[]{:S(2)}, u32[]{:S(2)}) collective-permute-start(bf16[128,512]{1,0:T(8,128)(2,1)S(1)} %get-tuple-element.50), channel_id=1, source_target_pairs={{0,1},{1,0},{2,3},{3,2},{4,5},{5,4},{6,7},{7,6},{8,9},{9,8},{10,11... | collective-permute-start | bytes 393224 | tf_op jit(solution)/shard_map/ppermute | solution.py:336
  46.8 2.5 %collective-permute-start.17 = (bf16[128,512]{1,0:T(8,128)(2,1)S(1)}, bf16[128,512]{1,0:T(8,128)(2,1)S(1)}, u32[]{:S(2)}, u32[]{:S(2)}) collective-permute-start(bf16[128,512]{1,0:T(8,128)(2,1)S(1)} %get-tuple-element.49), channel_id=1, source_target_pairs={{0,3},{1,2},{2,1},{3,0},{4,7},{5,6},{6,5},{7,4},{8,11},{9,10},{10,... | collective-permute-start | bytes 393224 | tf_op jit(solution)/shard_map/ppermute | solution.py:336
  49.3 1.3 %collective-permute-done.18 = bf16[128,512]{1,0:T(8,128)(2,1)S(1)} collective-permute-done((bf16[128,512]{1,0:T(8,128)(2,1)S(1)}, bf16[128,512]{1,0:T(8,128)(2,1)S(1)}, u32[]{:S(2)}, u32[]{:S(2)}) %collective-permute-start.18) | collective-permute-done | bytes 131104 | tf_op jit(solution)/shard_map/ppermute | solution.py:336
  50.6 5.9 %collective-permute-done.17 = bf16[128,512]{1,0:T(8,128)(2,1)S(1)} collective-permute-done((bf16[128,512]{1,0:T(8,128)(2,1)S(1)}, bf16[128,512]{1,0:T(8,128)(2,1)S(1)}, u32[]{:S(2)}, u32[]{:S(2)}) %collective-permute-start.17) | collective-permute-done | bytes 131104 | tf_op jit(solution)/shard_map/ppermute | solution.py:336
  56.5 4.1 %collective-permute-done.16 = bf16[128,512]{1,0:T(8,128)(2,1)S(1)} collective-permute-done((bf16[128,512]{1,0:T(8,128)(2,1)S(1)}, bf16[128,512]{1,0:T(8,128)(2,1)S(1)}, u32[]{:S(2)}, u32[]{:S(2)}) %collective-permute-start.16) | collective-permute-done | bytes 131104 | tf_op jit(solution)/shard_map/ppermute | solution.py:336
  60.6 0.7 %fusion = bf16[1,128,512]{2,1,0:T(8,128)(2,1)} fusion(bf16[128,512]{1,0:T(8,128)(2,1)S(1)} %collective-permute-done.18, bf16[128,512]{1,0:T(8,128)(2,1)S(1)} %collective-permute-done.17, bf16[128,512]{1,0:T(8,128)(2,1)S(1)} %collective-permute-done.16, bf16[128,512]{1,0:T(8,128)(2,1)S(1)} %get-tuple-element.47), kind=kLoop, calls=%fused_computation.1 | loop fusion | flops 524288 | bytes 655360 | tf_op jit(solution)/shard_map/broadcast_in_dim | solution.py:386
  (38 shorter events, 4.5 us)
Async XLA Ops:
  2.4 12.1 %collective-permute-start.4 = (bf16[256,768]{1,0:T(8,128)(2,1)S(1)}, bf16[256,768]{1,0:T(8,128)(2,1)S(1)}, u32[]{:S(2)}, u32[]{:S(2)}) collective-permute-start(bf16[256,768]{1,0:T(8,128)(2,1)S(1)} %get-tuple-element.30.refs_4_), channel_id=1, source_target_pairs={{0,8},{4,12},{8,0},{12,4},{16,24},{20,28},{24,16},{28,20},{1,9},{5... | collective-permute-start | bytes 1179656 | tf_op jit(solution)/shard_map/ppermute | solution.py:336
  5.4 10.6 %collective-permute-start.5 = (bf16[256,768]{1,0:T(8,128)(2,1)S(1)}, bf16[256,768]{1,0:T(8,128)(2,1)S(1)}, u32[]{:S(2)}, u32[]{:S(2)}) collective-permute-start(bf16[256,768]{1,0:T(8,128)(2,1)S(1)} %get-tuple-element.30.refs_4_), channel_id=1, source_target_pairs={{0,16},{4,20},{8,24},{12,28},{16,0},{20,4},{24,8},{28,12},{1,17},{... | collective-permute-start | bytes 1179656 | tf_op jit(solution)/shard_map/ppermute | solution.py:336
  6.9 2.0 %collective-permute-start = (bf16[128,256]{1,0:T(8,128)(2,1)S(1)}, bf16[128,256]{1,0:T(8,128)(2,1)S(1)}, u32[]{:S(2)}, u32[]{:S(2)}) collective-permute-start(bf16[128,256]{1,0:T(8,128)(2,1)S(1)} %get-tuple-element.29), channel_id=1, source_target_pairs={{0,4},{4,0},{8,12},{12,8},{16,20},{20,16},{24,28},{28,24},{1,5},{5... | collective-permute-start | bytes 196616 | tf_op jit(solution)/shard_map/ppermute | solution.py:336
  6.9 0.7 %copy-start.2 = (s32[8]{0:T(128)S(1)}, s32[8]{0:T(128)}, u32[]{:S(2)}) copy-start(s32[8]{0:T(128)} %param.17) | copy-start | bytes 100
  7.6 1.2 %copy-start.1 = (bf16[2048]{0:T(1024)(128)(2,1)S(1)}, bf16[2048]{0:T(1024)(128)(2,1)}, u32[]{:S(2)}) copy-start(bf16[2048]{0:T(1024)(128)(2,1)} %param.10) | copy-start | bytes 12292
  8.9 9.2 %collective-permute-start.1 = (bf16[256,256]{1,0:T(8,128)(2,1)S(1)}, bf16[256,256]{1,0:T(8,128)(2,1)S(1)}, u32[]{:S(2)}, u32[]{:S(2)}) collective-permute-start(bf16[256,256]{1,0:T(8,128)(2,1)S(1)} %constant_dynamic-update-slice_fusion.refs_0_), channel_id=1, source_target_pairs={{0,1},{1,0},{2,3},{3,2},{4,5},{5,4},{6,7},{7,6},{8,9},{9,8},{10,11... | collective-permute-start | bytes 393224 | tf_op jit(solution)/shard_map/ppermute | solution.py:336
  10.6 12.9 %collective-permute-start.2 = (bf16[256,256]{1,0:T(8,128)(2,1)S(1)}, bf16[256,256]{1,0:T(8,128)(2,1)S(1)}, u32[]{:S(2)}, u32[]{:S(2)}) collective-permute-start(bf16[256,256]{1,0:T(8,128)(2,1)S(1)} %constant_dynamic-update-slice_fusion.refs_0_), channel_id=1, source_target_pairs={{0,2},{1,3},{2,0},{3,1},{4,6},{5,7},{6,4},{7,5},{8,10},{9,11},{10,... | collective-permute-start | bytes 393224 | tf_op jit(solution)/shard_map/ppermute | solution.py:336
  13.2 10.3 %collective-permute-start.3 = (bf16[256,256]{1,0:T(8,128)(2,1)S(1)}, bf16[256,256]{1,0:T(8,128)(2,1)S(1)}, u32[]{:S(2)}, u32[]{:S(2)}) collective-permute-start(bf16[256,256]{1,0:T(8,128)(2,1)S(1)} %constant_dynamic-update-slice_fusion.refs_0_), channel_id=1, source_target_pairs={{0,3},{1,2},{2,1},{3,0},{4,7},{5,6},{6,5},{7,4},{8,11},{9,10},{10,... | collective-permute-start | bytes 393224 | tf_op jit(solution)/shard_map/ppermute | solution.py:336
  16.0 8.7 %collective-permute-start.6 = (bf16[128,768]{1,0:T(8,128)(2,1)S(1)}, bf16[128,768]{1,0:T(8,128)(2,1)S(1)}, u32[]{:S(2)}, u32[]{:S(2)}) collective-permute-start(bf16[128,768]{1,0:T(8,128)(2,1)S(1)} %slice.8), channel_id=1, source_target_pairs={{0,16},{4,20},{8,24},{12,28},{16,0},{20,4},{24,8},{28,12},{1,17},{... | collective-permute-start | bytes 589832 | tf_op jit(solution)/shard_map/ppermute | solution.py:336
  17.5 7.1 %collective-permute-start.7 = (bf16[128,768]{1,0:T(8,128)(2,1)S(1)}, bf16[128,768]{1,0:T(8,128)(2,1)S(1)}, u32[]{:S(2)}, u32[]{:S(2)}) collective-permute-start(bf16[128,768]{1,0:T(8,128)(2,1)S(1)} %slice.9), channel_id=1, source_target_pairs={{0,8},{4,12},{8,0},{12,4},{16,24},{20,28},{24,16},{28,20},{1,9},{5... | collective-permute-start | bytes 589832 | tf_op jit(solution)/shard_map/ppermute | solution.py:336
  24.7 1.0 %copy-start = (bf16[512,256]{1,0:T(8,128)(2,1)S(1)}, bf16[512,256]{1,0:T(8,128)(2,1)}, u32[]{:S(2)}) copy-start(bf16[512,256]{1,0:T(8,128)(2,1)} %refs_0_.1) | copy-start | bytes 786436
  25.0 4.1 %collective-permute-start.8 = (f32[128,896]{1,0:T(8,128)S(1)}, f32[128,896]{1,0:T(8,128)S(1)}, u32[]{:S(2)}, u32[]{:S(2)}) collective-permute-start(f32[128,896]{1,0:T(8,128)S(1)} %get-tuple-element.40), channel_id=1, source_target_pairs={{0,4},{4,0},{8,12},{12,8},{16,20},{20,16},{24,28},{28,24},{1,5},{5... | collective-permute-start | bytes 1376264 | tf_op jit(solution)/shard_map/ppermute | solution.py:336
  25.6 15.1 %collective-permute-start.12 = (bf16[512,256]{1,0:T(8,128)(2,1)S(1)}, bf16[512,256]{1,0:T(8,128)(2,1)S(1)}, u32[]{:S(2)}, u32[]{:S(2)}) collective-permute-start(bf16[512,256]{1,0:T(8,128)(2,1)S(1)} %copy-done), channel_id=1, source_target_pairs={{0,4},{4,0},{8,12},{12,8},{16,20},{20,16},{24,28},{28,24},{1,5},{5... | collective-permute-start | bytes 786440 | tf_op jit(solution)/shard_map/ppermute | solution.py:336
  25.6 10.5 %collective-permute-start.9 = (bf16[512,256]{1,0:T(8,128)(2,1)S(1)}, bf16[512,256]{1,0:T(8,128)(2,1)S(1)}, u32[]{:S(2)}, u32[]{:S(2)}) collective-permute-start(bf16[512,256]{1,0:T(8,128)(2,1)S(1)} %copy-done), channel_id=1, source_target_pairs={{0,8},{4,12},{8,0},{12,4},{16,24},{20,28},{24,16},{28,20},{1,9},{5... | collective-permute-start | bytes 786440 | tf_op jit(solution)/shard_map/ppermute | solution.py:336
  26.2 14.1 %collective-permute-start.10 = (bf16[512,256]{1,0:T(8,128)(2,1)S(1)}, bf16[512,256]{1,0:T(8,128)(2,1)S(1)}, u32[]{:S(2)}, u32[]{:S(2)}) collective-permute-start(bf16[512,256]{1,0:T(8,128)(2,1)S(1)} %copy-done), channel_id=1, source_target_pairs={{0,16},{4,20},{8,24},{12,28},{16,0},{20,4},{24,8},{28,12},{1,17},{... | collective-permute-start | bytes 786440 | tf_op jit(solution)/shard_map/ppermute | solution.py:336
  26.7 13.6 %collective-permute-start.11 = (bf16[512,256]{1,0:T(8,128)(2,1)S(1)}, bf16[512,256]{1,0:T(8,128)(2,1)S(1)}, u32[]{:S(2)}, u32[]{:S(2)}) collective-permute-start(bf16[512,256]{1,0:T(8,128)(2,1)S(1)} %copy-done), channel_id=1, source_target_pairs={{0,24},{4,28},{8,16},{12,20},{16,8},{20,12},{24,0},{28,4},{1,25},{... | collective-permute-start | bytes 786440 | tf_op jit(solution)/shard_map/ppermute | solution.py:336
  40.2 1.5 %collective-permute-start.13 = (bf16[512,256]{1,0:T(8,128)(2,1)S(1)}, bf16[512,256]{1,0:T(8,128)(2,1)S(1)}, u32[]{:S(2)}, u32[]{:S(2)}) collective-permute-start(bf16[512,256]{1,0:T(8,128)(2,1)S(1)} %collective-permute-done.9.refs_2_), channel_id=1, source_target_pairs={{0,4},{4,0},{8,12},{12,8},{16,20},{20,16},{24,28},{28,24},{1,5},{5... | collective-permute-start | bytes 786440 | tf_op jit(solution)/shard_map/ppermute | solution.py:336
  40.2 1.9 %collective-permute-start.14 = (bf16[512,256]{1,0:T(8,128)(2,1)S(1)}, bf16[512,256]{1,0:T(8,128)(2,1)S(1)}, u32[]{:S(2)}, u32[]{:S(2)}) collective-permute-start(bf16[512,256]{1,0:T(8,128)(2,1)S(1)} %collective-permute-done.10.refs_4_), channel_id=1, source_target_pairs={{0,4},{4,0},{8,12},{12,8},{16,20},{20,16},{24,28},{28,24},{1,5},{5... | collective-permute-start | bytes 786440 | tf_op jit(solution)/shard_map/ppermute | solution.py:336
  40.7 1.8 %collective-permute-start.15 = (bf16[512,256]{1,0:T(8,128)(2,1)S(1)}, bf16[512,256]{1,0:T(8,128)(2,1)S(1)}, u32[]{:S(2)}, u32[]{:S(2)}) collective-permute-start(bf16[512,256]{1,0:T(8,128)(2,1)S(1)} %collective-permute-done.11.refs_6_), channel_id=1, source_target_pairs={{0,4},{4,0},{8,12},{12,8},{16,20},{20,16},{24,28},{28,24},{1,5},{5... | collective-permute-start | bytes 786440 | tf_op jit(solution)/shard_map/ppermute | solution.py:336
  44.1 6.5 %collective-permute-start.18 = (bf16[128,512]{1,0:T(8,128)(2,1)S(1)}, bf16[128,512]{1,0:T(8,128)(2,1)S(1)}, u32[]{:S(2)}, u32[]{:S(2)}) collective-permute-start(bf16[128,512]{1,0:T(8,128)(2,1)S(1)} %get-tuple-element.50), channel_id=1, source_target_pairs={{0,1},{1,0},{2,3},{3,2},{4,5},{5,4},{6,7},{7,6},{8,9},{9,8},{10,11... | collective-permute-start | bytes 393224 | tf_op jit(solution)/shard_map/ppermute | solution.py:336
  46.8 9.7 %collective-permute-start.17 = (bf16[128,512]{1,0:T(8,128)(2,1)S(1)}, bf16[128,512]{1,0:T(8,128)(2,1)S(1)}, u32[]{:S(2)}, u32[]{:S(2)}) collective-permute-start(bf16[128,512]{1,0:T(8,128)(2,1)S(1)} %get-tuple-element.49), channel_id=1, source_target_pairs={{0,3},{1,2},{2,1},{3,0},{4,7},{5,6},{6,5},{7,4},{8,11},{9,10},{10,... | collective-permute-start | bytes 393224 | tf_op jit(solution)/shard_map/ppermute | solution.py:336
  49.3 11.3 %collective-permute-start.16 = (bf16[128,512]{1,0:T(8,128)(2,1)S(1)}, bf16[128,512]{1,0:T(8,128)(2,1)S(1)}, u32[]{:S(2)}, u32[]{:S(2)}) collective-permute-start(bf16[128,512]{1,0:T(8,128)(2,1)S(1)} %get-tuple-element.48), channel_id=1, source_target_pairs={{0,2},{1,3},{2,0},{3,1},{4,6},{5,7},{6,4},{7,5},{8,10},{9,11},{10,... | collective-permute-start | bytes 393224 | tf_op jit(solution)/shard_map/ppermute | solution.py:336

commit v2 on v1

--- a/solution.py
+++ b/solution.py
@@ -57,36 +57,70 @@
     return copies
 
 
-def pack_kernel(place_ref, hidden_ref, wq_ref, wk_ref, wv_ref, w_out, keep_out, send_out, sems):
+def pack_kernel(
+    place_ref,
+    hidden_ref,
+    wq_ref,
+    wk_ref,
+    wv_ref,
+    wo_ref,
+    top_out,
+    bottom_out,
+    keep_out,
+    send_out,
+    sems,
+):
     odd = place_ref[1]
+    rows, width = wq_ref.shape
+    half, column = rows // 2, top_out.shape[1]
+    kv = wk_ref.shape[1]
+    pairs = []
+    for part, out in enumerate((top_out, bottom_out)):
+        source = pl.ds(part * half, half)
+        first = 0
+        for c in range(width // column):
+            pairs.append((wq_ref.at[source, pl.ds(c * column, column)], out.at[pl.ds(first, half)]))
+            first += half
+        for i, w in enumerate((wk_ref, wv_ref)):
+            pairs.append((w.at[source], out.at[pl.ds(first, half), pl.ds(i * kv, kv)]))
+        first += half
+        depth = wo_ref.shape[0] // 2
+        pairs.append((wo_ref.at[pl.ds(part * depth, depth)], out.at[pl.ds(first, depth)]))
     half = keep_out.shape[1]
     mine = pl.ds(pl.multiple_of(odd * half, half), half)
     other = pl.ds(pl.multiple_of((1 - odd) * half, half), half)
-    pairs = [(hidden_ref.at[:, other], send_out), (hidden_ref.at[:, mine], keep_out)]
-    first = 0
-    for w in (wq_ref, wk_ref, wv_ref):
-        width = w.shape[1]
-        pairs.append((w, w_out.at[:, pl.ds(first, width)]))
-        first += width
+    pairs += [(hidden_ref.at[:, other], send_out), (hidden_ref.at[:, mine], keep_out)]
     for copy in fetch(pairs, sems):
         copy.wait()
 
 
-def pack(place, hidden, w_query, w_key, w_value):
-    width = w_query.shape[1] + w_key.shape[1] + w_value.shape[1]
+def pack(place, hidden, w_query, w_key, w_value, w_out):
+    column = 2 * w_key.shape[1]
+    rows = w_query.shape[0] // 2 * (w_query.shape[1] // column + 1) + w_out.shape[0] // 2
     columns = like((hidden.shape[0], hidden.shape[1] // 2))
     return call(
         pack_kernel,
-        (like((w_query.shape[0], width)), columns, columns),
-        [SM] + [HB] * 4,
-        scratch=[pltpu.SemaphoreType.DMA((5,))],
+        (like((rows, column)), like((rows, column)), columns, columns),
+        [SM] + [HB] * 5,
+        scratch=[pltpu.SemaphoreType.DMA((12,))],
         name="pack",
-    )(place, hidden, w_query, w_key, w_value)
+    )(place, hidden, w_query, w_key, w_value, w_out)
+
+
+def product(rows, top_ref, bottom_ref):
+    half = rows.shape[1] // 2
+    parts = []
+    for first in range(0, 3 * half, half):
+        block = jnp.concatenate(
+            [top_ref[first : first + half], bottom_ref[first : first + half]], axis=0
+        )
+        parts.append(jnp.dot(rows, block, preferred_element_type=jnp.float32))
+    return jnp.concatenate(parts, axis=1)
 
 
 def near_kernel(shards, place_ref, gain_ref, *refs):
-    columns, weights = refs[:shards], refs[shards : 2 * shards - 1]
-    partial_out, last_out, square_out, buf = refs[2 * shards - 1 :]
+    columns, weights = refs[:shards], refs[shards : 3 * shards - 2]
+    partial_out, last_out, square_out, project_out, buf = refs[3 * shards - 2 :]
     mine, odd, plane = place_ref[0], place_ref[1], place_ref[2]
     square = 0.0
     for m in range(shards):
@@ -96,35 +130,37 @@
         buf[m] = (rows * gain).astype(jnp.bfloat16)
     square_out[...] = jnp.broadcast_to(square, square_out.shape)
     partial_out[...] = sum(
-        jnp.dot(buf[mine ^ j], w[...], preferred_element_type=jnp.float32)
-        for j, w in enumerate(weights)
+        product(buf[mine ^ j], weights[2 * j], weights[2 * j + 1]) for j in range(shards - 1)
     )
     last_out[...] = buf[mine ^ (shards - 1)]
-
-
-def near_products(place, gain, columns, weights):
+    depth = project_out.shape[1] // 2
+    first = weights[0].shape[0] - depth
+    for j in range(shards - 1):
+        project_out[j, :depth] = weights[2 * j][first:]
+        project_out[j, depth:] = weights[2 * j + 1][first:]
+
+
+def near_products(place, gain, columns, weights, q_rows):
     shards = len(columns)
     rows, width = columns[0].shape
+    depth = weights[0].shape[0] - q_rows
     return call(
         functools.partial(near_kernel, shards),
         (
-            like((rows, weights[0].shape[1]), jnp.float32),
+            like((rows, 3 * width), jnp.float32),
             like((rows, width)),
             like((rows, 128), jnp.float32),
+            like((shards - 1, 2 * depth, weights[0].shape[1])),
         ),
-        [SM, VM] + [VM] * (2 * shards - 1),
+        [SM, VM] + [VM] * (3 * shards - 2),
         scratch=[pltpu.VMEM((shards, rows, width), jnp.bfloat16)],
-        busy=2.0,
+        busy=0.1,
         name="near_products",
     )(place, gain.reshape(2 * shards, 1, width), *columns, *weights)
 
 
 def far_kernel(partial_ref, last_ref, square_ref, top_ref, bottom_ref, keep_out, send_out):
-    half = top_ref.shape[0]
-    total = partial_ref[...]
-    for i, w in enumerate((top_ref, bottom_ref)):
-        part = last_ref[:, i * half : (i + 1) * half]
-        total += jnp.dot(part, w[...], preferred_element_type=jnp.float32)
+    total = partial_ref[...] + product(last_ref[...], top_ref, bottom_ref)
     tokens = keep_out.shape[0]
     width = total.shape[1]
     for out, first in ((keep_out, 0), (send_out, tokens)):
@@ -139,7 +175,7 @@
         far_kernel,
         (out, out),
         [VM] * 5,
-        busy=1.0,
+        busy=0.1,
         name="far_products",
     )(partial, last, square, top, bottom)
 
@@ -286,42 +322,49 @@
             pltpu.VMEM(keys.shape, jnp.bfloat16),
             pltpu.SemaphoreType.DMA((2,)),
         ],
-        busy=9.0,
+        busy=4.0,
         name="attention",
     )(length, cosine, sine, here, there, keys, values)
 
 
-def out_kernel(chips, place_ref, mixed_ref, *refs):
-    weights, outs = refs[: 2 * chips], refs[2 * chips :]
+def out_kernel(distances, chips, place_ref, mixed_ref, own_ref, sibling_ref, *refs):
+    last, outs = refs[:4], refs[4:]
     mine, odd = place_ref[0], place_ref[1]
-    width = weights[0].shape[1]
     mixed = mixed_ref[...]
-    for j in range(chips):
-        own, sib = [
-            jnp.dot(mixed, w[...], preferred_element_type=jnp.float32).astype(jnp.bfloat16)
-            for w in weights[2 * j : 2 * j + 2]
+    width = outs[0].shape[1] // 2
+
+    def store(out, weights):
+        terms = [
+            jnp.dot(mixed, w, preferred_element_type=jnp.float32).astype(jnp.bfloat16)
+            for w in weights
         ]
-        lower = jnp.where(odd == 0, own, sib)
-        upper = jnp.where(odd == 0, sib, own)
-        for m in range(chips):
-
-            @pl.when((mine ^ j) == m)
-            def _(m=m, lower=lower, upper=upper):
-                outs[m][:, :width] = lower
-                outs[m][:, width:] = upper
-
-
-def project(mixed, place, weights):
-    chips = len(weights) // 2
+        out[:, :width] = jnp.where(odd == 0, terms[0], terms[1])
+        out[:, width:] = jnp.where(odd == 0, terms[1], terms[0])
+
+    for out, m in zip(outs, distances, strict=True):
+        j = mine ^ m
+
+        @pl.when(j < chips - 1)
+        def _(out=out, j=j):
+            store(out, [own_ref[j], sibling_ref[j]])
+
+        @pl.when(j == chips - 1)
+        def _(out=out):
+            depth = last[2].shape[0]
+            halves = [h[h.shape[0] - depth :] for h in last]
+            store(out, [jnp.concatenate(halves[:2], axis=0), jnp.concatenate(halves[2:], axis=0)])
+
+
+def project(distances, mixed, place, own, sibling, last):
     rows = mixed.shape[0]
-    width = weights[0].shape[1]
+    width = own.shape[2]
     return call(
-        functools.partial(out_kernel, chips),
-        tuple(like((rows, 2 * width)) for _ in range(chips)),
-        [SM, VM] + [VM] * len(weights),
-        busy=3.0,
+        functools.partial(out_kernel, distances, own.shape[0] + 1),
+        tuple(like((rows, 2 * width)) for _ in distances),
+        [SM] + [VM] * 7,
+        busy=1.0,
         name="project",
-    )(place, mixed, *weights)
+    )(place, mixed, own, sibling, *last)
 
 
 def phases(length_now, row_count):
@@ -353,20 +396,27 @@
     length = lax.dynamic_slice_in_dim(cache_lengths, lax.axis_index("req"), 1, 0)
     tokens = hidden.shape[1]
 
-    own, keep, send = pack(place, hidden[0], w_query, w_key, w_value)
-    from_x, from_y = swap(own, "req", SIDE_X), swap(own, "req", SIDE_Y)
-    columns = jnp.concatenate([keep, core(send)], axis=0)
-    arrived = {m: swap(columns, "tp", m) for m in (2, 3, 1)}
-    columns = [columns] + [arrived[m] for m in (1, 2, 3)]
-    half = own.shape[0] // 2
-    top, bottom, w_out_later = lax.optimization_barrier((from_x[:half], from_y[half:], w_out))
-    top, bottom = swap(top, "req", SIDE_Y), swap(bottom, "req", SIDE_X)
-    o_x, o_y, o_d = [swap(w_out_later, "req", m) for m in (SIDE_X, SIDE_Y, SIDE_X | SIDE_Y)]
-
-    partial, last, square = near_products(place, norm_gain, columns, [own, from_x, from_y])
+    top, bottom, keep, send = pack(place, hidden[0], w_query, w_key, w_value, w_out)
+    x_top, y_bottom = swap(top, "req", SIDE_X), swap(bottom, "req", SIDE_Y)
+    got, top_later, bottom_later = lax.optimization_barrier((core(send), top, bottom))
+    x_bottom, y_top = swap(bottom_later, "req", SIDE_X), swap(top_later, "req", SIDE_Y)
+    columns = jnp.concatenate([keep, got], axis=0)
+    two = swap(columns, "tp", 2)
+    q_rows = w_query.shape[0] // 2 * 3
+    d_top, d_bottom = swap(x_top, "req", SIDE_Y), swap(y_bottom, "req", SIDE_X)
+    _, _, columns_later, two_later = lax.optimization_barrier((x_top, y_bottom, columns, two))
+    one, three = swap(columns_later, "tp", 1), swap(two_later, "tp", 1)
+
+    partial, last, square, o_near = near_products(
+        place,
+        norm_gain,
+        [columns, one, two, three],
+        [top, bottom, x_top, x_bottom, y_top, y_bottom],
+        q_rows,
+    )
     cosine, sine = phases(length[0], tokens)
     partial, cosine, sine = lax.optimization_barrier((partial, cosine, sine))
-    here, there = far_products(partial, last, square, top, bottom)
+    here, there = far_products(partial, last, square, d_top, d_bottom)
     mixed, new_keys, new_values = attention(
         length,
         norm_gain.shape[0],
@@ -377,11 +427,14 @@
         cache_keys[0],
         cache_values[0],
     )
-    mixed, o_x, o_y, o_d = lax.optimization_barrier((mixed, o_x, o_y, o_d))
-    o_blocks = [w for block in (w_out, o_x, o_y, o_d) for w in (block, core(block))]
-    terms = project(mixed, place, o_blocks)
+    o_sibling = core(o_near)
+    o_last = [d_top, d_bottom, core(d_top[q_rows:]), core(d_bottom[q_rows:])]
+    terms = {}
+    terms[2], terms[3] = project((2, 3), mixed, place, o_near, o_sibling, o_last)
+    mixed, terms[2], terms[3] = lax.optimization_barrier((mixed, terms[2], terms[3]))
+    terms[0], terms[1] = project((0, 1), mixed, place, o_near, o_sibling, o_last)
     total = terms[0].astype(jnp.float32)
-    for m in (2, 3, 1):
+    for m in (1, 2, 3):
         total = total + swap(terms[m], "tp", m).astype(jnp.float32)
     return total.astype(jnp.bfloat16)[None], new_keys[None], new_values[None]
 

time: 61.5 us -> 54.1 us (0.88)
  waiting for transfers between devices: 24.8 us -> 17 us
  starting transfers between devices: 20.4 us -> 21.3 us
  Pallas kernels: 11.7 us -> 12.4 us
    ppermute x19 -> x17, waiting for transfers between devices: 24.8 us -> 17 us  [swap(): return lax.ppermute(x, axis, [(i, i ^ mask) for i in range(count)])]
    ppermute x19 -> x17, starting transfers between devices: 20.4 us -> 21.3 us  [swap(): return lax.ppermute(x, axis, [(i, i ^ mask) for i in range(count)])]
    pallas_call x5 -> x6, Pallas kernels: 11.7 us -> 12.4 us  [placed(): run(*[pltpu.with_memory_space_constraint(x, pltpu.HBM) if spec is HB else...]
  transfers between devices with their start and end apart: 19 -> 17, of which waited for: 10 -> 7; matrix products, arithmetic and copies ran while one was open for 3% -> 3% of each run, Pallas kernels for 13% -> 17%
where the time goes in v2:
time: 54.1 us; the launch traced here: 54.5 us
  starting transfers between devices  21.3 us (39%)
  waiting for transfers between devices  17 us (31%)
  Pallas kernels  12.4 us (23%)
  other arithmetic  1.76 us (3%)
  local copies, waits for them, and re-layouts  1.28 us (2%)
  between operations  0.81 us (1%)
    ppermute x17, starting transfers between devices, swap(): return lax.ppermute(x, axis, [(i, i ^ mask) for i in range(count)])  21.3 us
    ppermute x17, waiting for transfers between devices, swap(): return lax.ppermute(x, axis, [(i, i ^ mask) for i in range(count)])  17 us
    pallas_call x6, Pallas kernels, placed(): run(*[pltpu.with_memory_space_constraint(x, pltpu.HBM) if spec is HB else...  12.4 us
  transfers between devices with their start and end apart: 17, of which 7 were waited for; matrix products, arithmetic and copies ran while one was open for 3% of the time, Pallas kernels for 17%

profile of v2, /device:TPU:0, one launch (start us, length us, event | category | flops | bytes accessed | tf_op | source)
XLA Modules:
  0.0 54.5 jit_solution(11035437644366582506)
XLA Ops:
  0.7 1.8 %pack.1 = (bf16[640,256]{1,0:T(8,128)(2,1)S(1)}, bf16[640,256]{1,0:T(8,128)(2,1)S(1)}, bf16[128,256]{1,0:T(8,128)(2,1)S(1)}, bf16[128,256]{1,0:T(8,128)(2,1)S(1)}) custom-call(s32[3]{0:T(128)S(1)} %pad_add_fusion.place_ref, bf16[128,512]{1,0:T(8,128)(2,1)} %bitcast.13, bf16[256,512]{1,0:T(8,128)(2,1)} %wq_ref.1, bf16[256,128]{1,0:T(8,128)(2,1)} %wk_ref.1, ...), custom_call_target="tpu_custom_call" | custom-call | flops 1100000000 | bytes 65536 | tf_op jit(solution)/shard_map/pack/pallas_call | solution.py:39
  3.1 2.6 %collective-permute-start.1 = (bf16[640,256]{1,0:T(8,128)(2,1)S(1)}, bf16[640,256]{1,0:T(8,128)(2,1)S(1)}, u32[]{:S(2)}, u32[]{:S(2)}) collective-permute-start(bf16[640,256]{1,0:T(8,128)(2,1)S(1)} %get-tuple-element.39.refs_4_), channel_id=1, source_target_pairs={{0,8},{4,12},{8,0},{12,4},{16,24},{20,28},{24,16},{28,20},{1,9},{5... | collective-permute-start | bytes 983048 | tf_op jit(solution)/shard_map/ppermute | solution.py:379
  5.6 1.5 %collective-permute-start.2 = (bf16[640,256]{1,0:T(8,128)(2,1)S(1)}, bf16[640,256]{1,0:T(8,128)(2,1)S(1)}, u32[]{:S(2)}, u32[]{:S(2)}) collective-permute-start(bf16[640,256]{1,0:T(8,128)(2,1)S(1)} %get-tuple-element.38.refs_5_), channel_id=1, source_target_pairs={{0,16},{4,20},{8,24},{12,28},{16,0},{20,4},{24,8},{28,12},{1,17},{... | collective-permute-start | bytes 983048 | tf_op jit(solution)/shard_map/ppermute | solution.py:379
  7.2 0.6 %collective-permute-start.6 = (bf16[640,256]{1,0:T(8,128)(2,1)S(1)}, bf16[640,256]{1,0:T(8,128)(2,1)S(1)}, u32[]{:S(2)}, u32[]{:S(2)}) collective-permute-start(bf16[640,256]{1,0:T(8,128)(2,1)S(1)} %get-tuple-element.38.refs_5_), channel_id=1, source_target_pairs={{0,8},{4,12},{8,0},{12,4},{16,24},{20,28},{24,16},{28,20},{1,9},{5... | collective-permute-start | bytes 983048 | tf_op jit(solution)/shard_map/ppermute | solution.py:379
  7.8 2.6 %collective-permute-start.3 = (bf16[256,256]{1,0:T(8,128)(2,1)S(1)}, bf16[256,256]{1,0:T(8,128)(2,1)S(1)}, u32[]{:S(2)}, u32[]{:S(2)}) collective-permute-start(bf16[256,256]{1,0:T(8,128)(2,1)S(1)} %constant_dynamic-update-slice_fusion.refs_0_), channel_id=1, source_target_pairs={{0,2},{1,3},{2,0},{3,1},{4,6},{5,7},{6,4},{7,5},{8,10},{9,11},{10,... | collective-permute-start | bytes 393224 | tf_op jit(solution)/shard_map/ppermute | solution.py:379
  12.3 1.9 %collective-permute-done.1.refs_6_ = bf16[640,256]{1,0:T(8,128)(2,1)S(1)} collective-permute-done((bf16[640,256]{1,0:T(8,128)(2,1)S(1)}, bf16[640,256]{1,0:T(8,128)(2,1)S(1)}, u32[]{:S(2)}, u32[]{:S(2)}) %collective-permute-start.1) | collective-permute-done | bytes 327712 | tf_op jit(solution)/shard_map/ppermute | solution.py:379
  14.2 2.0 %collective-permute-start.8 = (bf16[640,256]{1,0:T(8,128)(2,1)S(1)}, bf16[640,256]{1,0:T(8,128)(2,1)S(1)}, u32[]{:S(2)}, u32[]{:S(2)}) collective-permute-start(bf16[640,256]{1,0:T(8,128)(2,1)S(1)} %collective-permute-done.1.refs_6_), channel_id=1, source_target_pairs={{0,16},{4,20},{8,24},{12,28},{16,0},{20,4},{24,8},{28,12},{1,17},{... | collective-permute-start | bytes 983048 | tf_op jit(solution)/shard_map/ppermute | solution.py:379
  16.2 1.5 %collective-permute-start.9 = (bf16[640,256]{1,0:T(8,128)(2,1)S(1)}, bf16[640,256]{1,0:T(8,128)(2,1)S(1)}, u32[]{:S(2)}, u32[]{:S(2)}) collective-permute-start(bf16[640,256]{1,0:T(8,128)(2,1)S(1)} %collective-permute-done.2.refs_9_), channel_id=1, source_target_pairs={{0,8},{4,12},{8,0},{12,4},{16,24},{20,28},{24,16},{28,20},{1,9},{5... | collective-permute-start | bytes 983048 | tf_op jit(solution)/shard_map/ppermute | solution.py:379
  17.7 0.6 %add_convert_fusion.1 = f32[128]{0:T(128)S(1)} fusion(s32[]{:T(128)} %bitcast.4), kind=kLoop, calls=%fused_computation.8 | loop fusion | flops 256 | bytes 516 | tf_op jit(solution)/shard_map/convert_element_type | solution.py:371
  18.3 1.6 %collective-permute-start.4 = (bf16[256,256]{1,0:T(8,128)(2,1)S(1)}, bf16[256,256]{1,0:T(8,128)(2,1)S(1)}, u32[]{:S(2)}, u32[]{:S(2)}) collective-permute-start(bf16[256,256]{1,0:T(8,128)(2,1)S(1)} %constant_dynamic-update-slice_fusion.refs_0_), channel_id=1, source_target_pairs={{0,1},{1,0},{2,3},{3,2},{4,5},{5,4},{6,7},{7,6},{8,9},{9,8},{10,11... | collective-permute-start | bytes 393224 | tf_op jit(solution)/shard_map/ppermute | solution.py:379
  20.0 1.2 %collective-permute-done.6.refs_7_ = bf16[640,256]{1,0:T(8,128)(2,1)S(1)} collective-permute-done((bf16[640,256]{1,0:T(8,128)(2,1)S(1)}, bf16[640,256]{1,0:T(8,128)(2,1)S(1)}, u32[]{:S(2)}, u32[]{:S(2)}) %collective-permute-start.6) | collective-permute-done | bytes 327712 | tf_op jit(solution)/shard_map/ppermute | solution.py:379
  21.2 2.0 %collective-permute-start.5 = (bf16[256,256]{1,0:T(8,128)(2,1)S(1)}, bf16[256,256]{1,0:T(8,128)(2,1)S(1)}, u32[]{:S(2)}, u32[]{:S(2)}) collective-permute-start(bf16[256,256]{1,0:T(8,128)(2,1)S(1)} %collective-permute-done.3.refs_2_), channel_id=1, source_target_pairs={{0,1},{1,0},{2,3},{3,2},{4,5},{5,4},{6,7},{7,6},{8,9},{9,8},{10,11... | collective-permute-start | bytes 393224 | tf_op jit(solution)/shard_map/ppermute | solution.py:379
  23.6 2.6 %collective-permute-done.5.refs_3_ = bf16[256,256]{1,0:T(8,128)(2,1)S(1)} collective-permute-done((bf16[256,256]{1,0:T(8,128)(2,1)S(1)}, bf16[256,256]{1,0:T(8,128)(2,1)S(1)}, u32[]{:S(2)}, u32[]{:S(2)}) %collective-permute-start.5) | collective-permute-done | bytes 131104 | tf_op jit(solution)/shard_map/ppermute | solution.py:379
  26.2 1.2 %near_products.1 = (f32[256,768]{1,0:T(8,128)S(1)}, bf16[256,256]{1,0:T(8,128)(2,1)S(1)}, f32[256,128]{1,0:T(8,128)S(1)}, bf16[3,512,256]{2,1,0:T(8,128)(2,1)S(1)}) custom-call(s32[3]{0:T(128)S(1)} %pad_add_fusion.place_ref, bf16[8,1,256]{2,1,0:T(2,128)(2,1)S(1)} %reshape.24.gain_ref, bf16[256,256]{1,0:T(8,128)(2,1)S(1)} %constant_dynamic-update-slice_fusion.refs_0_, ...), custom_call_target="tpu_custom_call" | custom-call | flops 110000000 | bytes 65536 | tf_op jit(solution)/shard_map/near_products/pallas_call | solution.py:39
  27.4 2.0 %collective-permute-done.8.top_ref.refs_0_ = bf16[640,256]{1,0:T(8,128)(2,1)S(1)} collective-permute-done((bf16[640,256]{1,0:T(8,128)(2,1)S(1)}, bf16[640,256]{1,0:T(8,128)(2,1)S(1)}, u32[]{:S(2)}, u32[]{:S(2)}) %collective-permute-start.8) | collective-permute-done | bytes 327712 | tf_op jit(solution)/shard_map/ppermute | solution.py:379
  31.0 0.6 %collective-permute-done.10.there_ref = f32[128,896]{1,0:T(8,128)S(1)} collective-permute-done((f32[128,896]{1,0:T(8,128)S(1)}, f32[128,896]{1,0:T(8,128)S(1)}, u32[]{:S(2)}, u32[]{:S(2)}) %collective-permute-start.10) | collective-permute-done | bytes 458784 | tf_op jit(solution)/shard_map/ppermute | solution.py:379
  31.6 7.0 %attention.1 = (bf16[128,512]{1,0:T(8,128)(2,1)S(1)}, bf16[128,128]{1,0:T(8,128)(2,1)}, bf16[128,128]{1,0:T(8,128)(2,1)}) custom-call(s32[1]{0:T(128)} %dynamic_slice.3.length_ref, f32[128,128]{1,0:T(8,128)S(1)} %get-tuple-element.41.cos_ref, f32[128,128]{1,0:T(8,128)S(1)} %get-tuple-element.42.sin_ref, f32[128,896]{1,0:T(8,128)S(1)} %get-tuple-element.46.here_ref, ...), custom_call_target="tpu_custom_call" | custom-call | flops 4400000000 | bytes 65536 | tf_op jit(solution)/shard_map/attention/pallas_call | solution.py:39
  38.7 1.0 %project.2 = (bf16[128,512]{1,0:T(8,128)(2,1)S(1)}, bf16[128,512]{1,0:T(8,128)(2,1)S(1)}) custom-call(s32[3]{0:T(128)S(1)} %pad_add_fusion.place_ref, bf16[128,512]{1,0:T(8,128)(2,1)S(1)} %get-tuple-element.52.mixed_ref, bf16[3,512,256]{2,1,0:T(8,128)(2,1)S(1)} %get-tuple-element.49.own_ref, bf16[3,512,256]{2,1,0:T(8,128)(2,1)S(1)} %collective-permute-done.11.sibling_ref, ...), custom_call_target="tpu_custom_call" | custom-call | flops 1100000000 | bytes 65536 | tf_op jit(solution)/shard_map/project/pallas_call | solution.py:39
  39.7 3.7 %collective-permute-start.16 = (bf16[128,512]{1,0:T(8,128)(2,1)S(1)}, bf16[128,512]{1,0:T(8,128)(2,1)S(1)}, u32[]{:S(2)}, u32[]{:S(2)}) collective-permute-start(bf16[128,512]{1,0:T(8,128)(2,1)S(1)} %get-tuple-element.56), channel_id=1, source_target_pairs={{0,3},{1,2},{2,1},{3,0},{4,7},{5,6},{6,5},{7,4},{8,11},{9,10},{10,... | collective-permute-start | bytes 393224 | tf_op jit(solution)/shard_map/ppermute | solution.py:379
  43.4 1.0 %project.3 = (bf16[128,512]{1,0:T(8,128)(2,1)S(1)}, bf16[128,512]{1,0:T(8,128)(2,1)S(1)}) custom-call(s32[3]{0:T(128)S(1)} %pad_add_fusion.place_ref, bf16[128,512]{1,0:T(8,128)(2,1)S(1)} %get-tuple-element.52.mixed_ref, bf16[3,512,256]{2,1,0:T(8,128)(2,1)S(1)} %get-tuple-element.49.own_ref, bf16[3,512,256]{2,1,0:T(8,128)(2,1)S(1)} %collective-permute-done.11.sibling_ref, ...), custom_call_target="tpu_custom_call" | custom-call | flops 1100000000 | bytes 65536 | tf_op jit(solution)/shard_map/project/pallas_call | solution.py:39
  44.4 0.8 %collective-permute-start.14 = (bf16[128,512]{1,0:T(8,128)(2,1)S(1)}, bf16[128,512]{1,0:T(8,128)(2,1)S(1)}, u32[]{:S(2)}, u32[]{:S(2)}) collective-permute-start(bf16[128,512]{1,0:T(8,128)(2,1)S(1)} %get-tuple-element.54), channel_id=1, source_target_pairs={{0,1},{1,0},{2,3},{3,2},{4,5},{5,4},{6,7},{7,6},{8,9},{9,8},{10,11... | collective-permute-start | bytes 393224 | tf_op jit(solution)/shard_map/ppermute | solution.py:379
  45.3 2.6 %collective-permute-done.16 = bf16[128,512]{1,0:T(8,128)(2,1)S(1)} collective-permute-done((bf16[128,512]{1,0:T(8,128)(2,1)S(1)}, bf16[128,512]{1,0:T(8,128)(2,1)S(1)}, u32[]{:S(2)}, u32[]{:S(2)}) %collective-permute-start.16) | collective-permute-done | bytes 131104 | tf_op jit(solution)/shard_map/ppermute | solution.py:379
  47.8 6.0 %collective-permute-done.15 = bf16[128,512]{1,0:T(8,128)(2,1)S(1)} collective-permute-done((bf16[128,512]{1,0:T(8,128)(2,1)S(1)}, bf16[128,512]{1,0:T(8,128)(2,1)S(1)}, u32[]{:S(2)}, u32[]{:S(2)}) %collective-permute-start.15) | collective-permute-done | bytes 131104 | tf_op jit(solution)/shard_map/ppermute | solution.py:379
  53.8 0.7 %fusion = bf16[1,128,512]{2,1,0:T(8,128)(2,1)} fusion(bf16[128,512]{1,0:T(8,128)(2,1)S(1)} %collective-permute-done.16, bf16[128,512]{1,0:T(8,128)(2,1)S(1)} %collective-permute-done.15, bf16[128,512]{1,0:T(8,128)(2,1)S(1)} %collective-permute-done.14, bf16[128,512]{1,0:T(8,128)(2,1)S(1)} %get-tuple-element.53), kind=kLoop, calls=%fused_computation.1 | loop fusion | flops 524288 | bytes 655360 | tf_op jit(solution)/shard_map/broadcast_in_dim | solution.py:439
  (33 shorter events, 4.3 us)
Async XLA Ops:
  2.6 4.6 %collective-permute-start = (bf16[128,256]{1,0:T(8,128)(2,1)S(1)}, bf16[128,256]{1,0:T(8,128)(2,1)S(1)}, u32[]{:S(2)}, u32[]{:S(2)}) collective-permute-start(bf16[128,256]{1,0:T(8,128)(2,1)S(1)} %get-tuple-element.32), channel_id=1, source_target_pairs={{0,4},{4,0},{8,12},{12,8},{16,20},{20,16},{24,28},{28,24},{1,5},{5... | collective-permute-start | bytes 196616 | tf_op jit(solution)/shard_map/ppermute | solution.py:379
  3.1 11.1 %collective-permute-start.1 = (bf16[640,256]{1,0:T(8,128)(2,1)S(1)}, bf16[640,256]{1,0:T(8,128)(2,1)S(1)}, u32[]{:S(2)}, u32[]{:S(2)}) collective-permute-start(bf16[640,256]{1,0:T(8,128)(2,1)S(1)} %get-tuple-element.39.refs_4_), channel_id=1, source_target_pairs={{0,8},{4,12},{8,0},{12,4},{16,24},{20,28},{24,16},{28,20},{1,9},{5... | collective-permute-start | bytes 983048 | tf_op jit(solution)/shard_map/ppermute | solution.py:379
  5.6 10.6 %collective-permute-start.2 = (bf16[640,256]{1,0:T(8,128)(2,1)S(1)}, bf16[640,256]{1,0:T(8,128)(2,1)S(1)}, u32[]{:S(2)}, u32[]{:S(2)}) collective-permute-start(bf16[640,256]{1,0:T(8,128)(2,1)S(1)} %get-tuple-element.38.refs_5_), channel_id=1, source_target_pairs={{0,16},{4,20},{8,24},{12,28},{16,0},{20,4},{24,8},{28,12},{1,17},{... | collective-permute-start | bytes 983048 | tf_op jit(solution)/shard_map/ppermute | solution.py:379
  7.2 14.1 %collective-permute-start.6 = (bf16[640,256]{1,0:T(8,128)(2,1)S(1)}, bf16[640,256]{1,0:T(8,128)(2,1)S(1)}, u32[]{:S(2)}, u32[]{:S(2)}) collective-permute-start(bf16[640,256]{1,0:T(8,128)(2,1)S(1)} %get-tuple-element.38.refs_5_), channel_id=1, source_target_pairs={{0,8},{4,12},{8,0},{12,4},{16,24},{20,28},{24,16},{28,20},{1,9},{5... | collective-permute-start | bytes 983048 | tf_op jit(solution)/shard_map/ppermute | solution.py:379
  7.8 2.7 %copy-start = (bf16[2048]{0:T(1024)(128)(2,1)S(1)}, bf16[2048]{0:T(1024)(128)(2,1)}, u32[]{:S(2)}) copy-start(bf16[2048]{0:T(1024)(128)(2,1)} %param.10) | copy-start | bytes 12292
  7.8 10.6 %collective-permute-start.3 = (bf16[256,256]{1,0:T(8,128)(2,1)S(1)}, bf16[256,256]{1,0:T(8,128)(2,1)S(1)}, u32[]{:S(2)}, u32[]{:S(2)}) collective-permute-start(bf16[256,256]{1,0:T(8,128)(2,1)S(1)} %constant_dynamic-update-slice_fusion.refs_0_), channel_id=1, source_target_pairs={{0,2},{1,3},{2,0},{3,1},{4,6},{5,7},{6,4},{7,5},{8,10},{9,11},{10,... | collective-permute-start | bytes 393224 | tf_op jit(solution)/shard_map/ppermute | solution.py:379
  10.5 0.7 %copy-start.1 = (s32[8]{0:T(128)S(1)}, s32[8]{0:T(128)}, u32[]{:S(2)}) copy-start(s32[8]{0:T(128)} %param.17) | copy-start | bytes 100
  11.7 11.9 %collective-permute-start.7 = (bf16[640,256]{1,0:T(8,128)(2,1)S(1)}, bf16[640,256]{1,0:T(8,128)(2,1)S(1)}, u32[]{:S(2)}, u32[]{:S(2)}) collective-permute-start(bf16[640,256]{1,0:T(8,128)(2,1)S(1)} %get-tuple-element.39.refs_4_), channel_id=1, source_target_pairs={{0,16},{4,20},{8,24},{12,28},{16,0},{20,4},{24,8},{28,12},{1,17},{... | collective-permute-start | bytes 983048 | tf_op jit(solution)/shard_map/ppermute | solution.py:379
  14.2 15.3 %collective-permute-start.8 = (bf16[640,256]{1,0:T(8,128)(2,1)S(1)}, bf16[640,256]{1,0:T(8,128)(2,1)S(1)}, u32[]{:S(2)}, u32[]{:S(2)}) collective-permute-start(bf16[640,256]{1,0:T(8,128)(2,1)S(1)} %collective-permute-done.1.refs_6_), channel_id=1, source_target_pairs={{0,16},{4,20},{8,24},{12,28},{16,0},{20,4},{24,8},{28,12},{1,17},{... | collective-permute-start | bytes 983048 | tf_op jit(solution)/shard_map/ppermute | solution.py:379
  16.2 13.3 %collective-permute-start.9 = (bf16[640,256]{1,0:T(8,128)(2,1)S(1)}, bf16[640,256]{1,0:T(8,128)(2,1)S(1)}, u32[]{:S(2)}, u32[]{:S(2)}) collective-permute-start(bf16[640,256]{1,0:T(8,128)(2,1)S(1)} %collective-permute-done.2.refs_9_), channel_id=1, source_target_pairs={{0,8},{4,12},{8,0},{12,4},{16,24},{20,28},{24,16},{28,20},{1,9},{5... | collective-permute-start | bytes 983048 | tf_op jit(solution)/shard_map/ppermute | solution.py:379
  18.3 5.2 %collective-permute-start.4 = (bf16[256,256]{1,0:T(8,128)(2,1)S(1)}, bf16[256,256]{1,0:T(8,128)(2,1)S(1)}, u32[]{:S(2)}, u32[]{:S(2)}) collective-permute-start(bf16[256,256]{1,0:T(8,128)(2,1)S(1)} %constant_dynamic-update-slice_fusion.refs_0_), channel_id=1, source_target_pairs={{0,1},{1,0},{2,3},{3,2},{4,5},{5,4},{6,7},{7,6},{8,9},{9,8},{10,11... | collective-permute-start | bytes 393224 | tf_op jit(solution)/shard_map/ppermute | solution.py:379
  21.2 5.0 %collective-permute-start.5 = (bf16[256,256]{1,0:T(8,128)(2,1)S(1)}, bf16[256,256]{1,0:T(8,128)(2,1)S(1)}, u32[]{:S(2)}, u32[]{:S(2)}) collective-permute-start(bf16[256,256]{1,0:T(8,128)(2,1)S(1)} %collective-permute-done.3.refs_2_), channel_id=1, source_target_pairs={{0,1},{1,0},{2,3},{3,2},{4,5},{5,4},{6,7},{7,6},{8,9},{9,8},{10,11... | collective-permute-start | bytes 393224 | tf_op jit(solution)/shard_map/ppermute | solution.py:379
  29.7 1.9 %collective-permute-start.10 = (f32[128,896]{1,0:T(8,128)S(1)}, f32[128,896]{1,0:T(8,128)S(1)}, u32[]{:S(2)}, u32[]{:S(2)}) collective-permute-start(f32[128,896]{1,0:T(8,128)S(1)} %get-tuple-element.47), channel_id=1, source_target_pairs={{0,4},{4,0},{8,12},{12,8},{16,20},{20,16},{24,28},{28,24},{1,5},{5... | collective-permute-start | bytes 1376264 | tf_op jit(solution)/shard_map/ppermute | solution.py:379
  29.8 8.8 %collective-permute-start.11 = (bf16[3,512,256]{2,1,0:T(8,128)(2,1)S(1)}, bf16[3,512,256]{2,1,0:T(8,128)(2,1)S(1)}, u32[]{:S(2)}, u32[]{:S(2)}) collective-permute-start(bf16[3,512,256]{2,1,0:T(8,128)(2,1)S(1)} %get-tuple-element.49.own_ref), channel_id=1, source_target_pairs={{0,4},{4,0},{8,12},{12,8},{16,20},{20,16},{24,28},{28,24},{1,5},{5... | collective-permute-start | bytes 2359304 | tf_op jit(solution)/shard_map/ppermute | solution.py:379
  30.3 8.3 %collective-permute-start.12 = (bf16[256,256]{1,0:T(8,128)(2,1)S(1)}, bf16[256,256]{1,0:T(8,128)(2,1)S(1)}, u32[]{:S(2)}, u32[]{:S(2)}) collective-permute-start(bf16[256,256]{1,0:T(8,128)(2,1)S(1)} %slice.8), channel_id=1, source_target_pairs={{0,4},{4,0},{8,12},{12,8},{16,20},{20,16},{24,28},{28,24},{1,5},{5... | collective-permute-start | bytes 393224 | tf_op jit(solution)/shard_map/ppermute | solution.py:379
  30.5 8.2 %collective-permute-start.13 = (bf16[256,256]{1,0:T(8,128)(2,1)S(1)}, bf16[256,256]{1,0:T(8,128)(2,1)S(1)}, u32[]{:S(2)}, u32[]{:S(2)}) collective-permute-start(bf16[256,256]{1,0:T(8,128)(2,1)S(1)} %slice.9), channel_id=1, source_target_pairs={{0,4},{4,0},{8,12},{12,8},{16,20},{20,16},{24,28},{28,24},{1,5},{5... | collective-permute-start | bytes 393224 | tf_op jit(solution)/shard_map/ppermute | solution.py:379
  39.7 8.1 %collective-permute-start.16 = (bf16[128,512]{1,0:T(8,128)(2,1)S(1)}, bf16[128,512]{1,0:T(8,128)(2,1)S(1)}, u32[]{:S(2)}, u32[]{:S(2)}) collective-permute-start(bf16[128,512]{1,0:T(8,128)(2,1)S(1)} %get-tuple-element.56), channel_id=1, source_target_pairs={{0,3},{1,2},{2,1},{3,0},{4,7},{5,6},{6,5},{7,4},{8,11},{9,10},{10,... | collective-permute-start | bytes 393224 | tf_op jit(solution)/shard_map/ppermute | solution.py:379
  43.4 10.4 %collective-permute-start.15 = (bf16[128,512]{1,0:T(8,128)(2,1)S(1)}, bf16[128,512]{1,0:T(8,128)(2,1)S(1)}, u32[]{:S(2)}, u32[]{:S(2)}) collective-permute-start(bf16[128,512]{1,0:T(8,128)(2,1)S(1)} %get-tuple-element.55), channel_id=1, source_target_pairs={{0,2},{1,3},{2,0},{3,1},{4,6},{5,7},{6,4},{7,5},{8,10},{9,11},{10,... | collective-permute-start | bytes 393224 | tf_op jit(solution)/shard_map/ppermute | solution.py:379
  44.4 9.4 %collective-permute-start.14 = (bf16[128,512]{1,0:T(8,128)(2,1)S(1)}, bf16[128,512]{1,0:T(8,128)(2,1)S(1)}, u32[]{:S(2)}, u32[]{:S(2)}) collective-permute-start(bf16[128,512]{1,0:T(8,128)(2,1)S(1)} %get-tuple-element.54), channel_id=1, source_target_pairs={{0,1},{1,0},{2,3},{3,2},{4,5},{5,4},{6,7},{7,6},{8,9},{9,8},{10,11... | collective-permute-start | bytes 393224 | tf_op jit(solution)/shard_map/ppermute | solution.py:379

commit v3 on v2

--- a/solution.py
+++ b/solution.py
@@ -12,21 +12,23 @@
 rope_base = 1000000.0
 norm_eps = 1e-05
 masked_score = -1e30
-KV_BLOCK = 512
+CACHE_STEPS = 4
+QUERY_ROWS = 256
+SIXTEENTHS = 8
 FLOPS_PER_US = 1.1e9
-VMEM_BYTES = 16 * 1024 * 1024
+VMEM_BYTES = 24 * 1024 * 1024
 
 VM = pl.BlockSpec(memory_space=pltpu.VMEM)
 HB = pl.BlockSpec(memory_space=pltpu.HBM)
 SM = pl.BlockSpec(memory_space=pltpu.SMEM)
 
 
-def call(kernel, out_shape, in_specs, scratch=(), busy=1.0, name=None):
+def call(kernel, out_shape, in_specs, scratch=(), busy=1.0, name=None, out_specs=None):
     run = pl.pallas_call(
         kernel,
         out_shape=out_shape,
         in_specs=in_specs,
-        out_specs=jax.tree.map(lambda _: VM, out_shape),
+        out_specs=out_specs or jax.tree.map(lambda _: VM, out_shape),
         scratch_shapes=list(scratch),
         compiler_params=pltpu.CompilerParams(vmem_limit_bytes=VMEM_BYTES),
         cost_estimate=pl.CostEstimate(
@@ -57,8 +59,11 @@
     return copies
 
 
+def upper(rows):
+    return rows * SIXTEENTHS // 16
+
+
 def pack_kernel(
-    place_ref,
     hidden_ref,
     wq_ref,
     wk_ref,
@@ -70,22 +75,23 @@
     send_out,
     sems,
 ):
-    odd = place_ref[1]
+    odd = lax.axis_index("req") % 2
     rows, width = wq_ref.shape
-    half, column = rows // 2, top_out.shape[1]
-    kv = wk_ref.shape[1]
+    column, kv = top_out.shape[1], wk_ref.shape[1]
     pairs = []
     for part, out in enumerate((top_out, bottom_out)):
-        source = pl.ds(part * half, half)
+        start, size = part * upper(rows), (upper(rows), rows - upper(rows))[part]
+        source = pl.ds(start, size)
         first = 0
         for c in range(width // column):
-            pairs.append((wq_ref.at[source, pl.ds(c * column, column)], out.at[pl.ds(first, half)]))
-            first += half
+            pairs.append((wq_ref.at[source, pl.ds(c * column, column)], out.at[pl.ds(first, size)]))
+            first += size
         for i, w in enumerate((wk_ref, wv_ref)):
-            pairs.append((w.at[source], out.at[pl.ds(first, half), pl.ds(i * kv, kv)]))
-        first += half
-        depth = wo_ref.shape[0] // 2
-        pairs.append((wo_ref.at[pl.ds(part * depth, depth)], out.at[pl.ds(first, depth)]))
+            pairs.append((w.at[source], out.at[pl.ds(first, size), pl.ds(i * kv, kv)]))
+        first += size
+        depth = wo_ref.shape[0]
+        start, size = part * upper(depth), (upper(depth), depth - upper(depth))[part]
+        pairs.append((wo_ref.at[pl.ds(start, size)], out.at[pl.ds(first, size)]))
     half = keep_out.shape[1]
     mine = pl.ds(pl.multiple_of(odd * half, half), half)
     other = pl.ds(pl.multiple_of((1 - odd) * half, half), half)
@@ -94,25 +100,28 @@
         copy.wait()
 
 
-def pack(place, hidden, w_query, w_key, w_value, w_out):
+def pack(hidden, w_query, w_key, w_value, w_out):
     column = 2 * w_key.shape[1]
-    rows = w_query.shape[0] // 2 * (w_query.shape[1] // column + 1) + w_out.shape[0] // 2
+    blocks = w_query.shape[1] // column + 1
+    rows = w_query.shape[0] * blocks + w_out.shape[0]
+    top = upper(w_query.shape[0]) * blocks + upper(w_out.shape[0])
     columns = like((hidden.shape[0], hidden.shape[1] // 2))
     return call(
         pack_kernel,
-        (like((rows, column)), like((rows, column)), columns, columns),
-        [SM] + [HB] * 5,
+        (like((top, column)), like((rows - top, column)), columns, columns),
+        [HB] * 5,
         scratch=[pltpu.SemaphoreType.DMA((12,))],
         name="pack",
-    )(place, hidden, w_query, w_key, w_value, w_out)
+    )(hidden, w_query, w_key, w_value, w_out)
 
 
 def product(rows, top_ref, bottom_ref):
-    half = rows.shape[1] // 2
+    depth = rows.shape[1]
+    high, low = upper(depth), depth - upper(depth)
     parts = []
-    for first in range(0, 3 * half, half):
+    for c in range(3):
         block = jnp.concatenate(
-            [top_ref[first : first + half], bottom_ref[first : first + half]], axis=0
+            [top_ref[c * high : (c + 1) * high], bottom_ref[c * low : (c + 1) * low]], axis=0
         )
         parts.append(jnp.dot(rows, block, preferred_element_type=jnp.float32))
     return jnp.concatenate(parts, axis=1)
@@ -133,24 +142,23 @@
         product(buf[mine ^ j], weights[2 * j], weights[2 * j + 1]) for j in range(shards - 1)
     )
     last_out[...] = buf[mine ^ (shards - 1)]
-    depth = project_out.shape[1] // 2
-    first = weights[0].shape[0] - depth
+    depth = project_out.shape[1]
+    high = upper(depth)
     for j in range(shards - 1):
-        project_out[j, :depth] = weights[2 * j][first:]
-        project_out[j, depth:] = weights[2 * j + 1][first:]
-
-
-def near_products(place, gain, columns, weights, q_rows):
+        project_out[j, :high] = weights[2 * j][weights[2 * j].shape[0] - high :]
+        project_out[j, high:] = weights[2 * j + 1][weights[2 * j + 1].shape[0] - depth + high :]
+
+
+def near_products(place, gain, columns, weights, depth):
     shards = len(columns)
     rows, width = columns[0].shape
-    depth = weights[0].shape[0] - q_rows
     return call(
         functools.partial(near_kernel, shards),
         (
             like((rows, 3 * width), jnp.float32),
             like((rows, width)),
             like((rows, 128), jnp.float32),
-            like((shards - 1, 2 * depth, weights[0].shape[1])),
+            like((shards - 1, depth, weights[0].shape[1])),
         ),
         [SM, VM] + [VM] * (3 * shards - 2),
         scratch=[pltpu.VMEM((shards, rows, width), jnp.bfloat16)],
@@ -209,37 +217,51 @@
             head += 1
 
 
-def attend(q_ref, acc_ref, peak_ref, keys, values, mask):
-    half = q_ref.shape[0] // 2
+def one_over(x):
+    near = pl.reciprocal(x, approx=True)
+    return near * (2.0 - x * near)
+
+
+def attend(q_ref, keys, values, mask):
+    tokens = mask.shape[0]
     low = lax.broadcasted_iota(jnp.int32, values.shape, 1) < HD
     one = jnp.ones_like(values)
-    for g in range(2):
-        part = pl.ds(g * half, half)
-        scores = lax.dot_general(
-            q_ref[part, :], keys, (((1,), (1,)), ((), ())), preferred_element_type=jnp.float32
+    mine = [jnp.where(low, values, one), jnp.where(low, one, values)]
+    queries = q_ref.shape[0]
+    mask = jnp.tile(mask, (QUERY_ROWS // tokens, 1))
+
+    def score(start):
+        return lax.dot_general(
+            q_ref[start : start + QUERY_ROWS, :],
+            keys,
+            (((1,), (1,)), ((), ())),
+            preferred_element_type=jnp.float32,
         )
-        if mask is not None:
-            scores = jnp.where(mask(scores.shape), scores, masked_score)
-        old = peak_ref[part, :]
-        new = jnp.maximum(old, jnp.max(scores, axis=-1, keepdims=True))
-        weights = jnp.exp2(scores - jnp.tile(new, (1, scores.shape[1] // 128))).astype(jnp.bfloat16)
-        mine = jnp.where(low if g == 0 else jnp.logical_not(low), values, one)
-        acc_ref[part, :] = acc_ref[part, :] * jnp.exp2(old - new) + jnp.dot(
-            weights, mine, preferred_element_type=jnp.float32
+
+    heads = []
+    upcoming = score(0)
+    for start in range(0, queries, QUERY_ROWS):
+        scores = upcoming
+        if start + QUERY_ROWS < queries:
+            upcoming = score(start + QUERY_ROWS)
+        scores = jnp.where(mask, scores, masked_score)
+        peak = jnp.max(scores, axis=-1, keepdims=True)
+        weights = jnp.exp2(scores - peak).astype(jnp.bfloat16)
+        total = jnp.dot(
+            weights, mine[start * 2 // queries], preferred_element_type=jnp.float32
         )
-        peak_ref[part, :] = new
-
-
-def finish(acc_ref, out_ref, tokens):
-    heads = acc_ref.shape[0] // tokens
-    low = lax.broadcasted_iota(jnp.int32, (tokens, 128), 1) < HD
+        mixed = total * one_over(pltpu.roll(total, HD, 1))
+        heads += [mixed[i : i + tokens] for i in range(0, QUERY_ROWS, tokens)]
+    return heads
+
+
+def lay_out(heads, out_ref):
+    low = lax.broadcasted_iota(jnp.int32, heads[0].shape, 1) < HD
     slabs = []
-    for h in range(heads):
-        acc = acc_ref[h * tokens : (h + 1) * tokens, :]
-        mixed = acc / pltpu.roll(acc, HD, 1)
-        straight = (h % 2 == 0) == (h < heads // 2)
+    for h, mixed in enumerate(heads):
+        straight = (h % 2 == 0) == (h < len(heads) // 2)
         slabs.append(mixed if straight else pltpu.roll(mixed, HD, 1))
-    for s in range(heads // 2):
+    for s in range(len(heads) // 2):
         both = jnp.where(low, slabs[2 * s], slabs[2 * s + 1])
         out_ref[:, s * 128 : (s + 1) * 128] = both.astype(jnp.bfloat16)
 
@@ -254,10 +276,15 @@
     there_ref,
     k_ref,
     v_ref,
-    *refs,
+    out_ref,
+    nk_out,
+    nv_out,
+    nk_ref,
+    nv_ref,
+    q_ref,
+    out_sems,
 ):
-    out_ref, nk_ref, nv_ref, q_ref, acc_ref, peak_ref, k_buf, v_buf, sems = refs
-    cache = fetch([(k_ref, k_buf), (v_ref, v_buf)], sems)
+    length = length_ref[0]
     total = here_ref[...] + there_ref[...]
     width = total.shape[1] - 128
     scale = lax.rsqrt(total[:, width:] / features + norm_eps)
@@ -265,43 +292,31 @@
     tokens = total.shape[0]
     q_width = width - 2 * kv_width
     cosine, sine = cos_ref[...], sin_ref[...]
-    place_queries(rotate(total[:, :q_width], cosine, sine), q_ref)
     (keys,) = rotate(total[:, q_width : q_width + kv_width], cosine, sine)
     nk_ref[...] = keys.astype(jnp.bfloat16)
     nv_ref[...] = total[:, q_width + kv_width :].astype(jnp.bfloat16)
-
-    length = length_ref[0]
-    acc_ref[...] = jnp.zeros_like(acc_ref)
-    peak_ref[...] = jnp.full_like(peak_ref, masked_score)
-    run = functools.partial(attend, q_ref, acc_ref, peak_ref)
-    run(
-        nk_ref[...],
-        nv_ref[...],
-        lambda shape: lax.broadcasted_iota(jnp.int32, shape, 1)
-        <= lax.broadcasted_iota(jnp.int32, shape, 0) % tokens,
-    )
-    for copy in cache:
+    fresh = fetch([(nk_ref, nk_out), (nv_ref, nv_out)], out_sems)
+    place_queries(rotate(total[:, :q_width], cosine, sine), q_ref)
+
+    step = k_ref.shape[0] // CACHE_STEPS
+    for cached in range(step, k_ref.shape[0] + 1, step):
+
+        @pl.when((length > cached - step) & (length <= cached))
+        def _(cached=cached):
+            shape = (tokens, cached + tokens)
+            column = lax.broadcasted_iota(jnp.int32, shape, 1)
+            token = lax.broadcasted_iota(jnp.int32, shape, 0)
+            limit = jnp.where(column < cached, length, cached + 1 + token)
+            heads = attend(
+                q_ref,
+                jnp.concatenate([k_ref[:cached, :], nk_ref[...]], axis=0),
+                jnp.concatenate([v_ref[:cached, :], nv_ref[...]], axis=0),
+                column < limit,
+            )
+            lay_out(heads, out_ref)
+
+    for copy in fresh:
         copy.wait()
-
-    def step(i, _):
-        rows = pl.ds(pl.multiple_of(i * KV_BLOCK, KV_BLOCK), KV_BLOCK)
-        run(k_buf[rows, :], v_buf[rows, :], None)
-        return 0
-
-    full = length // KV_BLOCK
-    lax.fori_loop(0, full, step, 0)
-    left = length - full * KV_BLOCK
-
-    @pl.when(left > 0)
-    def _():
-        rows = pl.ds(pl.multiple_of(full * KV_BLOCK, KV_BLOCK), KV_BLOCK)
-        run(
-            k_buf[rows, :],
-            v_buf[rows, :],
-            lambda shape: lax.broadcasted_iota(jnp.int32, shape, 1) < left,
-        )
-
-    finish(acc_ref, out_ref, tokens)
 
 
 def attention(length, features, cosine, sine, here, there, keys, values):
@@ -313,13 +328,12 @@
     return call(
         functools.partial(attention_kernel, features, kv_width),
         (like((tokens, q_width)), fresh, fresh),
-        [SM, VM, VM, VM, VM, HB, HB],
+        [SM, VM, VM, VM, VM, VM, VM],
+        out_specs=(VM, HB, HB),
         scratch=[
+            pltpu.VMEM(fresh.shape, jnp.bfloat16),
+            pltpu.VMEM(fresh.shape, jnp.bfloat16),
             pltpu.VMEM((queries, 128), jnp.bfloat16),
-            pltpu.VMEM((queries, 128), jnp.float32),
-            pltpu.VMEM((queries, 128), jnp.float32),
-            pltpu.VMEM(keys.shape, jnp.bfloat16),
-            pltpu.VMEM(keys.shape, jnp.bfloat16),
             pltpu.SemaphoreType.DMA((2,)),
         ],
         busy=4.0,
@@ -350,8 +364,7 @@
 
         @pl.when(j == chips - 1)
         def _(out=out):
-            depth = last[2].shape[0]
-            halves = [h[h.shape[0] - depth :] for h in last]
+            halves = [h[h.shape[0] - last[2 + i % 2].shape[0] :] for i, h in enumerate(last)]
             store(out, [jnp.concatenate(halves[:2], axis=0), jnp.concatenate(halves[2:], axis=0)])
 
 
@@ -396,23 +409,24 @@
     length = lax.dynamic_slice_in_dim(cache_lengths, lax.axis_index("req"), 1, 0)
     tokens = hidden.shape[1]
 
-    top, bottom, keep, send = pack(place, hidden[0], w_query, w_key, w_value, w_out)
+    top, bottom, keep, send = pack(hidden[0], w_query, w_key, w_value, w_out)
     x_top, y_bottom = swap(top, "req", SIDE_X), swap(bottom, "req", SIDE_Y)
     got, top_later, bottom_later = lax.optimization_barrier((core(send), top, bottom))
     x_bottom, y_top = swap(bottom_later, "req", SIDE_X), swap(top_later, "req", SIDE_Y)
     columns = jnp.concatenate([keep, got], axis=0)
     two = swap(columns, "tp", 2)
-    q_rows = w_query.shape[0] // 2 * 3
     d_top, d_bottom = swap(x_top, "req", SIDE_Y), swap(y_bottom, "req", SIDE_X)
     _, _, columns_later, two_later = lax.optimization_barrier((x_top, y_bottom, columns, two))
-    one, three = swap(columns_later, "tp", 1), swap(two_later, "tp", 1)
+    one = swap(columns_later, "tp", 1)
+    _, two_later = lax.optimization_barrier((x_bottom, two_later))
+    three = swap(two_later, "tp", 1)
 
     partial, last, square, o_near = near_products(
         place,
         norm_gain,
         [columns, one, two, three],
         [top, bottom, x_top, x_bottom, y_top, y_bottom],
-        q_rows,
+        w_out.shape[0],
     )
     cosine, sine = phases(length[0], tokens)
     partial, cosine, sine = lax.optimization_barrier((partial, cosine, sine))
@@ -428,7 +442,9 @@
         cache_values[0],
     )
     o_sibling = core(o_near)
-    o_last = [d_top, d_bottom, core(d_top[q_rows:]), core(d_bottom[q_rows:])]
+    high = upper(w_out.shape[0])
+    first, second = d_top.shape[0] - high, d_bottom.shape[0] - w_out.shape[0] + high
+    o_last = [d_top, d_bottom, core(d_top[first:]), core(d_bottom[second:])]
     terms = {}
     terms[2], terms[3] = project((2, 3), mixed, place, o_near, o_sibling, o_last)
     mixed, terms[2], terms[3] = lax.optimization_barrier((mixed, terms[2], terms[3]))

time: 54.1 us -> 50.9 us (0.941)
  Pallas kernels: 12.4 us -> 9.27 us
  starting transfers between devices: 21.3 us -> 19.5 us
  local copies, waits for them, and re-layouts: 1.28 us -> 2.12 us
    pallas_call x6, Pallas kernels: 12.4 us -> 9.27 us  [placed(): run(*[pltpu.with_memory_space_constraint(x, pltpu.HBM) if spec is HB else...]
    ppermute x17, starting transfers between devices: 21.3 us -> 19.5 us  [swap(): return lax.ppermute(x, axis, [(i, i ^ mask) for i in range(count)])]
    unnamed x5 -> x9, local copies, waits for them, and re-layouts: 0.58 us -> 1.35 us
  transfers between devices with their start and end apart: 17 -> 17, of which waited for: 7 -> 7; matrix products, arithmetic and copies ran while one was open for 3% -> 4% of each run, Pallas kernels for 17% -> 13%
where the time goes in v3:
time: 50.9 us; the launch traced here: 51 us
  starting transfers between devices  19.5 us (38%)
  waiting for transfers between devices  17.5 us (34%)
  Pallas kernels  9.27 us (18%)
  local copies, waits for them, and re-layouts  2.12 us (4%)
  other arithmetic  1.79 us (4%)
  between operations  0.78 us (2%)
    ppermute x17, starting transfers between devices, swap(): return lax.ppermute(x, axis, [(i, i ^ mask) for i in range(count)])  19.5 us
    ppermute x17, waiting for transfers between devices, swap(): return lax.ppermute(x, axis, [(i, i ^ mask) for i in range(count)])  17.5 us
    pallas_call x6, Pallas kernels, placed(): run(*[pltpu.with_memory_space_constraint(x, pltpu.HBM) if spec is HB else...  9.27 us
    unnamed x9, local copies, waits for them, and re-layouts  1.35 us
  transfers between devices with their start and end apart: 17, of which 7 were waited for; matrix products, arithmetic and copies ran while one was open for 4% of the time, Pallas kernels for 13%

profile of v3, /device:TPU:0, one launch (start us, length us, event | category | flops | bytes accessed | tf_op | source)
XLA Modules:
  0.0 51.0 jit_solution(7963985670773442710)
XLA Ops:
  0.6 1.3 %pack.1 = (bf16[640,256]{1,0:T(8,128)(2,1)S(1)}, bf16[640,256]{1,0:T(8,128)(2,1)S(1)}, bf16[128,256]{1,0:T(8,128)(2,1)S(1)}, bf16[128,256]{1,0:T(8,128)(2,1)S(1)}) custom-call(bf16[128,512]{1,0:T(8,128)(2,1)} %bitcast.13, bf16[256,512]{1,0:T(8,128)(2,1)} %wq_ref.1, bf16[256,128]{1,0:T(8,128)(2,1)} %wk_ref.1, bf16[256,128]{1,0:T(8,128)(2,1)} %wv_ref.1, ...), custom_call_target="tpu_custom_call" | custom-call | flops 1100000000 | bytes 65536 | tf_op jit(solution)/shard_map/pack/pallas_call | solution.py:41
  2.4 2.6 %collective-permute-start.1 = (bf16[640,256]{1,0:T(8,128)(2,1)S(1)}, bf16[640,256]{1,0:T(8,128)(2,1)S(1)}, u32[]{:S(2)}, u32[]{:S(2)}) collective-permute-start(bf16[640,256]{1,0:T(8,128)(2,1)S(1)} %get-tuple-element.41.refs_4_), channel_id=1, source_target_pairs={{0,8},{4,12},{8,0},{12,4},{16,24},{20,28},{24,16},{28,20},{1,9},{5... | collective-permute-start | bytes 983048 | tf_op jit(solution)/shard_map/ppermute | solution.py:392
  5.0 1.5 %collective-permute-start.2 = (bf16[640,256]{1,0:T(8,128)(2,1)S(1)}, bf16[640,256]{1,0:T(8,128)(2,1)S(1)}, u32[]{:S(2)}, u32[]{:S(2)}) collective-permute-start(bf16[640,256]{1,0:T(8,128)(2,1)S(1)} %get-tuple-element.38.refs_5_), channel_id=1, source_target_pairs={{0,16},{4,20},{8,24},{12,28},{16,0},{20,4},{24,8},{28,12},{1,17},{... | collective-permute-start | bytes 983048 | tf_op jit(solution)/shard_map/ppermute | solution.py:392
  7.1 2.6 %collective-permute-start.3 = (bf16[256,256]{1,0:T(8,128)(2,1)S(1)}, bf16[256,256]{1,0:T(8,128)(2,1)S(1)}, u32[]{:S(2)}, u32[]{:S(2)}) collective-permute-start(bf16[256,256]{1,0:T(8,128)(2,1)S(1)} %constant_dynamic-update-slice_fusion.refs_0_), channel_id=1, source_target_pairs={{0,2},{1,3},{2,0},{3,1},{4,6},{5,7},{6,4},{7,5},{8,10},{9,11},{10,... | collective-permute-start | bytes 393224 | tf_op jit(solution)/shard_map/ppermute | solution.py:392
  9.8 0.7 %copy-done.3 = s32[8]{0:T(128)S(1)} copy-done((s32[8]{0:T(128)S(1)}, s32[8]{0:T(128)}, u32[]{:S(2)}) %copy-start.3) | copy-done | bytes 56
  10.5 0.6 %dynamic_slice.3.length_ref = s32[1]{0:T(128)} dynamic-slice(s32[8]{0:T(128)S(1)} %copy-done.3, s32[]{:T(128)S(6)} %select_n.16), dynamic_slice_sizes={1} | dynamic-slice | bytes 12 | tf_op jit(solution)/shard_map/dynamic_slice | solution.py:409
  11.1 0.7 %add_convert_fusion.1 = f32[128]{0:T(128)S(1)} fusion(s32[]{:T(128)} %bitcast.4), kind=kLoop, calls=%fused_computation.8 | loop fusion | flops 256 | bytes 516 | tf_op jit(solution)/shard_map/convert_element_type | solution.py:384
  12.5 3.4 %collective-permute-done.3.refs_2_ = bf16[256,256]{1,0:T(8,128)(2,1)S(1)} collective-permute-done((bf16[256,256]{1,0:T(8,128)(2,1)S(1)}, bf16[256,256]{1,0:T(8,128)(2,1)S(1)}, u32[]{:S(2)}, u32[]{:S(2)}) %collective-permute-start.3) | collective-permute-done | bytes 131104 | tf_op jit(solution)/shard_map/ppermute | solution.py:392
  15.9 1.3 %collective-permute-start.4 = (bf16[256,256]{1,0:T(8,128)(2,1)S(1)}, bf16[256,256]{1,0:T(8,128)(2,1)S(1)}, u32[]{:S(2)}, u32[]{:S(2)}) collective-permute-start(bf16[256,256]{1,0:T(8,128)(2,1)S(1)} %constant_dynamic-update-slice_fusion.refs_0_), channel_id=1, source_target_pairs={{0,1},{1,0},{2,3},{3,2},{4,5},{5,4},{6,7},{7,6},{8,9},{9,8},{10,11... | collective-permute-start | bytes 393224 | tf_op jit(solution)/shard_map/ppermute | solution.py:392
  17.1 1.5 %collective-permute-start.8 = (bf16[640,256]{1,0:T(8,128)(2,1)S(1)}, bf16[640,256]{1,0:T(8,128)(2,1)S(1)}, u32[]{:S(2)}, u32[]{:S(2)}) collective-permute-start(bf16[640,256]{1,0:T(8,128)(2,1)S(1)} %collective-permute-done.1.refs_6_), channel_id=1, source_target_pairs={{0,16},{4,20},{8,24},{12,28},{16,0},{20,4},{24,8},{28,12},{1,17},{... | collective-permute-start | bytes 983048 | tf_op jit(solution)/shard_map/ppermute | solution.py:392
  19.2 1.4 %collective-permute-done.5.refs_7_ = bf16[640,256]{1,0:T(8,128)(2,1)S(1)} collective-permute-done((bf16[640,256]{1,0:T(8,128)(2,1)S(1)}, bf16[640,256]{1,0:T(8,128)(2,1)S(1)}, u32[]{:S(2)}, u32[]{:S(2)}) %collective-permute-start.5) | collective-permute-done | bytes 327712 | tf_op jit(solution)/shard_map/ppermute | solution.py:392
  20.6 2.0 %collective-permute-start.6 = (bf16[256,256]{1,0:T(8,128)(2,1)S(1)}, bf16[256,256]{1,0:T(8,128)(2,1)S(1)}, u32[]{:S(2)}, u32[]{:S(2)}) collective-permute-start(bf16[256,256]{1,0:T(8,128)(2,1)S(1)} %collective-permute-done.3.refs_2_), channel_id=1, source_target_pairs={{0,1},{1,0},{2,3},{3,2},{4,5},{5,4},{6,7},{7,6},{8,9},{9,8},{10,11... | collective-permute-start | bytes 393224 | tf_op jit(solution)/shard_map/ppermute | solution.py:392
  23.0 0.7 %copy-done.2 = bf16[2048]{0:T(1024)(128)(2,1)S(1)} copy-done((bf16[2048]{0:T(1024)(128)(2,1)S(1)}, bf16[2048]{0:T(1024)(128)(2,1)}, u32[]{:S(2)}) %copy-start.2) | copy-done | bytes 4120
  23.7 1.9 %collective-permute-done.6.refs_3_ = bf16[256,256]{1,0:T(8,128)(2,1)S(1)} collective-permute-done((bf16[256,256]{1,0:T(8,128)(2,1)S(1)}, bf16[256,256]{1,0:T(8,128)(2,1)S(1)}, u32[]{:S(2)}, u32[]{:S(2)}) %collective-permute-start.6) | collective-permute-done | bytes 131104 | tf_op jit(solution)/shard_map/ppermute | solution.py:392
  25.6 1.2 %near_products.1 = (f32[256,768]{1,0:T(8,128)S(1)}, bf16[256,256]{1,0:T(8,128)(2,1)S(1)}, f32[256,128]{1,0:T(8,128)S(1)}, bf16[3,512,256]{2,1,0:T(8,128)(2,1)S(1)}) custom-call(s32[3]{0:T(128)S(1)} %pad_add_fusion.place_ref, bf16[8,1,256]{2,1,0:T(2,128)(2,1)S(1)} %reshape.24.gain_ref, bf16[256,256]{1,0:T(8,128)(2,1)S(1)} %constant_dynamic-update-slice_fusion.refs_0_, ...), custom_call_target="tpu_custom_call" | custom-call | flops 110000000 | bytes 65536 | tf_op jit(solution)/shard_map/near_products/pallas_call | solution.py:41
  26.8 2.1 %collective-permute-done.8.top_ref.refs_0_ = bf16[640,256]{1,0:T(8,128)(2,1)S(1)} collective-permute-done((bf16[640,256]{1,0:T(8,128)(2,1)S(1)}, bf16[640,256]{1,0:T(8,128)(2,1)S(1)}, u32[]{:S(2)}, u32[]{:S(2)}) %collective-permute-start.8) | collective-permute-done | bytes 327712 | tf_op jit(solution)/shard_map/ppermute | solution.py:392
  31.0 4.5 %attention.1 = (bf16[128,512]{1,0:T(8,128)(2,1)S(1)}, bf16[128,128]{1,0:T(8,128)(2,1)}, bf16[128,128]{1,0:T(8,128)(2,1)}) custom-call(s32[1]{0:T(128)} %dynamic_slice.3.length_ref, f32[128,128]{1,0:T(8,128)S(1)} %get-tuple-element.43.cos_ref, f32[128,128]{1,0:T(8,128)S(1)} %get-tuple-element.44.sin_ref, f32[128,896]{1,0:T(8,128)S(1)} %get-tuple-element.48.here_ref, ...), custom_call_target="tpu_custom_call" | custom-call | flops 4400000000 | bytes 65536 | tf_op jit(solution)/shard_map/attention/pallas_call | solution.py:41
  35.5 1.0 %project.2 = (bf16[128,512]{1,0:T(8,128)(2,1)S(1)}, bf16[128,512]{1,0:T(8,128)(2,1)S(1)}) custom-call(s32[3]{0:T(128)S(1)} %pad_add_fusion.place_ref, bf16[128,512]{1,0:T(8,128)(2,1)S(1)} %get-tuple-element.54.mixed_ref, bf16[3,512,256]{2,1,0:T(8,128)(2,1)S(1)} %get-tuple-element.51.own_ref, bf16[3,512,256]{2,1,0:T(8,128)(2,1)S(1)} %collective-permute-done.11.sibling_ref, ...), custom_call_target="tpu_custom_call" | custom-call | flops 1100000000 | bytes 65536 | tf_op jit(solution)/shard_map/project/pallas_call | solution.py:41
  36.6 3.7 %collective-permute-start.16 = (bf16[128,512]{1,0:T(8,128)(2,1)S(1)}, bf16[128,512]{1,0:T(8,128)(2,1)S(1)}, u32[]{:S(2)}, u32[]{:S(2)}) collective-permute-start(bf16[128,512]{1,0:T(8,128)(2,1)S(1)} %get-tuple-element.58), channel_id=1, source_target_pairs={{0,3},{1,2},{2,1},{3,0},{4,7},{5,6},{6,5},{7,4},{8,11},{9,10},{10,... | collective-permute-start | bytes 393224 | tf_op jit(solution)/shard_map/ppermute | solution.py:392
  40.2 1.0 %project.3 = (bf16[128,512]{1,0:T(8,128)(2,1)S(1)}, bf16[128,512]{1,0:T(8,128)(2,1)S(1)}) custom-call(s32[3]{0:T(128)S(1)} %pad_add_fusion.place_ref, bf16[128,512]{1,0:T(8,128)(2,1)S(1)} %get-tuple-element.54.mixed_ref, bf16[3,512,256]{2,1,0:T(8,128)(2,1)S(1)} %get-tuple-element.51.own_ref, bf16[3,512,256]{2,1,0:T(8,128)(2,1)S(1)} %collective-permute-done.11.sibling_ref, ...), custom_call_target="tpu_custom_call" | custom-call | flops 1100000000 | bytes 65536 | tf_op jit(solution)/shard_map/project/pallas_call | solution.py:41
  41.3 0.8 %collective-permute-start.14 = (bf16[128,512]{1,0:T(8,128)(2,1)S(1)}, bf16[128,512]{1,0:T(8,128)(2,1)S(1)}, u32[]{:S(2)}, u32[]{:S(2)}) collective-permute-start(bf16[128,512]{1,0:T(8,128)(2,1)S(1)} %get-tuple-element.56), channel_id=1, source_target_pairs={{0,1},{1,0},{2,3},{3,2},{4,5},{5,4},{6,7},{7,6},{8,9},{9,8},{10,11... | collective-permute-start | bytes 393224 | tf_op jit(solution)/shard_map/ppermute | solution.py:392
  42.1 2.2 %collective-permute-done.16 = bf16[128,512]{1,0:T(8,128)(2,1)S(1)} collective-permute-done((bf16[128,512]{1,0:T(8,128)(2,1)S(1)}, bf16[128,512]{1,0:T(8,128)(2,1)S(1)}, u32[]{:S(2)}, u32[]{:S(2)}) %collective-permute-start.16) | collective-permute-done | bytes 131104 | tf_op jit(solution)/shard_map/ppermute | solution.py:392
  44.3 6.0 %collective-permute-done.15 = bf16[128,512]{1,0:T(8,128)(2,1)S(1)} collective-permute-done((bf16[128,512]{1,0:T(8,128)(2,1)S(1)}, bf16[128,512]{1,0:T(8,128)(2,1)S(1)}, u32[]{:S(2)}, u32[]{:S(2)}) %collective-permute-start.15) | collective-permute-done | bytes 131104 | tf_op jit(solution)/shard_map/ppermute | solution.py:392
  50.3 0.7 %fusion = bf16[1,128,512]{2,1,0:T(8,128)(2,1)} fusion(bf16[128,512]{1,0:T(8,128)(2,1)S(1)} %collective-permute-done.16, bf16[128,512]{1,0:T(8,128)(2,1)S(1)} %collective-permute-done.15, bf16[128,512]{1,0:T(8,128)(2,1)S(1)} %collective-permute-done.14, bf16[128,512]{1,0:T(8,128)(2,1)S(1)} %get-tuple-element.55), kind=kLoop, calls=%fused_computation.1 | loop fusion | flops 524288 | bytes 655360 | tf_op jit(solution)/shard_map/broadcast_in_dim | solution.py:455
  (37 shorter events, 5.0 us)
Async XLA Ops:
  1.9 4.6 %collective-permute-start = (bf16[128,256]{1,0:T(8,128)(2,1)S(1)}, bf16[128,256]{1,0:T(8,128)(2,1)S(1)}, u32[]{:S(2)}, u32[]{:S(2)}) collective-permute-start(bf16[128,256]{1,0:T(8,128)(2,1)S(1)} %get-tuple-element.33), channel_id=1, source_target_pairs={{0,4},{4,0},{8,12},{12,8},{16,20},{20,16},{24,28},{28,24},{1,5},{5... | collective-permute-start | bytes 196616 | tf_op jit(solution)/shard_map/ppermute | solution.py:392
  2.4 13.4 %collective-permute-start.1 = (bf16[640,256]{1,0:T(8,128)(2,1)S(1)}, bf16[640,256]{1,0:T(8,128)(2,1)S(1)}, u32[]{:S(2)}, u32[]{:S(2)}) collective-permute-start(bf16[640,256]{1,0:T(8,128)(2,1)S(1)} %get-tuple-element.41.refs_4_), channel_id=1, source_target_pairs={{0,8},{4,12},{8,0},{12,4},{16,24},{20,28},{24,16},{28,20},{1,9},{5... | collective-permute-start | bytes 983048 | tf_op jit(solution)/shard_map/ppermute | solution.py:392
  5.0 10.9 %collective-permute-start.2 = (bf16[640,256]{1,0:T(8,128)(2,1)S(1)}, bf16[640,256]{1,0:T(8,128)(2,1)S(1)}, u32[]{:S(2)}, u32[]{:S(2)}) collective-permute-start(bf16[640,256]{1,0:T(8,128)(2,1)S(1)} %get-tuple-element.38.refs_5_), channel_id=1, source_target_pairs={{0,16},{4,20},{8,24},{12,28},{16,0},{20,4},{24,8},{28,12},{1,17},{... | collective-permute-start | bytes 983048 | tf_op jit(solution)/shard_map/ppermute | solution.py:392
  6.5 14.1 %collective-permute-start.5 = (bf16[640,256]{1,0:T(8,128)(2,1)S(1)}, bf16[640,256]{1,0:T(8,128)(2,1)S(1)}, u32[]{:S(2)}, u32[]{:S(2)}) collective-permute-start(bf16[640,256]{1,0:T(8,128)(2,1)S(1)} %get-tuple-element.38.refs_5_), channel_id=1, source_target_pairs={{0,8},{4,12},{8,0},{12,4},{16,24},{20,28},{24,16},{28,20},{1,9},{5... | collective-permute-start | bytes 983048 | tf_op jit(solution)/shard_map/ppermute | solution.py:392
  7.1 8.7 %collective-permute-start.3 = (bf16[256,256]{1,0:T(8,128)(2,1)S(1)}, bf16[256,256]{1,0:T(8,128)(2,1)S(1)}, u32[]{:S(2)}, u32[]{:S(2)}) collective-permute-start(bf16[256,256]{1,0:T(8,128)(2,1)S(1)} %constant_dynamic-update-slice_fusion.refs_0_), channel_id=1, source_target_pairs={{0,2},{1,3},{2,0},{3,1},{4,6},{5,7},{6,4},{7,5},{8,10},{9,11},{10,... | collective-permute-start | bytes 393224 | tf_op jit(solution)/shard_map/ppermute | solution.py:392
  9.8 0.7 %copy-start.3 = (s32[8]{0:T(128)S(1)}, s32[8]{0:T(128)}, u32[]{:S(2)}) copy-start(s32[8]{0:T(128)} %param.17) | copy-start | bytes 100
  11.8 11.9 %collective-permute-start.7 = (bf16[640,256]{1,0:T(8,128)(2,1)S(1)}, bf16[640,256]{1,0:T(8,128)(2,1)S(1)}, u32[]{:S(2)}, u32[]{:S(2)}) collective-permute-start(bf16[640,256]{1,0:T(8,128)(2,1)S(1)} %get-tuple-element.41.refs_4_), channel_id=1, source_target_pairs={{0,16},{4,20},{8,24},{12,28},{16,0},{20,4},{24,8},{28,12},{1,17},{... | collective-permute-start | bytes 983048 | tf_op jit(solution)/shard_map/ppermute | solution.py:392
  15.9 7.9 %collective-permute-start.4 = (bf16[256,256]{1,0:T(8,128)(2,1)S(1)}, bf16[256,256]{1,0:T(8,128)(2,1)S(1)}, u32[]{:S(2)}, u32[]{:S(2)}) collective-permute-start(bf16[256,256]{1,0:T(8,128)(2,1)S(1)} %constant_dynamic-update-slice_fusion.refs_0_), channel_id=1, source_target_pairs={{0,1},{1,0},{2,3},{3,2},{4,5},{5,4},{6,7},{7,6},{8,9},{9,8},{10,11... | collective-permute-start | bytes 393224 | tf_op jit(solution)/shard_map/ppermute | solution.py:392
  17.1 11.7 %collective-permute-start.8 = (bf16[640,256]{1,0:T(8,128)(2,1)S(1)}, bf16[640,256]{1,0:T(8,128)(2,1)S(1)}, u32[]{:S(2)}, u32[]{:S(2)}) collective-permute-start(bf16[640,256]{1,0:T(8,128)(2,1)S(1)} %collective-permute-done.1.refs_6_), channel_id=1, source_target_pairs={{0,16},{4,20},{8,24},{12,28},{16,0},{20,4},{24,8},{28,12},{1,17},{... | collective-permute-start | bytes 983048 | tf_op jit(solution)/shard_map/ppermute | solution.py:392
  18.7 10.2 %collective-permute-start.9 = (bf16[640,256]{1,0:T(8,128)(2,1)S(1)}, bf16[640,256]{1,0:T(8,128)(2,1)S(1)}, u32[]{:S(2)}, u32[]{:S(2)}) collective-permute-start(bf16[640,256]{1,0:T(8,128)(2,1)S(1)} %collective-permute-done.2.refs_9_), channel_id=1, source_target_pairs={{0,8},{4,12},{8,0},{12,4},{16,24},{20,28},{24,16},{28,20},{1,9},{5... | collective-permute-start | bytes 983048 | tf_op jit(solution)/shard_map/ppermute | solution.py:392
  20.6 5.0 %collective-permute-start.6 = (bf16[256,256]{1,0:T(8,128)(2,1)S(1)}, bf16[256,256]{1,0:T(8,128)(2,1)S(1)}, u32[]{:S(2)}, u32[]{:S(2)}) collective-permute-start(bf16[256,256]{1,0:T(8,128)(2,1)S(1)} %collective-permute-done.3.refs_2_), channel_id=1, source_target_pairs={{0,1},{1,0},{2,3},{3,2},{4,5},{5,4},{6,7},{7,6},{8,9},{9,8},{10,11... | collective-permute-start | bytes 393224 | tf_op jit(solution)/shard_map/ppermute | solution.py:392
  23.0 0.7 %copy-start.2 = (bf16[2048]{0:T(1024)(128)(2,1)S(1)}, bf16[2048]{0:T(1024)(128)(2,1)}, u32[]{:S(2)}) copy-start(bf16[2048]{0:T(1024)(128)(2,1)} %param.10) | copy-start | bytes 12292
  28.8 2.2 %copy-start.1 = (bf16[1,2048,128]{2,1,0:T(8,128)(2,1)S(1)}, bf16[1,2048,128]{2,1,0:T(8,128)(2,1)}, u32[]{:S(2)}) copy-start(bf16[1,2048,128]{2,1,0:T(8,128)(2,1)} %param.16) | copy-start | bytes 1572868
  29.1 1.9 %copy-start = (bf16[1,2048,128]{2,1,0:T(8,128)(2,1)S(1)}, bf16[1,2048,128]{2,1,0:T(8,128)(2,1)}, u32[]{:S(2)}) copy-start(bf16[1,2048,128]{2,1,0:T(8,128)(2,1)} %param.15) | copy-start | bytes 1572868
  29.1 1.9 %collective-permute-start.10 = (f32[128,896]{1,0:T(8,128)S(1)}, f32[128,896]{1,0:T(8,128)S(1)}, u32[]{:S(2)}, u32[]{:S(2)}) collective-permute-start(f32[128,896]{1,0:T(8,128)S(1)} %get-tuple-element.49), channel_id=1, source_target_pairs={{0,4},{4,0},{8,12},{12,8},{16,20},{20,16},{24,28},{28,24},{1,5},{5... | collective-permute-start | bytes 1376264 | tf_op jit(solution)/shard_map/ppermute | solution.py:392
  29.2 6.3 %collective-permute-start.11 = (bf16[3,512,256]{2,1,0:T(8,128)(2,1)S(1)}, bf16[3,512,256]{2,1,0:T(8,128)(2,1)S(1)}, u32[]{:S(2)}, u32[]{:S(2)}) collective-permute-start(bf16[3,512,256]{2,1,0:T(8,128)(2,1)S(1)} %get-tuple-element.51.own_ref), channel_id=1, source_target_pairs={{0,4},{4,0},{8,12},{12,8},{16,20},{20,16},{24,28},{28,24},{1,5},{5... | collective-permute-start | bytes 2359304 | tf_op jit(solution)/shard_map/ppermute | solution.py:392
  29.7 5.8 %collective-permute-start.12 = (bf16[256,256]{1,0:T(8,128)(2,1)S(1)}, bf16[256,256]{1,0:T(8,128)(2,1)S(1)}, u32[]{:S(2)}, u32[]{:S(2)}) collective-permute-start(bf16[256,256]{1,0:T(8,128)(2,1)S(1)} %slice.8), channel_id=1, source_target_pairs={{0,4},{4,0},{8,12},{12,8},{16,20},{20,16},{24,28},{28,24},{1,5},{5... | collective-permute-start | bytes 393224 | tf_op jit(solution)/shard_map/ppermute | solution.py:392
  29.9 5.6 %collective-permute-start.13 = (bf16[256,256]{1,0:T(8,128)(2,1)S(1)}, bf16[256,256]{1,0:T(8,128)(2,1)S(1)}, u32[]{:S(2)}, u32[]{:S(2)}) collective-permute-start(bf16[256,256]{1,0:T(8,128)(2,1)S(1)} %slice.9), channel_id=1, source_target_pairs={{0,4},{4,0},{8,12},{12,8},{16,20},{20,16},{24,28},{28,24},{1,5},{5... | collective-permute-start | bytes 393224 | tf_op jit(solution)/shard_map/ppermute | solution.py:392
  36.6 7.7 %collective-permute-start.16 = (bf16[128,512]{1,0:T(8,128)(2,1)S(1)}, bf16[128,512]{1,0:T(8,128)(2,1)S(1)}, u32[]{:S(2)}, u32[]{:S(2)}) collective-permute-start(bf16[128,512]{1,0:T(8,128)(2,1)S(1)} %get-tuple-element.58), channel_id=1, source_target_pairs={{0,3},{1,2},{2,1},{3,0},{4,7},{5,6},{6,5},{7,4},{8,11},{9,10},{10,... | collective-permute-start | bytes 393224 | tf_op jit(solution)/shard_map/ppermute | solution.py:392
  40.2 10.0 %collective-permute-start.15 = (bf16[128,512]{1,0:T(8,128)(2,1)S(1)}, bf16[128,512]{1,0:T(8,128)(2,1)S(1)}, u32[]{:S(2)}, u32[]{:S(2)}) collective-permute-start(bf16[128,512]{1,0:T(8,128)(2,1)S(1)} %get-tuple-element.57), channel_id=1, source_target_pairs={{0,2},{1,3},{2,0},{3,1},{4,6},{5,7},{6,4},{7,5},{8,10},{9,11},{10,... | collective-permute-start | bytes 393224 | tf_op jit(solution)/shard_map/ppermute | solution.py:392
  41.3 9.0 %collective-permute-start.14 = (bf16[128,512]{1,0:T(8,128)(2,1)S(1)}, bf16[128,512]{1,0:T(8,128)(2,1)S(1)}, u32[]{:S(2)}, u32[]{:S(2)}) collective-permute-start(bf16[128,512]{1,0:T(8,128)(2,1)S(1)} %get-tuple-element.56), channel_id=1, source_target_pairs={{0,1},{1,0},{2,3},{3,2},{4,5},{5,4},{6,7},{7,6},{8,9},{9,8},{10,11... | collective-permute-start | bytes 393224 | tf_op jit(solution)/shard_map/ppermute | solution.py:392

commit v4 on v3

--- a/solution.py
+++ b/solution.py
@@ -244,7 +244,9 @@
         scores = upcoming
         if start + QUERY_ROWS < queries:
             upcoming = score(start + QUERY_ROWS)
-        scores = jnp.where(mask, scores, masked_score)
+        sure = scores.shape[1] - mask.shape[1]
+        unsure = jnp.where(mask, scores[:, sure:], masked_score)
+        scores = jnp.concatenate([scores[:, :sure], unsure], axis=1) if sure else unsure
         peak = jnp.max(scores, axis=-1, keepdims=True)
         weights = jnp.exp2(scores - peak).astype(jnp.bfloat16)
         total = jnp.dot(
@@ -303,8 +305,8 @@
 
         @pl.when((length > cached - step) & (length <= cached))
         def _(cached=cached):
-            shape = (tokens, cached + tokens)
-            column = lax.broadcasted_iota(jnp.int32, shape, 1)
+            shape = (tokens, step + tokens)
+            column = cached - step + lax.broadcasted_iota(jnp.int32, shape, 1)
             token = lax.broadcasted_iota(jnp.int32, shape, 0)
             limit = jnp.where(column < cached, length, cached + 1 + token)
             heads = attend(
@@ -431,6 +433,7 @@
     cosine, sine = phases(length[0], tokens)
     partial, cosine, sine = lax.optimization_barrier((partial, cosine, sine))
     here, there = far_products(partial, last, square, d_top, d_bottom)
+    there, o_near = lax.optimization_barrier((there, o_near))
     mixed, new_keys, new_values = attention(
         length,
         norm_gain.shape[0],
@@ -446,11 +449,11 @@
     first, second = d_top.shape[0] - high, d_bottom.shape[0] - w_out.shape[0] + high
     o_last = [d_top, d_bottom, core(d_top[first:]), core(d_bottom[second:])]
     terms = {}
-    terms[2], terms[3] = project((2, 3), mixed, place, o_near, o_sibling, o_last)
+    terms[2], terms[3] = project((2, 3,), mixed, place, o_near, o_sibling, o_last)
     mixed, terms[2], terms[3] = lax.optimization_barrier((mixed, terms[2], terms[3]))
-    terms[0], terms[1] = project((0, 1), mixed, place, o_near, o_sibling, o_last)
+    terms[0], terms[1] = project((0, 1,), mixed, place, o_near, o_sibling, o_last)
     total = terms[0].astype(jnp.float32)
-    for m in (1, 2, 3):
+    for m in (3, 1, 2):
         total = total + swap(terms[m], "tp", m).astype(jnp.float32)
     return total.astype(jnp.bfloat16)[None], new_keys[None], new_values[None]
 

time: 50.9 us -> 50 us (0.982); the launches traced: 51 us -> 49.1 us
  waiting for transfers between devices: 17.5 us -> 16 us
    ppermute x17, waiting for transfers between devices: 17.5 us -> 16 us  [swap(): return lax.ppermute(x, axis, [(i, i ^ mask) for i in range(count)])]
  transfers between devices with their start and end apart: 17 -> 17, of which waited for: 7 -> 8; matrix products, arithmetic and copies ran while one was open for 4% -> 4% of each run, Pallas kernels for 13% -> 13%
where the time goes in v4:
time: 50 us; the launch traced here: 49.1 us
  starting transfers between devices  19.5 us (39%)
  waiting for transfers between devices  16 us (32%)
  Pallas kernels  8.88 us (18%)
  local copies, waits for them, and re-layouts  2.12 us (4%)
  other arithmetic  1.78 us (4%)
  between operations  0.78 us (2%)
    ppermute x17, starting transfers between devices, swap(): return lax.ppermute(x, axis, [(i, i ^ mask) for i in range(count)])  19.5 us
    ppermute x17, waiting for transfers between devices, swap(): return lax.ppermute(x, axis, [(i, i ^ mask) for i in range(count)])  16 us
    pallas_call x6, Pallas kernels, placed(): run(*[pltpu.with_memory_space_constraint(x, pltpu.HBM) if spec is HB else...  8.88 us
    unnamed x9, local copies, waits for them, and re-layouts  1.35 us
  transfers between devices with their start and end apart: 17, of which 8 were waited for; matrix products, arithmetic and copies ran while one was open for 4% of the time, Pallas kernels for 13%

profile of v4, /device:TPU:0, one launch (start us, length us, event | category | flops | bytes accessed | tf_op | source)
XLA Modules:
  0.0 49.1 jit_solution(6798957119785723047)
XLA Ops:
  0.6 1.3 %pack.1 = (bf16[640,256]{1,0:T(8,128)(2,1)S(1)}, bf16[640,256]{1,0:T(8,128)(2,1)S(1)}, bf16[128,256]{1,0:T(8,128)(2,1)S(1)}, bf16[128,256]{1,0:T(8,128)(2,1)S(1)}) custom-call(bf16[128,512]{1,0:T(8,128)(2,1)} %bitcast.13, bf16[256,512]{1,0:T(8,128)(2,1)} %wq_ref.1, bf16[256,128]{1,0:T(8,128)(2,1)} %wk_ref.1, bf16[256,128]{1,0:T(8,128)(2,1)} %wv_ref.1, ...), custom_call_target="tpu_custom_call" | custom-call | flops 1100000000 | bytes 65536 | tf_op jit(solution)/shard_map/pack/pallas_call | solution.py:41
  2.4 2.6 %collective-permute-start.1 = (bf16[640,256]{1,0:T(8,128)(2,1)S(1)}, bf16[640,256]{1,0:T(8,128)(2,1)S(1)}, u32[]{:S(2)}, u32[]{:S(2)}) collective-permute-start(bf16[640,256]{1,0:T(8,128)(2,1)S(1)} %get-tuple-element.43.refs_4_), channel_id=1, source_target_pairs={{0,8},{4,12},{8,0},{12,4},{16,24},{20,28},{24,16},{28,20},{1,9},{5... | collective-permute-start | bytes 983048 | tf_op jit(solution)/shard_map/ppermute | solution.py:394
  5.0 1.5 %collective-permute-start.2 = (bf16[640,256]{1,0:T(8,128)(2,1)S(1)}, bf16[640,256]{1,0:T(8,128)(2,1)S(1)}, u32[]{:S(2)}, u32[]{:S(2)}) collective-permute-start(bf16[640,256]{1,0:T(8,128)(2,1)S(1)} %get-tuple-element.40.refs_5_), channel_id=1, source_target_pairs={{0,16},{4,20},{8,24},{12,28},{16,0},{20,4},{24,8},{28,12},{1,17},{... | collective-permute-start | bytes 983048 | tf_op jit(solution)/shard_map/ppermute | solution.py:394
  7.1 2.6 %collective-permute-start.3 = (bf16[256,256]{1,0:T(8,128)(2,1)S(1)}, bf16[256,256]{1,0:T(8,128)(2,1)S(1)}, u32[]{:S(2)}, u32[]{:S(2)}) collective-permute-start(bf16[256,256]{1,0:T(8,128)(2,1)S(1)} %constant_dynamic-update-slice_fusion.refs_0_), channel_id=1, source_target_pairs={{0,2},{1,3},{2,0},{3,1},{4,6},{5,7},{6,4},{7,5},{8,10},{9,11},{10,... | collective-permute-start | bytes 393224 | tf_op jit(solution)/shard_map/ppermute | solution.py:394
  9.8 0.7 %copy-done.3 = s32[8]{0:T(128)S(1)} copy-done((s32[8]{0:T(128)S(1)}, s32[8]{0:T(128)}, u32[]{:S(2)}) %copy-start.3) | copy-done | bytes 56
  11.1 0.7 %add_convert_fusion.1 = f32[128]{0:T(128)S(1)} fusion(s32[]{:T(128)} %bitcast.4), kind=kLoop, calls=%fused_computation.8 | loop fusion | flops 256 | bytes 516 | tf_op jit(solution)/shard_map/convert_element_type | solution.py:386
  12.5 3.4 %collective-permute-done.3.refs_2_ = bf16[256,256]{1,0:T(8,128)(2,1)S(1)} collective-permute-done((bf16[256,256]{1,0:T(8,128)(2,1)S(1)}, bf16[256,256]{1,0:T(8,128)(2,1)S(1)}, u32[]{:S(2)}, u32[]{:S(2)}) %collective-permute-start.3) | collective-permute-done | bytes 131104 | tf_op jit(solution)/shard_map/ppermute | solution.py:394
  15.9 1.3 %collective-permute-start.4 = (bf16[256,256]{1,0:T(8,128)(2,1)S(1)}, bf16[256,256]{1,0:T(8,128)(2,1)S(1)}, u32[]{:S(2)}, u32[]{:S(2)}) collective-permute-start(bf16[256,256]{1,0:T(8,128)(2,1)S(1)} %constant_dynamic-update-slice_fusion.refs_0_), channel_id=1, source_target_pairs={{0,1},{1,0},{2,3},{3,2},{4,5},{5,4},{6,7},{7,6},{8,9},{9,8},{10,11... | collective-permute-start | bytes 393224 | tf_op jit(solution)/shard_map/ppermute | solution.py:394
  17.1 1.5 %collective-permute-start.8 = (bf16[640,256]{1,0:T(8,128)(2,1)S(1)}, bf16[640,256]{1,0:T(8,128)(2,1)S(1)}, u32[]{:S(2)}, u32[]{:S(2)}) collective-permute-start(bf16[640,256]{1,0:T(8,128)(2,1)S(1)} %collective-permute-done.1.refs_6_), channel_id=1, source_target_pairs={{0,16},{4,20},{8,24},{12,28},{16,0},{20,4},{24,8},{28,12},{1,17},{... | collective-permute-start | bytes 983048 | tf_op jit(solution)/shard_map/ppermute | solution.py:394
  19.2 1.4 %collective-permute-done.5.refs_7_ = bf16[640,256]{1,0:T(8,128)(2,1)S(1)} collective-permute-done((bf16[640,256]{1,0:T(8,128)(2,1)S(1)}, bf16[640,256]{1,0:T(8,128)(2,1)S(1)}, u32[]{:S(2)}, u32[]{:S(2)}) %collective-permute-start.5) | collective-permute-done | bytes 327712 | tf_op jit(solution)/shard_map/ppermute | solution.py:394
  20.6 2.0 %collective-permute-start.6 = (bf16[256,256]{1,0:T(8,128)(2,1)S(1)}, bf16[256,256]{1,0:T(8,128)(2,1)S(1)}, u32[]{:S(2)}, u32[]{:S(2)}) collective-permute-start(bf16[256,256]{1,0:T(8,128)(2,1)S(1)} %collective-permute-done.3.refs_2_), channel_id=1, source_target_pairs={{0,1},{1,0},{2,3},{3,2},{4,5},{5,4},{6,7},{7,6},{8,9},{9,8},{10,11... | collective-permute-start | bytes 393224 | tf_op jit(solution)/shard_map/ppermute | solution.py:394
  23.0 0.7 %copy-done.2 = bf16[2048]{0:T(1024)(128)(2,1)S(1)} copy-done((bf16[2048]{0:T(1024)(128)(2,1)S(1)}, bf16[2048]{0:T(1024)(128)(2,1)}, u32[]{:S(2)}) %copy-start.2) | copy-done | bytes 4120
  23.7 1.9 %collective-permute-done.6.refs_3_ = bf16[256,256]{1,0:T(8,128)(2,1)S(1)} collective-permute-done((bf16[256,256]{1,0:T(8,128)(2,1)S(1)}, bf16[256,256]{1,0:T(8,128)(2,1)S(1)}, u32[]{:S(2)}, u32[]{:S(2)}) %collective-permute-start.6) | collective-permute-done | bytes 131104 | tf_op jit(solution)/shard_map/ppermute | solution.py:394
  25.6 1.2 %near_products.1 = (f32[256,768]{1,0:T(8,128)S(1)}, bf16[256,256]{1,0:T(8,128)(2,1)S(1)}, f32[256,128]{1,0:T(8,128)S(1)}, bf16[3,512,256]{2,1,0:T(8,128)(2,1)S(1)}) custom-call(s32[3]{0:T(128)S(1)} %pad_add_fusion.place_ref, bf16[8,1,256]{2,1,0:T(2,128)(2,1)S(1)} %reshape.24.gain_ref, bf16[256,256]{1,0:T(8,128)(2,1)S(1)} %constant_dynamic-update-slice_fusion.refs_0_, ...), custom_call_target="tpu_custom_call" | custom-call | flops 110000000 | bytes 65536 | tf_op jit(solution)/shard_map/near_products/pallas_call | solution.py:41
  26.8 2.1 %collective-permute-done.8.top_ref.refs_0_ = bf16[640,256]{1,0:T(8,128)(2,1)S(1)} collective-permute-done((bf16[640,256]{1,0:T(8,128)(2,1)S(1)}, bf16[640,256]{1,0:T(8,128)(2,1)S(1)}, u32[]{:S(2)}, u32[]{:S(2)}) %collective-permute-start.8) | collective-permute-done | bytes 327712 | tf_op jit(solution)/shard_map/ppermute | solution.py:394
  31.0 4.1 %attention.1 = (bf16[128,512]{1,0:T(8,128)(2,1)S(1)}, bf16[128,128]{1,0:T(8,128)(2,1)}, bf16[128,128]{1,0:T(8,128)(2,1)}) custom-call(s32[1]{0:T(128)} %dynamic_slice.3.length_ref, f32[128,128]{1,0:T(8,128)S(1)} %get-tuple-element.45.cos_ref, f32[128,128]{1,0:T(8,128)S(1)} %get-tuple-element.46.sin_ref, f32[128,896]{1,0:T(8,128)S(1)} %get-tuple-element.50.here_ref, ...), custom_call_target="tpu_custom_call" | custom-call | flops 4400000000 | bytes 65536 | tf_op jit(solution)/shard_map/attention/pallas_call | solution.py:41
  35.1 1.0 %project.2 = (bf16[128,512]{1,0:T(8,128)(2,1)S(1)}, bf16[128,512]{1,0:T(8,128)(2,1)S(1)}) custom-call(s32[3]{0:T(128)S(1)} %pad_add_fusion.place_ref, bf16[128,512]{1,0:T(8,128)(2,1)S(1)} %get-tuple-element.58.mixed_ref, bf16[3,512,256]{2,1,0:T(8,128)(2,1)S(1)} %get-tuple-element.55.own_ref, bf16[3,512,256]{2,1,0:T(8,128)(2,1)S(1)} %collective-permute-done.11.sibling_ref, ...), custom_call_target="tpu_custom_call" | custom-call | flops 1100000000 | bytes 65536 | tf_op jit(solution)/shard_map/project/pallas_call | solution.py:41
  36.2 2.7 %collective-permute-start.16 = (bf16[128,512]{1,0:T(8,128)(2,1)S(1)}, bf16[128,512]{1,0:T(8,128)(2,1)S(1)}, u32[]{:S(2)}, u32[]{:S(2)}) collective-permute-start(bf16[128,512]{1,0:T(8,128)(2,1)S(1)} %get-tuple-element.62), channel_id=1, source_target_pairs={{0,2},{1,3},{2,0},{3,1},{4,6},{5,7},{6,4},{7,5},{8,10},{9,11},{10,... | collective-permute-start | bytes 393224 | tf_op jit(solution)/shard_map/ppermute | solution.py:394
  38.8 1.0 %project.3 = (bf16[128,512]{1,0:T(8,128)(2,1)S(1)}, bf16[128,512]{1,0:T(8,128)(2,1)S(1)}) custom-call(s32[3]{0:T(128)S(1)} %pad_add_fusion.place_ref, bf16[128,512]{1,0:T(8,128)(2,1)S(1)} %get-tuple-element.58.mixed_ref, bf16[3,512,256]{2,1,0:T(8,128)(2,1)S(1)} %get-tuple-element.55.own_ref, bf16[3,512,256]{2,1,0:T(8,128)(2,1)S(1)} %collective-permute-done.11.sibling_ref, ...), custom_call_target="tpu_custom_call" | custom-call | flops 1100000000 | bytes 65536 | tf_op jit(solution)/shard_map/project/pallas_call | solution.py:41
  39.9 1.6 %collective-permute-start.15 = (bf16[128,512]{1,0:T(8,128)(2,1)S(1)}, bf16[128,512]{1,0:T(8,128)(2,1)S(1)}, u32[]{:S(2)}, u32[]{:S(2)}) collective-permute-start(bf16[128,512]{1,0:T(8,128)(2,1)S(1)} %get-tuple-element.61), channel_id=1, source_target_pairs={{0,1},{1,0},{2,3},{3,2},{4,5},{5,4},{6,7},{7,6},{8,9},{9,8},{10,11... | collective-permute-start | bytes 393224 | tf_op jit(solution)/shard_map/ppermute | solution.py:394
  41.7 3.3 %collective-permute-done.16 = bf16[128,512]{1,0:T(8,128)(2,1)S(1)} collective-permute-done((bf16[128,512]{1,0:T(8,128)(2,1)S(1)}, bf16[128,512]{1,0:T(8,128)(2,1)S(1)}, u32[]{:S(2)}, u32[]{:S(2)}) %collective-permute-start.16) | collective-permute-done | bytes 131104 | tf_op jit(solution)/shard_map/ppermute | solution.py:394
  45.0 1.7 %collective-permute-done.15 = bf16[128,512]{1,0:T(8,128)(2,1)S(1)} collective-permute-done((bf16[128,512]{1,0:T(8,128)(2,1)S(1)}, bf16[128,512]{1,0:T(8,128)(2,1)S(1)}, u32[]{:S(2)}, u32[]{:S(2)}) %collective-permute-start.15) | collective-permute-done | bytes 131104 | tf_op jit(solution)/shard_map/ppermute | solution.py:394
  46.8 1.6 %collective-permute-done.14 = bf16[128,512]{1,0:T(8,128)(2,1)S(1)} collective-permute-done((bf16[128,512]{1,0:T(8,128)(2,1)S(1)}, bf16[128,512]{1,0:T(8,128)(2,1)S(1)}, u32[]{:S(2)}, u32[]{:S(2)}) %collective-permute-start.14) | collective-permute-done | bytes 131104 | tf_op jit(solution)/shard_map/ppermute | solution.py:394
  48.4 0.7 %fusion = bf16[1,128,512]{2,1,0:T(8,128)(2,1)} fusion(bf16[128,512]{1,0:T(8,128)(2,1)S(1)} %collective-permute-done.16, bf16[128,512]{1,0:T(8,128)(2,1)S(1)} %collective-permute-done.15, bf16[128,512]{1,0:T(8,128)(2,1)S(1)} %collective-permute-done.14, bf16[128,512]{1,0:T(8,128)(2,1)S(1)} %get-tuple-element.59), kind=kLoop, calls=%fused_computation.1 | loop fusion | flops 524288 | bytes 655360 | tf_op jit(solution)/shard_map/broadcast_in_dim | solution.py:458
  (37 shorter events, 5.8 us)
Async XLA Ops:
  1.9 4.6 %collective-permute-start = (bf16[128,256]{1,0:T(8,128)(2,1)S(1)}, bf16[128,256]{1,0:T(8,128)(2,1)S(1)}, u32[]{:S(2)}, u32[]{:S(2)}) collective-permute-start(bf16[128,256]{1,0:T(8,128)(2,1)S(1)} %get-tuple-element.35), channel_id=1, source_target_pairs={{0,4},{4,0},{8,12},{12,8},{16,20},{20,16},{24,28},{28,24},{1,5},{5... | collective-permute-start | bytes 196616 | tf_op jit(solution)/shard_map/ppermute | solution.py:394
  2.4 13.4 %collective-permute-start.1 = (bf16[640,256]{1,0:T(8,128)(2,1)S(1)}, bf16[640,256]{1,0:T(8,128)(2,1)S(1)}, u32[]{:S(2)}, u32[]{:S(2)}) collective-permute-start(bf16[640,256]{1,0:T(8,128)(2,1)S(1)} %get-tuple-element.43.refs_4_), channel_id=1, source_target_pairs={{0,8},{4,12},{8,0},{12,4},{16,24},{20,28},{24,16},{28,20},{1,9},{5... | collective-permute-start | bytes 983048 | tf_op jit(solution)/shard_map/ppermute | solution.py:394
  5.0 10.9 %collective-permute-start.2 = (bf16[640,256]{1,0:T(8,128)(2,1)S(1)}, bf16[640,256]{1,0:T(8,128)(2,1)S(1)}, u32[]{:S(2)}, u32[]{:S(2)}) collective-permute-start(bf16[640,256]{1,0:T(8,128)(2,1)S(1)} %get-tuple-element.40.refs_5_), channel_id=1, source_target_pairs={{0,16},{4,20},{8,24},{12,28},{16,0},{20,4},{24,8},{28,12},{1,17},{... | collective-permute-start | bytes 983048 | tf_op jit(solution)/shard_map/ppermute | solution.py:394
  6.5 14.1 %collective-permute-start.5 = (bf16[640,256]{1,0:T(8,128)(2,1)S(1)}, bf16[640,256]{1,0:T(8,128)(2,1)S(1)}, u32[]{:S(2)}, u32[]{:S(2)}) collective-permute-start(bf16[640,256]{1,0:T(8,128)(2,1)S(1)} %get-tuple-element.40.refs_5_), channel_id=1, source_target_pairs={{0,8},{4,12},{8,0},{12,4},{16,24},{20,28},{24,16},{28,20},{1,9},{5... | collective-permute-start | bytes 983048 | tf_op jit(solution)/shard_map/ppermute | solution.py:394
  7.1 8.7 %collective-permute-start.3 = (bf16[256,256]{1,0:T(8,128)(2,1)S(1)}, bf16[256,256]{1,0:T(8,128)(2,1)S(1)}, u32[]{:S(2)}, u32[]{:S(2)}) collective-permute-start(bf16[256,256]{1,0:T(8,128)(2,1)S(1)} %constant_dynamic-update-slice_fusion.refs_0_), channel_id=1, source_target_pairs={{0,2},{1,3},{2,0},{3,1},{4,6},{5,7},{6,4},{7,5},{8,10},{9,11},{10,... | collective-permute-start | bytes 393224 | tf_op jit(solution)/shard_map/ppermute | solution.py:394
  9.8 0.7 %copy-start.3 = (s32[8]{0:T(128)S(1)}, s32[8]{0:T(128)}, u32[]{:S(2)}) copy-start(s32[8]{0:T(128)} %param.17) | copy-start | bytes 100
  11.8 11.9 %collective-permute-start.7 = (bf16[640,256]{1,0:T(8,128)(2,1)S(1)}, bf16[640,256]{1,0:T(8,128)(2,1)S(1)}, u32[]{:S(2)}, u32[]{:S(2)}) collective-permute-start(bf16[640,256]{1,0:T(8,128)(2,1)S(1)} %get-tuple-element.43.refs_4_), channel_id=1, source_target_pairs={{0,16},{4,20},{8,24},{12,28},{16,0},{20,4},{24,8},{28,12},{1,17},{... | collective-permute-start | bytes 983048 | tf_op jit(solution)/shard_map/ppermute | solution.py:394
  15.9 7.9 %collective-permute-start.4 = (bf16[256,256]{1,0:T(8,128)(2,1)S(1)}, bf16[256,256]{1,0:T(8,128)(2,1)S(1)}, u32[]{:S(2)}, u32[]{:S(2)}) collective-permute-start(bf16[256,256]{1,0:T(8,128)(2,1)S(1)} %constant_dynamic-update-slice_fusion.refs_0_), channel_id=1, source_target_pairs={{0,1},{1,0},{2,3},{3,2},{4,5},{5,4},{6,7},{7,6},{8,9},{9,8},{10,11... | collective-permute-start | bytes 393224 | tf_op jit(solution)/shard_map/ppermute | solution.py:394
  17.1 11.7 %collective-permute-start.8 = (bf16[640,256]{1,0:T(8,128)(2,1)S(1)}, bf16[640,256]{1,0:T(8,128)(2,1)S(1)}, u32[]{:S(2)}, u32[]{:S(2)}) collective-permute-start(bf16[640,256]{1,0:T(8,128)(2,1)S(1)} %collective-permute-done.1.refs_6_), channel_id=1, source_target_pairs={{0,16},{4,20},{8,24},{12,28},{16,0},{20,4},{24,8},{28,12},{1,17},{... | collective-permute-start | bytes 983048 | tf_op jit(solution)/shard_map/ppermute | solution.py:394
  18.7 10.2 %collective-permute-start.9 = (bf16[640,256]{1,0:T(8,128)(2,1)S(1)}, bf16[640,256]{1,0:T(8,128)(2,1)S(1)}, u32[]{:S(2)}, u32[]{:S(2)}) collective-permute-start(bf16[640,256]{1,0:T(8,128)(2,1)S(1)} %collective-permute-done.2.refs_9_), channel_id=1, source_target_pairs={{0,8},{4,12},{8,0},{12,4},{16,24},{20,28},{24,16},{28,20},{1,9},{5... | collective-permute-start | bytes 983048 | tf_op jit(solution)/shard_map/ppermute | solution.py:394
  20.6 5.0 %collective-permute-start.6 = (bf16[256,256]{1,0:T(8,128)(2,1)S(1)}, bf16[256,256]{1,0:T(8,128)(2,1)S(1)}, u32[]{:S(2)}, u32[]{:S(2)}) collective-permute-start(bf16[256,256]{1,0:T(8,128)(2,1)S(1)} %collective-permute-done.3.refs_2_), channel_id=1, source_target_pairs={{0,1},{1,0},{2,3},{3,2},{4,5},{5,4},{6,7},{7,6},{8,9},{9,8},{10,11... | collective-permute-start | bytes 393224 | tf_op jit(solution)/shard_map/ppermute | solution.py:394
  23.0 0.7 %copy-start.2 = (bf16[2048]{0:T(1024)(128)(2,1)S(1)}, bf16[2048]{0:T(1024)(128)(2,1)}, u32[]{:S(2)}) copy-start(bf16[2048]{0:T(1024)(128)(2,1)} %param.10) | copy-start | bytes 12292
  28.8 2.2 %copy-start.1 = (bf16[1,2048,128]{2,1,0:T(8,128)(2,1)S(1)}, bf16[1,2048,128]{2,1,0:T(8,128)(2,1)}, u32[]{:S(2)}) copy-start(bf16[1,2048,128]{2,1,0:T(8,128)(2,1)} %param.16) | copy-start | bytes 1572868
  29.1 1.9 %copy-start = (bf16[1,2048,128]{2,1,0:T(8,128)(2,1)S(1)}, bf16[1,2048,128]{2,1,0:T(8,128)(2,1)}, u32[]{:S(2)}) copy-start(bf16[1,2048,128]{2,1,0:T(8,128)(2,1)} %param.15) | copy-start | bytes 1572868
  29.1 1.9 %collective-permute-start.10 = (f32[128,896]{1,0:T(8,128)S(1)}, f32[128,896]{1,0:T(8,128)S(1)}, u32[]{:S(2)}, u32[]{:S(2)}) collective-permute-start(f32[128,896]{1,0:T(8,128)S(1)} %get-tuple-element.53), channel_id=1, source_target_pairs={{0,4},{4,0},{8,12},{12,8},{16,20},{20,16},{24,28},{28,24},{1,5},{5... | collective-permute-start | bytes 1376264 | tf_op jit(solution)/shard_map/ppermute | solution.py:394
  29.2 5.9 %collective-permute-start.11 = (bf16[3,512,256]{2,1,0:T(8,128)(2,1)S(1)}, bf16[3,512,256]{2,1,0:T(8,128)(2,1)S(1)}, u32[]{:S(2)}, u32[]{:S(2)}) collective-permute-start(bf16[3,512,256]{2,1,0:T(8,128)(2,1)S(1)} %get-tuple-element.55.own_ref), channel_id=1, source_target_pairs={{0,4},{4,0},{8,12},{12,8},{16,20},{20,16},{24,28},{28,24},{1,5},{5... | collective-permute-start | bytes 2359304 | tf_op jit(solution)/shard_map/ppermute | solution.py:394
  29.7 5.4 %collective-permute-start.12 = (bf16[256,256]{1,0:T(8,128)(2,1)S(1)}, bf16[256,256]{1,0:T(8,128)(2,1)S(1)}, u32[]{:S(2)}, u32[]{:S(2)}) collective-permute-start(bf16[256,256]{1,0:T(8,128)(2,1)S(1)} %slice.8), channel_id=1, source_target_pairs={{0,4},{4,0},{8,12},{12,8},{16,20},{20,16},{24,28},{28,24},{1,5},{5... | collective-permute-start | bytes 393224 | tf_op jit(solution)/shard_map/ppermute | solution.py:394
  29.9 5.2 %collective-permute-start.13 = (bf16[256,256]{1,0:T(8,128)(2,1)S(1)}, bf16[256,256]{1,0:T(8,128)(2,1)S(1)}, u32[]{:S(2)}, u32[]{:S(2)}) collective-permute-start(bf16[256,256]{1,0:T(8,128)(2,1)S(1)} %slice.9), channel_id=1, source_target_pairs={{0,4},{4,0},{8,12},{12,8},{16,20},{20,16},{24,28},{28,24},{1,5},{5... | collective-permute-start | bytes 393224 | tf_op jit(solution)/shard_map/ppermute | solution.py:394
  36.2 8.8 %collective-permute-start.16 = (bf16[128,512]{1,0:T(8,128)(2,1)S(1)}, bf16[128,512]{1,0:T(8,128)(2,1)S(1)}, u32[]{:S(2)}, u32[]{:S(2)}) collective-permute-start(bf16[128,512]{1,0:T(8,128)(2,1)S(1)} %get-tuple-element.62), channel_id=1, source_target_pairs={{0,2},{1,3},{2,0},{3,1},{4,6},{5,7},{6,4},{7,5},{8,10},{9,11},{10,... | collective-permute-start | bytes 393224 | tf_op jit(solution)/shard_map/ppermute | solution.py:394
  39.9 6.9 %collective-permute-start.15 = (bf16[128,512]{1,0:T(8,128)(2,1)S(1)}, bf16[128,512]{1,0:T(8,128)(2,1)S(1)}, u32[]{:S(2)}, u32[]{:S(2)}) collective-permute-start(bf16[128,512]{1,0:T(8,128)(2,1)S(1)} %get-tuple-element.61), channel_id=1, source_target_pairs={{0,1},{1,0},{2,3},{3,2},{4,5},{5,4},{6,7},{7,6},{8,9},{9,8},{10,11... | collective-permute-start | bytes 393224 | tf_op jit(solution)/shard_map/ppermute | solution.py:394
  41.5 6.9 %collective-permute-start.14 = (bf16[128,512]{1,0:T(8,128)(2,1)S(1)}, bf16[128,512]{1,0:T(8,128)(2,1)S(1)}, u32[]{:S(2)}, u32[]{:S(2)}) collective-permute-start(bf16[128,512]{1,0:T(8,128)(2,1)S(1)} %get-tuple-element.60), channel_id=1, source_target_pairs={{0,3},{1,2},{2,1},{3,0},{4,7},{5,6},{6,5},{7,4},{8,11},{9,10},{10,... | collective-permute-start | bytes 393224 | tf_op jit(solution)/shard_map/ppermute | solution.py:394

commit v5 on v4

--- a/solution.py
+++ b/solution.py
@@ -12,8 +12,8 @@
 rope_base = 1000000.0
 norm_eps = 1e-05
 masked_score = -1e30
-CACHE_STEPS = 4
-QUERY_ROWS = 256
+CACHE_STEPS = 8
+QUERY_ROWS = 512
 SIXTEENTHS = 8
 FLOPS_PER_US = 1.1e9
 VMEM_BYTES = 24 * 1024 * 1024

time: 50 us -> 50 us (level)
  waiting for transfers between devices: 16 us -> 18.1 us
  Pallas kernels: 8.88 us -> 7.18 us
    ppermute x17, waiting for transfers between devices: 16 us -> 18.1 us  [swap(): return lax.ppermute(x, axis, [(i, i ^ mask) for i in range(count)])]
    pallas_call x6, Pallas kernels: 8.88 us -> 7.18 us  [placed(): run(*[pltpu.with_memory_space_constraint(x, pltpu.HBM) if spec is HB else...]
  transfers between devices with their start and end apart: 17 -> 17, of which waited for: 8 -> 7; matrix products, arithmetic and copies ran while one was open for 4% -> 4% of each run, Pallas kernels for 13% -> 9%
where the time goes in v5:
time: 50 us; the launch traced here: 49.4 us
  starting transfers between devices  19.5 us (39%)
  waiting for transfers between devices  18.1 us (36%)
  Pallas kernels  7.18 us (14%)
  local copies, waits for them, and re-layouts  2.12 us (4%)
  other arithmetic  1.79 us (4%)
  between operations  0.79 us (2%)
    ppermute x17, starting transfers between devices, swap(): return lax.ppermute(x, axis, [(i, i ^ mask) for i in range(count)])  19.5 us
    ppermute x17, waiting for transfers between devices, swap(): return lax.ppermute(x, axis, [(i, i ^ mask) for i in range(count)])  18.1 us
    pallas_call x6, Pallas kernels, placed(): run(*[pltpu.with_memory_space_constraint(x, pltpu.HBM) if spec is HB else...  7.18 us
    unnamed x9, local copies, waits for them, and re-layouts  1.35 us
  transfers between devices with their start and end apart: 17, of which 7 were waited for; matrix products, arithmetic and copies ran while one was open for 4% of the time, Pallas kernels for 9%

profile of v5, /device:TPU:0, one launch (start us, length us, event | category | flops | bytes accessed | tf_op | source)
XLA Modules:
  0.0 49.4 jit_solution(8994081054057733697)
XLA Ops:
  0.6 1.3 %pack.1 = (bf16[640,256]{1,0:T(8,128)(2,1)S(1)}, bf16[640,256]{1,0:T(8,128)(2,1)S(1)}, bf16[128,256]{1,0:T(8,128)(2,1)S(1)}, bf16[128,256]{1,0:T(8,128)(2,1)S(1)}) custom-call(bf16[128,512]{1,0:T(8,128)(2,1)} %bitcast.13, bf16[256,512]{1,0:T(8,128)(2,1)} %wq_ref.1, bf16[256,128]{1,0:T(8,128)(2,1)} %wk_ref.1, bf16[256,128]{1,0:T(8,128)(2,1)} %wv_ref.1, ...), custom_call_target="tpu_custom_call" | custom-call | flops 1100000000 | bytes 65536 | tf_op jit(solution)/shard_map/pack/pallas_call | solution.py:41
  2.4 2.6 %collective-permute-start.1 = (bf16[640,256]{1,0:T(8,128)(2,1)S(1)}, bf16[640,256]{1,0:T(8,128)(2,1)S(1)}, u32[]{:S(2)}, u32[]{:S(2)}) collective-permute-start(bf16[640,256]{1,0:T(8,128)(2,1)S(1)} %get-tuple-element.43.refs_4_), channel_id=1, source_target_pairs={{0,8},{4,12},{8,0},{12,4},{16,24},{20,28},{24,16},{28,20},{1,9},{5... | collective-permute-start | bytes 983048 | tf_op jit(solution)/shard_map/ppermute | solution.py:394
  5.0 1.5 %collective-permute-start.2 = (bf16[640,256]{1,0:T(8,128)(2,1)S(1)}, bf16[640,256]{1,0:T(8,128)(2,1)S(1)}, u32[]{:S(2)}, u32[]{:S(2)}) collective-permute-start(bf16[640,256]{1,0:T(8,128)(2,1)S(1)} %get-tuple-element.40.refs_5_), channel_id=1, source_target_pairs={{0,16},{4,20},{8,24},{12,28},{16,0},{20,4},{24,8},{28,12},{1,17},{... | collective-permute-start | bytes 983048 | tf_op jit(solution)/shard_map/ppermute | solution.py:394
  7.1 2.6 %collective-permute-start.3 = (bf16[256,256]{1,0:T(8,128)(2,1)S(1)}, bf16[256,256]{1,0:T(8,128)(2,1)S(1)}, u32[]{:S(2)}, u32[]{:S(2)}) collective-permute-start(bf16[256,256]{1,0:T(8,128)(2,1)S(1)} %constant_dynamic-update-slice_fusion.refs_0_), channel_id=1, source_target_pairs={{0,2},{1,3},{2,0},{3,1},{4,6},{5,7},{6,4},{7,5},{8,10},{9,11},{10,... | collective-permute-start | bytes 393224 | tf_op jit(solution)/shard_map/ppermute | solution.py:394
  9.8 0.7 %copy-done.3 = s32[8]{0:T(128)S(1)} copy-done((s32[8]{0:T(128)S(1)}, s32[8]{0:T(128)}, u32[]{:S(2)}) %copy-start.3) | copy-done | bytes 56
  10.5 0.6 %dynamic_slice.3.length_ref = s32[1]{0:T(128)} dynamic-slice(s32[8]{0:T(128)S(1)} %copy-done.3, s32[]{:T(128)S(6)} %select_n.16), dynamic_slice_sizes={1} | dynamic-slice | bytes 12 | tf_op jit(solution)/shard_map/dynamic_slice | solution.py:411
  11.1 0.7 %add_convert_fusion.1 = f32[128]{0:T(128)S(1)} fusion(s32[]{:T(128)} %bitcast.4), kind=kLoop, calls=%fused_computation.8 | loop fusion | flops 256 | bytes 516 | tf_op jit(solution)/shard_map/convert_element_type | solution.py:386
  12.5 3.4 %collective-permute-done.3.refs_2_ = bf16[256,256]{1,0:T(8,128)(2,1)S(1)} collective-permute-done((bf16[256,256]{1,0:T(8,128)(2,1)S(1)}, bf16[256,256]{1,0:T(8,128)(2,1)S(1)}, u32[]{:S(2)}, u32[]{:S(2)}) %collective-permute-start.3) | collective-permute-done | bytes 131104 | tf_op jit(solution)/shard_map/ppermute | solution.py:394
  15.9 1.3 %collective-permute-start.4 = (bf16[256,256]{1,0:T(8,128)(2,1)S(1)}, bf16[256,256]{1,0:T(8,128)(2,1)S(1)}, u32[]{:S(2)}, u32[]{:S(2)}) collective-permute-start(bf16[256,256]{1,0:T(8,128)(2,1)S(1)} %constant_dynamic-update-slice_fusion.refs_0_), channel_id=1, source_target_pairs={{0,1},{1,0},{2,3},{3,2},{4,5},{5,4},{6,7},{7,6},{8,9},{9,8},{10,11... | collective-permute-start | bytes 393224 | tf_op jit(solution)/shard_map/ppermute | solution.py:394
  17.1 1.5 %collective-permute-start.8 = (bf16[640,256]{1,0:T(8,128)(2,1)S(1)}, bf16[640,256]{1,0:T(8,128)(2,1)S(1)}, u32[]{:S(2)}, u32[]{:S(2)}) collective-permute-start(bf16[640,256]{1,0:T(8,128)(2,1)S(1)} %collective-permute-done.1.refs_6_), channel_id=1, source_target_pairs={{0,16},{4,20},{8,24},{12,28},{16,0},{20,4},{24,8},{28,12},{1,17},{... | collective-permute-start | bytes 983048 | tf_op jit(solution)/shard_map/ppermute | solution.py:394
  19.2 1.4 %collective-permute-done.5.refs_7_ = bf16[640,256]{1,0:T(8,128)(2,1)S(1)} collective-permute-done((bf16[640,256]{1,0:T(8,128)(2,1)S(1)}, bf16[640,256]{1,0:T(8,128)(2,1)S(1)}, u32[]{:S(2)}, u32[]{:S(2)}) %collective-permute-start.5) | collective-permute-done | bytes 327712 | tf_op jit(solution)/shard_map/ppermute | solution.py:394
  20.6 2.0 %collective-permute-start.6 = (bf16[256,256]{1,0:T(8,128)(2,1)S(1)}, bf16[256,256]{1,0:T(8,128)(2,1)S(1)}, u32[]{:S(2)}, u32[]{:S(2)}) collective-permute-start(bf16[256,256]{1,0:T(8,128)(2,1)S(1)} %collective-permute-done.3.refs_2_), channel_id=1, source_target_pairs={{0,1},{1,0},{2,3},{3,2},{4,5},{5,4},{6,7},{7,6},{8,9},{9,8},{10,11... | collective-permute-start | bytes 393224 | tf_op jit(solution)/shard_map/ppermute | solution.py:394
  23.0 0.7 %copy-done.2 = bf16[2048]{0:T(1024)(128)(2,1)S(1)} copy-done((bf16[2048]{0:T(1024)(128)(2,1)S(1)}, bf16[2048]{0:T(1024)(128)(2,1)}, u32[]{:S(2)}) %copy-start.2) | copy-done | bytes 4120
  23.7 1.9 %collective-permute-done.6.refs_3_ = bf16[256,256]{1,0:T(8,128)(2,1)S(1)} collective-permute-done((bf16[256,256]{1,0:T(8,128)(2,1)S(1)}, bf16[256,256]{1,0:T(8,128)(2,1)S(1)}, u32[]{:S(2)}, u32[]{:S(2)}) %collective-permute-start.6) | collective-permute-done | bytes 131104 | tf_op jit(solution)/shard_map/ppermute | solution.py:394
  25.6 1.2 %near_products.1 = (f32[256,768]{1,0:T(8,128)S(1)}, bf16[256,256]{1,0:T(8,128)(2,1)S(1)}, f32[256,128]{1,0:T(8,128)S(1)}, bf16[3,512,256]{2,1,0:T(8,128)(2,1)S(1)}) custom-call(s32[3]{0:T(128)S(1)} %pad_add_fusion.place_ref, bf16[8,1,256]{2,1,0:T(2,128)(2,1)S(1)} %reshape.24.gain_ref, bf16[256,256]{1,0:T(8,128)(2,1)S(1)} %constant_dynamic-update-slice_fusion.refs_0_, ...), custom_call_target="tpu_custom_call" | custom-call | flops 110000000 | bytes 65536 | tf_op jit(solution)/shard_map/near_products/pallas_call | solution.py:41
  26.8 2.1 %collective-permute-done.8.top_ref.refs_0_ = bf16[640,256]{1,0:T(8,128)(2,1)S(1)} collective-permute-done((bf16[640,256]{1,0:T(8,128)(2,1)S(1)}, bf16[640,256]{1,0:T(8,128)(2,1)S(1)}, u32[]{:S(2)}, u32[]{:S(2)}) %collective-permute-start.8) | collective-permute-done | bytes 327712 | tf_op jit(solution)/shard_map/ppermute | solution.py:394
  31.0 2.4 %attention.1 = (bf16[128,512]{1,0:T(8,128)(2,1)S(1)}, bf16[128,128]{1,0:T(8,128)(2,1)}, bf16[128,128]{1,0:T(8,128)(2,1)}) custom-call(s32[1]{0:T(128)} %dynamic_slice.3.length_ref, f32[128,128]{1,0:T(8,128)S(1)} %get-tuple-element.45.cos_ref, f32[128,128]{1,0:T(8,128)S(1)} %get-tuple-element.46.sin_ref, f32[128,896]{1,0:T(8,128)S(1)} %get-tuple-element.50.here_ref, ...), custom_call_target="tpu_custom_call" | custom-call | flops 4400000000 | bytes 65536 | tf_op jit(solution)/shard_map/attention/pallas_call | solution.py:41
  33.4 1.0 %project.2 = (bf16[128,512]{1,0:T(8,128)(2,1)S(1)}, bf16[128,512]{1,0:T(8,128)(2,1)S(1)}) custom-call(s32[3]{0:T(128)S(1)} %pad_add_fusion.place_ref, bf16[128,512]{1,0:T(8,128)(2,1)S(1)} %get-tuple-element.58.mixed_ref, bf16[3,512,256]{2,1,0:T(8,128)(2,1)S(1)} %get-tuple-element.55.own_ref, bf16[3,512,256]{2,1,0:T(8,128)(2,1)S(1)} %collective-permute-done.11.sibling_ref, ...), custom_call_target="tpu_custom_call" | custom-call | flops 1100000000 | bytes 65536 | tf_op jit(solution)/shard_map/project/pallas_call | solution.py:41
  34.5 2.6 %collective-permute-start.16 = (bf16[128,512]{1,0:T(8,128)(2,1)S(1)}, bf16[128,512]{1,0:T(8,128)(2,1)S(1)}, u32[]{:S(2)}, u32[]{:S(2)}) collective-permute-start(bf16[128,512]{1,0:T(8,128)(2,1)S(1)} %get-tuple-element.62), channel_id=1, source_target_pairs={{0,2},{1,3},{2,0},{3,1},{4,6},{5,7},{6,4},{7,5},{8,10},{9,11},{10,... | collective-permute-start | bytes 393224 | tf_op jit(solution)/shard_map/ppermute | solution.py:394
  37.1 1.0 %project.3 = (bf16[128,512]{1,0:T(8,128)(2,1)S(1)}, bf16[128,512]{1,0:T(8,128)(2,1)S(1)}) custom-call(s32[3]{0:T(128)S(1)} %pad_add_fusion.place_ref, bf16[128,512]{1,0:T(8,128)(2,1)S(1)} %get-tuple-element.58.mixed_ref, bf16[3,512,256]{2,1,0:T(8,128)(2,1)S(1)} %get-tuple-element.55.own_ref, bf16[3,512,256]{2,1,0:T(8,128)(2,1)S(1)} %collective-permute-done.11.sibling_ref, ...), custom_call_target="tpu_custom_call" | custom-call | flops 1100000000 | bytes 65536 | tf_op jit(solution)/shard_map/project/pallas_call | solution.py:41
  38.2 1.6 %collective-permute-start.15 = (bf16[128,512]{1,0:T(8,128)(2,1)S(1)}, bf16[128,512]{1,0:T(8,128)(2,1)S(1)}, u32[]{:S(2)}, u32[]{:S(2)}) collective-permute-start(bf16[128,512]{1,0:T(8,128)(2,1)S(1)} %get-tuple-element.61), channel_id=1, source_target_pairs={{0,1},{1,0},{2,3},{3,2},{4,5},{5,4},{6,7},{7,6},{8,9},{9,8},{10,11... | collective-permute-start | bytes 393224 | tf_op jit(solution)/shard_map/ppermute | solution.py:394
  40.0 3.5 %collective-permute-done.16 = bf16[128,512]{1,0:T(8,128)(2,1)S(1)} collective-permute-done((bf16[128,512]{1,0:T(8,128)(2,1)S(1)}, bf16[128,512]{1,0:T(8,128)(2,1)S(1)}, u32[]{:S(2)}, u32[]{:S(2)}) %collective-permute-start.16) | collective-permute-done | bytes 131104 | tf_op jit(solution)/shard_map/ppermute | solution.py:394
  43.5 5.2 %collective-permute-done.15 = bf16[128,512]{1,0:T(8,128)(2,1)S(1)} collective-permute-done((bf16[128,512]{1,0:T(8,128)(2,1)S(1)}, bf16[128,512]{1,0:T(8,128)(2,1)S(1)}, u32[]{:S(2)}, u32[]{:S(2)}) %collective-permute-start.15) | collective-permute-done | bytes 131104 | tf_op jit(solution)/shard_map/ppermute | solution.py:394
  48.7 0.7 %fusion = bf16[1,128,512]{2,1,0:T(8,128)(2,1)} fusion(bf16[128,512]{1,0:T(8,128)(2,1)S(1)} %collective-permute-done.16, bf16[128,512]{1,0:T(8,128)(2,1)S(1)} %collective-permute-done.15, bf16[128,512]{1,0:T(8,128)(2,1)S(1)} %collective-permute-done.14, bf16[128,512]{1,0:T(8,128)(2,1)S(1)} %get-tuple-element.59), kind=kLoop, calls=%fused_computation.1 | loop fusion | flops 524288 | bytes 655360 | tf_op jit(solution)/shard_map/broadcast_in_dim | solution.py:458
  (37 shorter events, 5.2 us)
Async XLA Ops:
  1.9 4.6 %collective-permute-start = (bf16[128,256]{1,0:T(8,128)(2,1)S(1)}, bf16[128,256]{1,0:T(8,128)(2,1)S(1)}, u32[]{:S(2)}, u32[]{:S(2)}) collective-permute-start(bf16[128,256]{1,0:T(8,128)(2,1)S(1)} %get-tuple-element.35), channel_id=1, source_target_pairs={{0,4},{4,0},{8,12},{12,8},{16,20},{20,16},{24,28},{28,24},{1,5},{5... | collective-permute-start | bytes 196616 | tf_op jit(solution)/shard_map/ppermute | solution.py:394
  2.4 13.4 %collective-permute-start.1 = (bf16[640,256]{1,0:T(8,128)(2,1)S(1)}, bf16[640,256]{1,0:T(8,128)(2,1)S(1)}, u32[]{:S(2)}, u32[]{:S(2)}) collective-permute-start(bf16[640,256]{1,0:T(8,128)(2,1)S(1)} %get-tuple-element.43.refs_4_), channel_id=1, source_target_pairs={{0,8},{4,12},{8,0},{12,4},{16,24},{20,28},{24,16},{28,20},{1,9},{5... | collective-permute-start | bytes 983048 | tf_op jit(solution)/shard_map/ppermute | solution.py:394
  5.0 10.9 %collective-permute-start.2 = (bf16[640,256]{1,0:T(8,128)(2,1)S(1)}, bf16[640,256]{1,0:T(8,128)(2,1)S(1)}, u32[]{:S(2)}, u32[]{:S(2)}) collective-permute-start(bf16[640,256]{1,0:T(8,128)(2,1)S(1)} %get-tuple-element.40.refs_5_), channel_id=1, source_target_pairs={{0,16},{4,20},{8,24},{12,28},{16,0},{20,4},{24,8},{28,12},{1,17},{... | collective-permute-start | bytes 983048 | tf_op jit(solution)/shard_map/ppermute | solution.py:394
  6.5 14.1 %collective-permute-start.5 = (bf16[640,256]{1,0:T(8,128)(2,1)S(1)}, bf16[640,256]{1,0:T(8,128)(2,1)S(1)}, u32[]{:S(2)}, u32[]{:S(2)}) collective-permute-start(bf16[640,256]{1,0:T(8,128)(2,1)S(1)} %get-tuple-element.40.refs_5_), channel_id=1, source_target_pairs={{0,8},{4,12},{8,0},{12,4},{16,24},{20,28},{24,16},{28,20},{1,9},{5... | collective-permute-start | bytes 983048 | tf_op jit(solution)/shard_map/ppermute | solution.py:394
  7.1 8.7 %collective-permute-start.3 = (bf16[256,256]{1,0:T(8,128)(2,1)S(1)}, bf16[256,256]{1,0:T(8,128)(2,1)S(1)}, u32[]{:S(2)}, u32[]{:S(2)}) collective-permute-start(bf16[256,256]{1,0:T(8,128)(2,1)S(1)} %constant_dynamic-update-slice_fusion.refs_0_), channel_id=1, source_target_pairs={{0,2},{1,3},{2,0},{3,1},{4,6},{5,7},{6,4},{7,5},{8,10},{9,11},{10,... | collective-permute-start | bytes 393224 | tf_op jit(solution)/shard_map/ppermute | solution.py:394
  9.8 0.7 %copy-start.3 = (s32[8]{0:T(128)S(1)}, s32[8]{0:T(128)}, u32[]{:S(2)}) copy-start(s32[8]{0:T(128)} %param.17) | copy-start | bytes 100
  11.8 11.9 %collective-permute-start.7 = (bf16[640,256]{1,0:T(8,128)(2,1)S(1)}, bf16[640,256]{1,0:T(8,128)(2,1)S(1)}, u32[]{:S(2)}, u32[]{:S(2)}) collective-permute-start(bf16[640,256]{1,0:T(8,128)(2,1)S(1)} %get-tuple-element.43.refs_4_), channel_id=1, source_target_pairs={{0,16},{4,20},{8,24},{12,28},{16,0},{20,4},{24,8},{28,12},{1,17},{... | collective-permute-start | bytes 983048 | tf_op jit(solution)/shard_map/ppermute | solution.py:394
  15.9 7.9 %collective-permute-start.4 = (bf16[256,256]{1,0:T(8,128)(2,1)S(1)}, bf16[256,256]{1,0:T(8,128)(2,1)S(1)}, u32[]{:S(2)}, u32[]{:S(2)}) collective-permute-start(bf16[256,256]{1,0:T(8,128)(2,1)S(1)} %constant_dynamic-update-slice_fusion.refs_0_), channel_id=1, source_target_pairs={{0,1},{1,0},{2,3},{3,2},{4,5},{5,4},{6,7},{7,6},{8,9},{9,8},{10,11... | collective-permute-start | bytes 393224 | tf_op jit(solution)/shard_map/ppermute | solution.py:394
  17.1 11.7 %collective-permute-start.8 = (bf16[640,256]{1,0:T(8,128)(2,1)S(1)}, bf16[640,256]{1,0:T(8,128)(2,1)S(1)}, u32[]{:S(2)}, u32[]{:S(2)}) collective-permute-start(bf16[640,256]{1,0:T(8,128)(2,1)S(1)} %collective-permute-done.1.refs_6_), channel_id=1, source_target_pairs={{0,16},{4,20},{8,24},{12,28},{16,0},{20,4},{24,8},{28,12},{1,17},{... | collective-permute-start | bytes 983048 | tf_op jit(solution)/shard_map/ppermute | solution.py:394
  18.7 10.2 %collective-permute-start.9 = (bf16[640,256]{1,0:T(8,128)(2,1)S(1)}, bf16[640,256]{1,0:T(8,128)(2,1)S(1)}, u32[]{:S(2)}, u32[]{:S(2)}) collective-permute-start(bf16[640,256]{1,0:T(8,128)(2,1)S(1)} %collective-permute-done.2.refs_9_), channel_id=1, source_target_pairs={{0,8},{4,12},{8,0},{12,4},{16,24},{20,28},{24,16},{28,20},{1,9},{5... | collective-permute-start | bytes 983048 | tf_op jit(solution)/shard_map/ppermute | solution.py:394
  20.6 5.0 %collective-permute-start.6 = (bf16[256,256]{1,0:T(8,128)(2,1)S(1)}, bf16[256,256]{1,0:T(8,128)(2,1)S(1)}, u32[]{:S(2)}, u32[]{:S(2)}) collective-permute-start(bf16[256,256]{1,0:T(8,128)(2,1)S(1)} %collective-permute-done.3.refs_2_), channel_id=1, source_target_pairs={{0,1},{1,0},{2,3},{3,2},{4,5},{5,4},{6,7},{7,6},{8,9},{9,8},{10,11... | collective-permute-start | bytes 393224 | tf_op jit(solution)/shard_map/ppermute | solution.py:394
  23.0 0.7 %copy-start.2 = (bf16[2048]{0:T(1024)(128)(2,1)S(1)}, bf16[2048]{0:T(1024)(128)(2,1)}, u32[]{:S(2)}) copy-start(bf16[2048]{0:T(1024)(128)(2,1)} %param.10) | copy-start | bytes 12292
  28.8 2.2 %copy-start.1 = (bf16[1,2048,128]{2,1,0:T(8,128)(2,1)S(1)}, bf16[1,2048,128]{2,1,0:T(8,128)(2,1)}, u32[]{:S(2)}) copy-start(bf16[1,2048,128]{2,1,0:T(8,128)(2,1)} %param.16) | copy-start | bytes 1572868
  29.1 1.9 %copy-start = (bf16[1,2048,128]{2,1,0:T(8,128)(2,1)S(1)}, bf16[1,2048,128]{2,1,0:T(8,128)(2,1)}, u32[]{:S(2)}) copy-start(bf16[1,2048,128]{2,1,0:T(8,128)(2,1)} %param.15) | copy-start | bytes 1572868
  29.1 1.9 %collective-permute-start.10 = (f32[128,896]{1,0:T(8,128)S(1)}, f32[128,896]{1,0:T(8,128)S(1)}, u32[]{:S(2)}, u32[]{:S(2)}) collective-permute-start(f32[128,896]{1,0:T(8,128)S(1)} %get-tuple-element.53), channel_id=1, source_target_pairs={{0,4},{4,0},{8,12},{12,8},{16,20},{20,16},{24,28},{28,24},{1,5},{5... | collective-permute-start | bytes 1376264 | tf_op jit(solution)/shard_map/ppermute | solution.py:394
  29.2 4.2 %collective-permute-start.11 = (bf16[3,512,256]{2,1,0:T(8,128)(2,1)S(1)}, bf16[3,512,256]{2,1,0:T(8,128)(2,1)S(1)}, u32[]{:S(2)}, u32[]{:S(2)}) collective-permute-start(bf16[3,512,256]{2,1,0:T(8,128)(2,1)S(1)} %get-tuple-element.55.own_ref), channel_id=1, source_target_pairs={{0,4},{4,0},{8,12},{12,8},{16,20},{20,16},{24,28},{28,24},{1,5},{5... | collective-permute-start | bytes 2359304 | tf_op jit(solution)/shard_map/ppermute | solution.py:394
  29.7 3.7 %collective-permute-start.12 = (bf16[256,256]{1,0:T(8,128)(2,1)S(1)}, bf16[256,256]{1,0:T(8,128)(2,1)S(1)}, u32[]{:S(2)}, u32[]{:S(2)}) collective-permute-start(bf16[256,256]{1,0:T(8,128)(2,1)S(1)} %slice.8), channel_id=1, source_target_pairs={{0,4},{4,0},{8,12},{12,8},{16,20},{20,16},{24,28},{28,24},{1,5},{5... | collective-permute-start | bytes 393224 | tf_op jit(solution)/shard_map/ppermute | solution.py:394
  29.9 3.5 %collective-permute-start.13 = (bf16[256,256]{1,0:T(8,128)(2,1)S(1)}, bf16[256,256]{1,0:T(8,128)(2,1)S(1)}, u32[]{:S(2)}, u32[]{:S(2)}) collective-permute-start(bf16[256,256]{1,0:T(8,128)(2,1)S(1)} %slice.9), channel_id=1, source_target_pairs={{0,4},{4,0},{8,12},{12,8},{16,20},{20,16},{24,28},{28,24},{1,5},{5... | collective-permute-start | bytes 393224 | tf_op jit(solution)/shard_map/ppermute | solution.py:394
  34.5 9.0 %collective-permute-start.16 = (bf16[128,512]{1,0:T(8,128)(2,1)S(1)}, bf16[128,512]{1,0:T(8,128)(2,1)S(1)}, u32[]{:S(2)}, u32[]{:S(2)}) collective-permute-start(bf16[128,512]{1,0:T(8,128)(2,1)S(1)} %get-tuple-element.62), channel_id=1, source_target_pairs={{0,2},{1,3},{2,0},{3,1},{4,6},{5,7},{6,4},{7,5},{8,10},{9,11},{10,... | collective-permute-start | bytes 393224 | tf_op jit(solution)/shard_map/ppermute | solution.py:394
  38.2 10.5 %collective-permute-start.15 = (bf16[128,512]{1,0:T(8,128)(2,1)S(1)}, bf16[128,512]{1,0:T(8,128)(2,1)S(1)}, u32[]{:S(2)}, u32[]{:S(2)}) collective-permute-start(bf16[128,512]{1,0:T(8,128)(2,1)S(1)} %get-tuple-element.61), channel_id=1, source_target_pairs={{0,1},{1,0},{2,3},{3,2},{4,5},{5,4},{6,7},{7,6},{8,9},{9,8},{10,11... | collective-permute-start | bytes 393224 | tf_op jit(solution)/shard_map/ppermute | solution.py:394
  39.8 8.9 %collective-permute-start.14 = (bf16[128,512]{1,0:T(8,128)(2,1)S(1)}, bf16[128,512]{1,0:T(8,128)(2,1)S(1)}, u32[]{:S(2)}, u32[]{:S(2)}) collective-permute-start(bf16[128,512]{1,0:T(8,128)(2,1)S(1)} %get-tuple-element.60), channel_id=1, source_target_pairs={{0,3},{1,2},{2,1},{3,0},{4,7},{5,6},{6,5},{7,4},{8,11},{9,10},{10,... | collective-permute-start | bytes 393224 | tf_op jit(solution)/shard_map/ppermute | solution.py:394

commit v6 on v5

--- a/solution.py
+++ b/solution.py
@@ -167,25 +167,23 @@
     )(place, gain.reshape(2 * shards, 1, width), *columns, *weights)
 
 
-def far_kernel(partial_ref, last_ref, square_ref, top_ref, bottom_ref, keep_out, send_out):
+def far_kernel(partial_ref, last_ref, top_ref, bottom_ref, keep_out, send_out):
     total = partial_ref[...] + product(last_ref[...], top_ref, bottom_ref)
     tokens = keep_out.shape[0]
-    width = total.shape[1]
     for out, first in ((keep_out, 0), (send_out, tokens)):
-        out[:, :width] = total[first : first + tokens]
-        out[:, width:] = square_ref[first : first + tokens, :]
-
-
-def far_products(partial, last, square, top, bottom):
+        out[...] = total[first : first + tokens]
+
+
+def far_products(partial, last, top, bottom):
     rows, width = partial.shape
-    out = like((rows // 2, width + 128), jnp.float32)
+    out = like((rows // 2, width), jnp.float32)
     return call(
         far_kernel,
         (out, out),
-        [VM] * 5,
+        [VM] * 4,
         busy=0.1,
         name="far_products",
-    )(partial, last, square, top, bottom)
+    )(partial, last, top, bottom)
 
 
 def rotate(rows, cosine, sine):
@@ -276,6 +274,8 @@
     sin_ref,
     here_ref,
     there_ref,
+    square_here_ref,
+    square_there_ref,
     k_ref,
     v_ref,
     out_ref,
@@ -288,9 +288,10 @@
 ):
     length = length_ref[0]
     total = here_ref[...] + there_ref[...]
-    width = total.shape[1] - 128
-    scale = lax.rsqrt(total[:, width:] / features + norm_eps)
-    total = total[:, :width] * jnp.tile(scale, (1, width // 128))
+    width = total.shape[1]
+    square = square_here_ref[: total.shape[0]] + square_there_ref[...]
+    scale = lax.rsqrt(square / features + norm_eps)
+    total = total * jnp.tile(scale, (1, width // 128))
     tokens = total.shape[0]
     q_width = width - 2 * kv_width
     cosine, sine = cos_ref[...], sin_ref[...]
@@ -321,16 +322,16 @@
         copy.wait()
 
 
-def attention(length, features, cosine, sine, here, there, keys, values):
+def attention(length, features, cosine, sine, here, there, square, square_there, keys, values):
     tokens = here.shape[0]
     kv_width = keys.shape[1]
-    q_width = here.shape[1] - 128 - 2 * kv_width
+    q_width = here.shape[1] - 2 * kv_width
     queries = q_width // HD * tokens
     fresh = like((tokens, kv_width))
     return call(
         functools.partial(attention_kernel, features, kv_width),
         (like((tokens, q_width)), fresh, fresh),
-        [SM, VM, VM, VM, VM, VM, VM],
+        [SM] + [VM] * 8,
         out_specs=(VM, HB, HB),
         scratch=[
             pltpu.VMEM(fresh.shape, jnp.bfloat16),
@@ -340,7 +341,7 @@
         ],
         busy=4.0,
         name="attention",
-    )(length, cosine, sine, here, there, keys, values)
+    )(length, cosine, sine, here, there, square, square_there, keys, values)
 
 
 def out_kernel(distances, chips, place_ref, mixed_ref, own_ref, sibling_ref, *refs):
@@ -432,7 +433,7 @@
     )
     cosine, sine = phases(length[0], tokens)
     partial, cosine, sine = lax.optimization_barrier((partial, cosine, sine))
-    here, there = far_products(partial, last, square, d_top, d_bottom)
+    here, there = far_products(partial, last, d_top, d_bottom)
     there, o_near = lax.optimization_barrier((there, o_near))
     mixed, new_keys, new_values = attention(
         length,
@@ -441,6 +442,8 @@
         sine,
         here,
         core(there),
+        square,
+        core(square[tokens:]),
         cache_keys[0],
         cache_values[0],
     )

time: 50 us -> 51.3 us (1.026)
  Pallas kernels: 7.18 us -> 7.88 us
  waiting for transfers between devices: 18.1 us -> 18.8 us
    ppermute x17 -> x18, waiting for transfers between devices: 18.1 us -> 18.8 us  [swap(): return lax.ppermute(x, axis, [(i, i ^ mask) for i in range(count)])]
    pallas_call x6, Pallas kernels: 7.18 us -> 7.88 us  [placed(): run(*[pltpu.with_memory_space_constraint(x, pltpu.HBM) if spec is HB else...]
    ppermute x17 -> x18, starting transfers between devices: 19.5 us -> 19.6 us  [swap(): return lax.ppermute(x, axis, [(i, i ^ mask) for i in range(count)])]
  transfers between devices with their start and end apart: 17 -> 18, of which waited for: 7 -> 7; matrix products, arithmetic and copies ran while one was open for 4% -> 4% of each run, Pallas kernels for 9% -> 10%
where the time goes in v6:
time: 51.3 us; the launch traced here: 51 us
  starting transfers between devices  19.6 us (38%)
  waiting for transfers between devices  18.8 us (37%)
  Pallas kernels  7.88 us (15%)
  local copies, waits for them, and re-layouts  2.15 us (4%)
  other arithmetic  1.8 us (4%)
  between operations  0.79 us (2%)
    ppermute x18, starting transfers between devices, swap(): return lax.ppermute(x, axis, [(i, i ^ mask) for i in range(count)])  19.6 us
    ppermute x18, waiting for transfers between devices, swap(): return lax.ppermute(x, axis, [(i, i ^ mask) for i in range(count)])  18.8 us
    pallas_call x6, Pallas kernels, placed(): run(*[pltpu.with_memory_space_constraint(x, pltpu.HBM) if spec is HB else...  7.88 us
    unnamed x9, local copies, waits for them, and re-layouts  1.35 us
  transfers between devices with their start and end apart: 18, of which 7 were waited for; matrix products, arithmetic and copies ran while one was open for 4% of the time, Pallas kernels for 10%

profile of v6, /device:TPU:0, one launch (start us, length us, event | category | flops | bytes accessed | tf_op | source)
XLA Modules:
  0.0 51.0 jit_solution(6063705491332434512)
XLA Ops:
  0.6 1.3 %pack.1 = (bf16[640,256]{1,0:T(8,128)(2,1)S(1)}, bf16[640,256]{1,0:T(8,128)(2,1)S(1)}, bf16[128,256]{1,0:T(8,128)(2,1)S(1)}, bf16[128,256]{1,0:T(8,128)(2,1)S(1)}) custom-call(bf16[128,512]{1,0:T(8,128)(2,1)} %bitcast.13, bf16[256,512]{1,0:T(8,128)(2,1)} %wq_ref.1, bf16[256,128]{1,0:T(8,128)(2,1)} %wk_ref.1, bf16[256,128]{1,0:T(8,128)(2,1)} %wv_ref.1, ...), custom_call_target="tpu_custom_call" | custom-call | flops 1100000000 | bytes 65536 | tf_op jit(solution)/shard_map/pack/pallas_call | solution.py:41
  2.4 2.6 %collective-permute-start.1 = (bf16[640,256]{1,0:T(8,128)(2,1)S(1)}, bf16[640,256]{1,0:T(8,128)(2,1)S(1)}, u32[]{:S(2)}, u32[]{:S(2)}) collective-permute-start(bf16[640,256]{1,0:T(8,128)(2,1)S(1)} %get-tuple-element.43.refs_4_), channel_id=1, source_target_pairs={{0,8},{4,12},{8,0},{12,4},{16,24},{20,28},{24,16},{28,20},{1,9},{5... | collective-permute-start | bytes 983048 | tf_op jit(solution)/shard_map/ppermute | solution.py:395
  5.0 1.5 %collective-permute-start.2 = (bf16[640,256]{1,0:T(8,128)(2,1)S(1)}, bf16[640,256]{1,0:T(8,128)(2,1)S(1)}, u32[]{:S(2)}, u32[]{:S(2)}) collective-permute-start(bf16[640,256]{1,0:T(8,128)(2,1)S(1)} %get-tuple-element.40.refs_5_), channel_id=1, source_target_pairs={{0,16},{4,20},{8,24},{12,28},{16,0},{20,4},{24,8},{28,12},{1,17},{... | collective-permute-start | bytes 983048 | tf_op jit(solution)/shard_map/ppermute | solution.py:395
  7.1 2.6 %collective-permute-start.3 = (bf16[256,256]{1,0:T(8,128)(2,1)S(1)}, bf16[256,256]{1,0:T(8,128)(2,1)S(1)}, u32[]{:S(2)}, u32[]{:S(2)}) collective-permute-start(bf16[256,256]{1,0:T(8,128)(2,1)S(1)} %constant_dynamic-update-slice_fusion.refs_0_), channel_id=1, source_target_pairs={{0,2},{1,3},{2,0},{3,1},{4,6},{5,7},{6,4},{7,5},{8,10},{9,11},{10,... | collective-permute-start | bytes 393224 | tf_op jit(solution)/shard_map/ppermute | solution.py:395
  10.5 0.7 %dynamic_slice.3.length_ref = s32[1]{0:T(128)} dynamic-slice(s32[8]{0:T(128)S(1)} %copy-done.3, s32[]{:T(128)S(6)} %select_n.16), dynamic_slice_sizes={1} | dynamic-slice | bytes 12 | tf_op jit(solution)/shard_map/dynamic_slice | solution.py:412
  11.2 0.7 %add_convert_fusion.1 = f32[128]{0:T(128)S(1)} fusion(s32[]{:T(128)} %bitcast.4), kind=kLoop, calls=%fused_computation.8 | loop fusion | flops 256 | bytes 516 | tf_op jit(solution)/shard_map/convert_element_type | solution.py:387
  12.5 3.4 %collective-permute-done.3.refs_2_ = bf16[256,256]{1,0:T(8,128)(2,1)S(1)} collective-permute-done((bf16[256,256]{1,0:T(8,128)(2,1)S(1)}, bf16[256,256]{1,0:T(8,128)(2,1)S(1)}, u32[]{:S(2)}, u32[]{:S(2)}) %collective-permute-start.3) | collective-permute-done | bytes 131104 | tf_op jit(solution)/shard_map/ppermute | solution.py:395
  15.9 1.3 %collective-permute-start.4 = (bf16[256,256]{1,0:T(8,128)(2,1)S(1)}, bf16[256,256]{1,0:T(8,128)(2,1)S(1)}, u32[]{:S(2)}, u32[]{:S(2)}) collective-permute-start(bf16[256,256]{1,0:T(8,128)(2,1)S(1)} %constant_dynamic-update-slice_fusion.refs_0_), channel_id=1, source_target_pairs={{0,1},{1,0},{2,3},{3,2},{4,5},{5,4},{6,7},{7,6},{8,9},{9,8},{10,11... | collective-permute-start | bytes 393224 | tf_op jit(solution)/shard_map/ppermute | solution.py:395
  17.1 1.5 %collective-permute-start.8 = (bf16[640,256]{1,0:T(8,128)(2,1)S(1)}, bf16[640,256]{1,0:T(8,128)(2,1)S(1)}, u32[]{:S(2)}, u32[]{:S(2)}) collective-permute-start(bf16[640,256]{1,0:T(8,128)(2,1)S(1)} %collective-permute-done.1.refs_6_), channel_id=1, source_target_pairs={{0,16},{4,20},{8,24},{12,28},{16,0},{20,4},{24,8},{28,12},{1,17},{... | collective-permute-start | bytes 983048 | tf_op jit(solution)/shard_map/ppermute | solution.py:395
  19.2 1.4 %collective-permute-done.5.refs_7_ = bf16[640,256]{1,0:T(8,128)(2,1)S(1)} collective-permute-done((bf16[640,256]{1,0:T(8,128)(2,1)S(1)}, bf16[640,256]{1,0:T(8,128)(2,1)S(1)}, u32[]{:S(2)}, u32[]{:S(2)}) %collective-permute-start.5) | collective-permute-done | bytes 327712 | tf_op jit(solution)/shard_map/ppermute | solution.py:395
  20.6 2.0 %collective-permute-start.6 = (bf16[256,256]{1,0:T(8,128)(2,1)S(1)}, bf16[256,256]{1,0:T(8,128)(2,1)S(1)}, u32[]{:S(2)}, u32[]{:S(2)}) collective-permute-start(bf16[256,256]{1,0:T(8,128)(2,1)S(1)} %collective-permute-done.3.refs_2_), channel_id=1, source_target_pairs={{0,1},{1,0},{2,3},{3,2},{4,5},{5,4},{6,7},{7,6},{8,9},{9,8},{10,11... | collective-permute-start | bytes 393224 | tf_op jit(solution)/shard_map/ppermute | solution.py:395
  23.0 0.7 %copy-done.2 = bf16[2048]{0:T(1024)(128)(2,1)S(1)} copy-done((bf16[2048]{0:T(1024)(128)(2,1)S(1)}, bf16[2048]{0:T(1024)(128)(2,1)}, u32[]{:S(2)}) %copy-start.2) | copy-done | bytes 4120
  23.7 1.9 %collective-permute-done.6.refs_3_ = bf16[256,256]{1,0:T(8,128)(2,1)S(1)} collective-permute-done((bf16[256,256]{1,0:T(8,128)(2,1)S(1)}, bf16[256,256]{1,0:T(8,128)(2,1)S(1)}, u32[]{:S(2)}, u32[]{:S(2)}) %collective-permute-start.6) | collective-permute-done | bytes 131104 | tf_op jit(solution)/shard_map/ppermute | solution.py:395
  25.6 1.2 %near_products.1 = (f32[256,768]{1,0:T(8,128)S(1)}, bf16[256,256]{1,0:T(8,128)(2,1)S(1)}, f32[256,128]{1,0:T(8,128)S(1)}, bf16[3,512,256]{2,1,0:T(8,128)(2,1)S(1)}) custom-call(s32[3]{0:T(128)S(1)} %pad_add_fusion.place_ref, bf16[8,1,256]{2,1,0:T(2,128)(2,1)S(1)} %reshape.24.gain_ref, bf16[256,256]{1,0:T(8,128)(2,1)S(1)} %constant_dynamic-update-slice_fusion.refs_0_, ...), custom_call_target="tpu_custom_call" | custom-call | flops 110000000 | bytes 65536 | tf_op jit(solution)/shard_map/near_products/pallas_call | solution.py:41
  26.8 2.1 %collective-permute-done.8.top_ref.refs_0_ = bf16[640,256]{1,0:T(8,128)(2,1)S(1)} collective-permute-done((bf16[640,256]{1,0:T(8,128)(2,1)S(1)}, bf16[640,256]{1,0:T(8,128)(2,1)S(1)}, u32[]{:S(2)}, u32[]{:S(2)}) %collective-permute-start.8) | collective-permute-done | bytes 327712 | tf_op jit(solution)/shard_map/ppermute | solution.py:395
  30.5 1.7 %collective-permute-done.11.square_there_ref = f32[128,128]{1,0:T(8,128)S(1)} collective-permute-done((f32[128,128]{1,0:T(8,128)S(1)}, f32[128,128]{1,0:T(8,128)S(1)}, u32[]{:S(2)}, u32[]{:S(2)}) %collective-permute-start.11) | collective-permute-done | bytes 65568 | tf_op jit(solution)/shard_map/ppermute | solution.py:395
  32.2 3.1 %attention.1 = (bf16[128,512]{1,0:T(8,128)(2,1)S(1)}, bf16[128,128]{1,0:T(8,128)(2,1)}, bf16[128,128]{1,0:T(8,128)(2,1)}) custom-call(s32[1]{0:T(128)} %dynamic_slice.3.length_ref, f32[128,128]{1,0:T(8,128)S(1)} %get-tuple-element.45.cos_ref, f32[128,128]{1,0:T(8,128)S(1)} %get-tuple-element.46.sin_ref, f32[128,768]{1,0:T(8,128)S(1)} %get-tuple-element.49.here_ref, ...), custom_call_target="tpu_custom_call" | custom-call | flops 4400000000 | bytes 65536 | tf_op jit(solution)/shard_map/attention/pallas_call | solution.py:41
  35.3 1.0 %project.2 = (bf16[128,512]{1,0:T(8,128)(2,1)S(1)}, bf16[128,512]{1,0:T(8,128)(2,1)S(1)}) custom-call(s32[3]{0:T(128)S(1)} %pad_add_fusion.place_ref, bf16[128,512]{1,0:T(8,128)(2,1)S(1)} %get-tuple-element.58.mixed_ref, bf16[3,512,256]{2,1,0:T(8,128)(2,1)S(1)} %get-tuple-element.55.own_ref, bf16[3,512,256]{2,1,0:T(8,128)(2,1)S(1)} %collective-permute-done.12.sibling_ref, ...), custom_call_target="tpu_custom_call" | custom-call | flops 1100000000 | bytes 65536 | tf_op jit(solution)/shard_map/project/pallas_call | solution.py:41
  36.3 2.7 %collective-permute-start.17 = (bf16[128,512]{1,0:T(8,128)(2,1)S(1)}, bf16[128,512]{1,0:T(8,128)(2,1)S(1)}, u32[]{:S(2)}, u32[]{:S(2)}) collective-permute-start(bf16[128,512]{1,0:T(8,128)(2,1)S(1)} %get-tuple-element.62), channel_id=1, source_target_pairs={{0,2},{1,3},{2,0},{3,1},{4,6},{5,7},{6,4},{7,5},{8,10},{9,11},{10,... | collective-permute-start | bytes 393224 | tf_op jit(solution)/shard_map/ppermute | solution.py:395
  39.0 1.0 %project.3 = (bf16[128,512]{1,0:T(8,128)(2,1)S(1)}, bf16[128,512]{1,0:T(8,128)(2,1)S(1)}) custom-call(s32[3]{0:T(128)S(1)} %pad_add_fusion.place_ref, bf16[128,512]{1,0:T(8,128)(2,1)S(1)} %get-tuple-element.58.mixed_ref, bf16[3,512,256]{2,1,0:T(8,128)(2,1)S(1)} %get-tuple-element.55.own_ref, bf16[3,512,256]{2,1,0:T(8,128)(2,1)S(1)} %collective-permute-done.12.sibling_ref, ...), custom_call_target="tpu_custom_call" | custom-call | flops 1100000000 | bytes 65536 | tf_op jit(solution)/shard_map/project/pallas_call | solution.py:41
  40.0 1.6 %collective-permute-start.16 = (bf16[128,512]{1,0:T(8,128)(2,1)S(1)}, bf16[128,512]{1,0:T(8,128)(2,1)S(1)}, u32[]{:S(2)}, u32[]{:S(2)}) collective-permute-start(bf16[128,512]{1,0:T(8,128)(2,1)S(1)} %get-tuple-element.61), channel_id=1, source_target_pairs={{0,1},{1,0},{2,3},{3,2},{4,5},{5,4},{6,7},{7,6},{8,9},{9,8},{10,11... | collective-permute-start | bytes 393224 | tf_op jit(solution)/shard_map/ppermute | solution.py:395
  41.9 4.5 %collective-permute-done.17 = bf16[128,512]{1,0:T(8,128)(2,1)S(1)} collective-permute-done((bf16[128,512]{1,0:T(8,128)(2,1)S(1)}, bf16[128,512]{1,0:T(8,128)(2,1)S(1)}, u32[]{:S(2)}, u32[]{:S(2)}) %collective-permute-start.17) | collective-permute-done | bytes 131104 | tf_op jit(solution)/shard_map/ppermute | solution.py:395
  46.4 3.9 %collective-permute-done.16 = bf16[128,512]{1,0:T(8,128)(2,1)S(1)} collective-permute-done((bf16[128,512]{1,0:T(8,128)(2,1)S(1)}, bf16[128,512]{1,0:T(8,128)(2,1)S(1)}, u32[]{:S(2)}, u32[]{:S(2)}) %collective-permute-start.16) | collective-permute-done | bytes 131104 | tf_op jit(solution)/shard_map/ppermute | solution.py:395
  50.3 0.7 %fusion = bf16[1,128,512]{2,1,0:T(8,128)(2,1)} fusion(bf16[128,512]{1,0:T(8,128)(2,1)S(1)} %collective-permute-done.17, bf16[128,512]{1,0:T(8,128)(2,1)S(1)} %collective-permute-done.16, bf16[128,512]{1,0:T(8,128)(2,1)S(1)} %collective-permute-done.15, bf16[128,512]{1,0:T(8,128)(2,1)S(1)} %get-tuple-element.59), kind=kLoop, calls=%fused_computation.1 | loop fusion | flops 524288 | bytes 655360 | tf_op jit(solution)/shard_map/broadcast_in_dim | solution.py:461
  (40 shorter events, 5.3 us)
Async XLA Ops:
  1.9 4.6 %collective-permute-start = (bf16[128,256]{1,0:T(8,128)(2,1)S(1)}, bf16[128,256]{1,0:T(8,128)(2,1)S(1)}, u32[]{:S(2)}, u32[]{:S(2)}) collective-permute-start(bf16[128,256]{1,0:T(8,128)(2,1)S(1)} %get-tuple-element.35), channel_id=1, source_target_pairs={{0,4},{4,0},{8,12},{12,8},{16,20},{20,16},{24,28},{28,24},{1,5},{5... | collective-permute-start | bytes 196616 | tf_op jit(solution)/shard_map/ppermute | solution.py:395
  2.4 13.4 %collective-permute-start.1 = (bf16[640,256]{1,0:T(8,128)(2,1)S(1)}, bf16[640,256]{1,0:T(8,128)(2,1)S(1)}, u32[]{:S(2)}, u32[]{:S(2)}) collective-permute-start(bf16[640,256]{1,0:T(8,128)(2,1)S(1)} %get-tuple-element.43.refs_4_), channel_id=1, source_target_pairs={{0,8},{4,12},{8,0},{12,4},{16,24},{20,28},{24,16},{28,20},{1,9},{5... | collective-permute-start | bytes 983048 | tf_op jit(solution)/shard_map/ppermute | solution.py:395
  5.0 10.9 %collective-permute-start.2 = (bf16[640,256]{1,0:T(8,128)(2,1)S(1)}, bf16[640,256]{1,0:T(8,128)(2,1)S(1)}, u32[]{:S(2)}, u32[]{:S(2)}) collective-permute-start(bf16[640,256]{1,0:T(8,128)(2,1)S(1)} %get-tuple-element.40.refs_5_), channel_id=1, source_target_pairs={{0,16},{4,20},{8,24},{12,28},{16,0},{20,4},{24,8},{28,12},{1,17},{... | collective-permute-start | bytes 983048 | tf_op jit(solution)/shard_map/ppermute | solution.py:395
  6.5 14.1 %collective-permute-start.5 = (bf16[640,256]{1,0:T(8,128)(2,1)S(1)}, bf16[640,256]{1,0:T(8,128)(2,1)S(1)}, u32[]{:S(2)}, u32[]{:S(2)}) collective-permute-start(bf16[640,256]{1,0:T(8,128)(2,1)S(1)} %get-tuple-element.40.refs_5_), channel_id=1, source_target_pairs={{0,8},{4,12},{8,0},{12,4},{16,24},{20,28},{24,16},{28,20},{1,9},{5... | collective-permute-start | bytes 983048 | tf_op jit(solution)/shard_map/ppermute | solution.py:395
  7.1 8.7 %collective-permute-start.3 = (bf16[256,256]{1,0:T(8,128)(2,1)S(1)}, bf16[256,256]{1,0:T(8,128)(2,1)S(1)}, u32[]{:S(2)}, u32[]{:S(2)}) collective-permute-start(bf16[256,256]{1,0:T(8,128)(2,1)S(1)} %constant_dynamic-update-slice_fusion.refs_0_), channel_id=1, source_target_pairs={{0,2},{1,3},{2,0},{3,1},{4,6},{5,7},{6,4},{7,5},{8,10},{9,11},{10,... | collective-permute-start | bytes 393224 | tf_op jit(solution)/shard_map/ppermute | solution.py:395
  9.8 0.7 %copy-start.3 = (s32[8]{0:T(128)S(1)}, s32[8]{0:T(128)}, u32[]{:S(2)}) copy-start(s32[8]{0:T(128)} %param.17) | copy-start | bytes 100
  11.9 11.9 %collective-permute-start.7 = (bf16[640,256]{1,0:T(8,128)(2,1)S(1)}, bf16[640,256]{1,0:T(8,128)(2,1)S(1)}, u32[]{:S(2)}, u32[]{:S(2)}) collective-permute-start(bf16[640,256]{1,0:T(8,128)(2,1)S(1)} %get-tuple-element.43.refs_4_), channel_id=1, source_target_pairs={{0,16},{4,20},{8,24},{12,28},{16,0},{20,4},{24,8},{28,12},{1,17},{... | collective-permute-start | bytes 983048 | tf_op jit(solution)/shard_map/ppermute | solution.py:395
  15.9 7.9 %collective-permute-start.4 = (bf16[256,256]{1,0:T(8,128)(2,1)S(1)}, bf16[256,256]{1,0:T(8,128)(2,1)S(1)}, u32[]{:S(2)}, u32[]{:S(2)}) collective-permute-start(bf16[256,256]{1,0:T(8,128)(2,1)S(1)} %constant_dynamic-update-slice_fusion.refs_0_), channel_id=1, source_target_pairs={{0,1},{1,0},{2,3},{3,2},{4,5},{5,4},{6,7},{7,6},{8,9},{9,8},{10,11... | collective-permute-start | bytes 393224 | tf_op jit(solution)/shard_map/ppermute | solution.py:395
  17.1 11.7 %collective-permute-start.8 = (bf16[640,256]{1,0:T(8,128)(2,1)S(1)}, bf16[640,256]{1,0:T(8,128)(2,1)S(1)}, u32[]{:S(2)}, u32[]{:S(2)}) collective-permute-start(bf16[640,256]{1,0:T(8,128)(2,1)S(1)} %collective-permute-done.1.refs_6_), channel_id=1, source_target_pairs={{0,16},{4,20},{8,24},{12,28},{16,0},{20,4},{24,8},{28,12},{1,17},{... | collective-permute-start | bytes 983048 | tf_op jit(solution)/shard_map/ppermute | solution.py:395
  18.7 10.2 %collective-permute-start.9 = (bf16[640,256]{1,0:T(8,128)(2,1)S(1)}, bf16[640,256]{1,0:T(8,128)(2,1)S(1)}, u32[]{:S(2)}, u32[]{:S(2)}) collective-permute-start(bf16[640,256]{1,0:T(8,128)(2,1)S(1)} %collective-permute-done.2.refs_9_), channel_id=1, source_target_pairs={{0,8},{4,12},{8,0},{12,4},{16,24},{20,28},{24,16},{28,20},{1,9},{5... | collective-permute-start | bytes 983048 | tf_op jit(solution)/shard_map/ppermute | solution.py:395
  20.6 5.0 %collective-permute-start.6 = (bf16[256,256]{1,0:T(8,128)(2,1)S(1)}, bf16[256,256]{1,0:T(8,128)(2,1)S(1)}, u32[]{:S(2)}, u32[]{:S(2)}) collective-permute-start(bf16[256,256]{1,0:T(8,128)(2,1)S(1)} %collective-permute-done.3.refs_2_), channel_id=1, source_target_pairs={{0,1},{1,0},{2,3},{3,2},{4,5},{5,4},{6,7},{7,6},{8,9},{9,8},{10,11... | collective-permute-start | bytes 393224 | tf_op jit(solution)/shard_map/ppermute | solution.py:395
  23.0 0.7 %copy-start.2 = (bf16[2048]{0:T(1024)(128)(2,1)S(1)}, bf16[2048]{0:T(1024)(128)(2,1)}, u32[]{:S(2)}) copy-start(bf16[2048]{0:T(1024)(128)(2,1)} %param.10) | copy-start | bytes 12292
  28.8 3.3 %copy-start.1 = (bf16[1,2048,128]{2,1,0:T(8,128)(2,1)S(1)}, bf16[1,2048,128]{2,1,0:T(8,128)(2,1)}, u32[]{:S(2)}) copy-start(bf16[1,2048,128]{2,1,0:T(8,128)(2,1)} %param.16) | copy-start | bytes 1572868
  29.1 3.0 %copy-start = (bf16[1,2048,128]{2,1,0:T(8,128)(2,1)S(1)}, bf16[1,2048,128]{2,1,0:T(8,128)(2,1)}, u32[]{:S(2)}) copy-start(bf16[1,2048,128]{2,1,0:T(8,128)(2,1)} %param.15) | copy-start | bytes 1572868
  29.1 3.0 %collective-permute-start.10 = (f32[128,768]{1,0:T(8,128)S(1)}, f32[128,768]{1,0:T(8,128)S(1)}, u32[]{:S(2)}, u32[]{:S(2)}) collective-permute-start(f32[128,768]{1,0:T(8,128)S(1)} %get-tuple-element.52), channel_id=1, source_target_pairs={{0,4},{4,0},{8,12},{12,8},{16,20},{20,16},{24,28},{28,24},{1,5},{5... | collective-permute-start | bytes 1179656 | tf_op jit(solution)/shard_map/ppermute | solution.py:395
  29.2 6.0 %collective-permute-start.12 = (bf16[3,512,256]{2,1,0:T(8,128)(2,1)S(1)}, bf16[3,512,256]{2,1,0:T(8,128)(2,1)S(1)}, u32[]{:S(2)}, u32[]{:S(2)}) collective-permute-start(bf16[3,512,256]{2,1,0:T(8,128)(2,1)S(1)} %get-tuple-element.55.own_ref), channel_id=1, source_target_pairs={{0,4},{4,0},{8,12},{12,8},{16,20},{20,16},{24,28},{28,24},{1,5},{5... | collective-permute-start | bytes 2359304 | tf_op jit(solution)/shard_map/ppermute | solution.py:395
  29.7 2.4 %collective-permute-start.11 = (f32[128,128]{1,0:T(8,128)S(1)}, f32[128,128]{1,0:T(8,128)S(1)}, u32[]{:S(2)}, u32[]{:S(2)}) collective-permute-start(f32[128,128]{1,0:T(8,128)S(1)} %slice.9), channel_id=1, source_target_pairs={{0,4},{4,0},{8,12},{12,8},{16,20},{20,16},{24,28},{28,24},{1,5},{5... | collective-permute-start | bytes 196616 | tf_op jit(solution)/shard_map/ppermute | solution.py:395
  29.8 5.4 %collective-permute-start.13 = (bf16[256,256]{1,0:T(8,128)(2,1)S(1)}, bf16[256,256]{1,0:T(8,128)(2,1)S(1)}, u32[]{:S(2)}, u32[]{:S(2)}) collective-permute-start(bf16[256,256]{1,0:T(8,128)(2,1)S(1)} %slice.12), channel_id=1, source_target_pairs={{0,4},{4,0},{8,12},{12,8},{16,20},{20,16},{24,28},{28,24},{1,5},{5... | collective-permute-start | bytes 393224 | tf_op jit(solution)/shard_map/ppermute | solution.py:395
  30.3 4.9 %collective-permute-start.14 = (bf16[256,256]{1,0:T(8,128)(2,1)S(1)}, bf16[256,256]{1,0:T(8,128)(2,1)S(1)}, u32[]{:S(2)}, u32[]{:S(2)}) collective-permute-start(bf16[256,256]{1,0:T(8,128)(2,1)S(1)} %slice.13), channel_id=1, source_target_pairs={{0,4},{4,0},{8,12},{12,8},{16,20},{20,16},{24,28},{28,24},{1,5},{5... | collective-permute-start | bytes 393224 | tf_op jit(solution)/shard_map/ppermute | solution.py:395
  36.3 10.1 %collective-permute-start.17 = (bf16[128,512]{1,0:T(8,128)(2,1)S(1)}, bf16[128,512]{1,0:T(8,128)(2,1)S(1)}, u32[]{:S(2)}, u32[]{:S(2)}) collective-permute-start(bf16[128,512]{1,0:T(8,128)(2,1)S(1)} %get-tuple-element.62), channel_id=1, source_target_pairs={{0,2},{1,3},{2,0},{3,1},{4,6},{5,7},{6,4},{7,5},{8,10},{9,11},{10,... | collective-permute-start | bytes 393224 | tf_op jit(solution)/shard_map/ppermute | solution.py:395
  40.0 10.3 %collective-permute-start.16 = (bf16[128,512]{1,0:T(8,128)(2,1)S(1)}, bf16[128,512]{1,0:T(8,128)(2,1)S(1)}, u32[]{:S(2)}, u32[]{:S(2)}) collective-permute-start(bf16[128,512]{1,0:T(8,128)(2,1)S(1)} %get-tuple-element.61), channel_id=1, source_target_pairs={{0,1},{1,0},{2,3},{3,2},{4,5},{5,4},{6,7},{7,6},{8,9},{9,8},{10,11... | collective-permute-start | bytes 393224 | tf_op jit(solution)/shard_map/ppermute | solution.py:395
  41.6 8.7 %collective-permute-start.15 = (bf16[128,512]{1,0:T(8,128)(2,1)S(1)}, bf16[128,512]{1,0:T(8,128)(2,1)S(1)}, u32[]{:S(2)}, u32[]{:S(2)}) collective-permute-start(bf16[128,512]{1,0:T(8,128)(2,1)S(1)} %get-tuple-element.60), channel_id=1, source_target_pairs={{0,3},{1,2},{2,1},{3,0},{4,7},{5,6},{6,5},{7,4},{8,11},{9,10},{10,... | collective-permute-start | bytes 393224 | tf_op jit(solution)/shard_map/ppermute | solution.py:395
